TPU v7x, 32 devices: a whole 2x2x4 slice. The times are simulated.
32 devices in a mesh: section: 2 (over core), row: 16 (over z, y, x).
Axes of the slice: x: 2, y: 2, z: 4, core: 2. Of those that a mesh axis runs over, the one named last changes fastest.
Arguments:
- tokens: bfloat16 [2, 8192, 384], P(None, 'row'), may hold values from -3 to 3
- conditions: bfloat16 [2, 32, 384], P(None, 'row'), may hold values from -2.5 to 2.5
- output_grad: bfloat16 [2, 8192, 384], P(None, 'row'), may hold values from -3 to 3
- layouts: int32 [2, 16], P(None, 'row'), may hold values from 0 to 2
- w_ada: bfloat16 [2, 384, 2304], P('section', 'row'), may hold values from -0.3125 to 0.3125
- b_ada: float32 [2, 2304], P('section'), may hold values from -0.5 to 0.5
- w_query: bfloat16 [2, 384, 384], P('section', 'row'), may hold values from -0.3125 to 0.3125
- w_key: bfloat16 [2, 384, 384], P('section', 'row'), may hold values from -0.3125 to 0.3125
- w_value: bfloat16 [2, 384, 384], P('section', 'row'), may hold values from -0.3125 to 0.3125
- w_gate: bfloat16 [2, 384, 384], P('section', 'row'), may hold values from -0.3125 to 0.3125
- w_out: bfloat16 [2, 384, 384], P('section', 'row'), may hold values from -0.4375 to 0.4375
- w_decay: bfloat16 [2, 384, 6], P('section', 'row'), may hold values from -0.3125 to 0.3125
- b_decay: float32 [2, 6], P('section'), may hold values from -3 to 6
- conv_kernel: float32 [2, 3, 384], P('section'), may hold values from -3 to 3
- w_up: bfloat16 [2, 384, 1536], P('section', 'row'), may hold values from -0.3125 to 0.3125
- b_up: float32 [2, 1536], P('section'), may hold values from -2 to 2
- w_down: bfloat16 [2, 1536, 384], P('section', 'row'), may hold values from -0.15625 to 0.15625
- b_down: float32 [2, 384], P('section'), may hold values from -2 to 2
Outputs:
- activations: bfloat16 [2, 2, 8192, 384], P('section', None, 'row')
- input_grads: float32 [2, 2, 8192, 384], P('section', None, 'row')
- cond_grads: float32 [2, 32, 384], P(None, 'row')
- grad_w_ada: float32 [2, 384, 2304], P('section', 'row')
- grad_b_ada: float32 [2, 2304], P('section')
- grad_w_query: float32 [2, 384, 384], P('section', 'row')
- grad_w_key: float32 [2, 384, 384], P('section', 'row')
- grad_w_value: float32 [2, 384, 384], P('section', 'row')
- grad_w_gate: float32 [2, 384, 384], P('section', 'row')
- grad_w_out: float32 [2, 384, 384], P('section', 'row')
- grad_w_decay: float32 [2, 384, 6], P('section', 'row')
- grad_b_decay: float32 [2, 6], P('section')
- grad_conv_kernel: float32 [2, 3, 384], P('section')
- grad_w_up: float32 [2, 384, 1536], P('section', 'row')
- grad_b_up: float32 [2, 1536], P('section')
- grad_w_down: float32 [2, 1536, 384], P('section', 'row')
- grad_b_down: float32 [2, 384], P('section')
Inputs may be any that keep to these rules, and one draw needn't show every extreme that they name: `layouts`: 0: the block of 512 rows holds one item of 16 x 32 patches; k: k items of 16 x 16 patches followed by empty rows.
All inputs are finite; a program needn't handle non-finite values.
Results may differ from a plain program's by a relative error of at most 0.018.
The roundings to bfloat16 on the way count: a program that leaves them out, or rounds other values in their place, can miss the bound.
Values may be sent and summed in bfloat16 or wider, within the bound.
No kernel may reach another device: no remote copies, remote signals or barrier semaphores. Data moves between devices by JAX's collectives and lax.ppermute only.
A program may use at most 256 MiB of HBM per device.

v0:
```python
import functools

import jax
import jax.numpy as jnp
from jax import lax
from jax.experimental import pallas as pl
from jax.experimental.pallas import tpu as pltpu
from jax.sharding import PartitionSpec as P

D = 384
HEADS = 6
HEAD_DIM = 64
FF = 1536
MICRO = 2
ROWS = 512
HALF = 256
SLOTS = 2
PAIR = 128
PAIRS = D // PAIR
QKVG = 4 * D
LANES = 128
GROUP = (QKVG + D + LANES) // 2
NEG = -1e30
SCALE = HEAD_DIM**-0.5

bf16 = jnp.bfloat16
f32 = jnp.float32


def mm(left, right):
    return jnp.dot(left, right, preferred_element_type=f32)


def mm_t(left, right):
    return lax.dot_general(left, right, (((1,), (1,)), ((), ())), preferred_element_type=f32)


def split(values):
    high = values.astype(bf16)
    return high, (values - high.astype(f32)).astype(bf16)


def split_three(values):
    high, rest = split(values)
    mid = values - high.astype(f32)
    middle, low = split(mid)
    return high, middle, low


def cat_left(values):
    high, low = split(values)
    return jnp.concatenate([high, low, high], axis=1)


def cat_right(values):
    high, low = split(values)
    return jnp.concatenate([high, high, low], axis=1)


def mm_near(left, right_pair, right_high):
    high, low = split(left)
    wide = mm(high, right_pair)
    return wide[:, :PAIR] + wide[:, PAIR:] + mm(low, right_high)


def lane_iota(rows, columns):
    return lax.broadcasted_iota(jnp.int32, (rows, columns), 1)


def row_iota(rows, columns):
    return lax.broadcasted_iota(jnp.int32, (rows, columns), 0)


def order_matrix(start, rows, wide, to_scan):
    t = row_iota(rows, ROWS) + start
    small = (t & 256) + ((t & 15) << 4) + ((t & 255) >> 4)
    if to_scan:
        large = ((t & 15) << 5) + (t >> 4)
    else:
        large = ((t & 31) << 4) + (t >> 5)
    source = jnp.where(wide, large, small)
    return jnp.where(lane_iota(rows, ROWS) == source, 1.0, 0.0).astype(bf16)


def normalise(values):
    centred = values - jnp.mean(values, axis=-1, keepdims=True)
    rate = lax.rsqrt(jnp.mean(centred * centred, axis=-1, keepdims=True) + 1e-06)
    return centred * rate, rate


def normalise_back(normal, rate, grad):
    return rate * (
        grad
        - jnp.mean(grad, axis=-1, keepdims=True)
        - normal * jnp.mean(grad * normal, axis=-1, keepdims=True)
    )


class In:
    def __init__(self, copy, kept):
        self.copy = copy
        self.kept = kept

    def __call__(self):
        if self.copy is not None:
            self.copy.wait()
            self.copy = None
        return self.kept


class Kernel:
    def __init__(self, layer, layouts):
        self.layer = layer
        self.section = lax.axis_index("section")
        self.own = self.section == layer
        self.layout = layouts[self.section, 0]
        self.wide = self.layout == 0
        self.live_rows = jnp.where(self.wide, ROWS, self.layout * HALF)
        self.pushed = {}

    def load(self, kind, refs, kept, sem):
        if kind == "own":
            mine, other = refs

            @pl.when(self.own)
            def _():
                pltpu.make_async_copy(mine, kept, sem).start()

            @pl.when(jnp.logical_not(self.own))
            def _():
                pltpu.make_async_copy(other, kept, sem).start()

            return In(pltpu.make_async_copy(mine, kept, sem), kept)
        (source,) = refs
        if kind == "micro":
            source = source.at[self.section if source.shape[0] == MICRO else 0]
        copy = pltpu.make_async_copy(source, kept, sem)
        copy.start()
        return In(copy, kept)

    def push(self, name):
        kept, target, sem = self.results[name]
        copy = pltpu.make_async_copy(kept, target, sem)
        copy.start()
        self.pushed[name] = copy

    def finish(self):
        for name in self.results:
            if name not in self.pushed:
                self.push(name)
        for copy in self.pushed.values():
            copy.wait()

    def slot(self, half):
        return jnp.where(self.wide, 0, half)

    def share(self, slot, part):
        row = pl.ds(2 * self.section + slot, 1)
        return self.mods()[row, part * D : (part + 1) * D]

    def bu(self):
        return self.small()[0:1, :]

    def bn(self):
        return self.small()[1:2, :D]

    def ck(self, tap):
        return self.small()[2 + tap : 3 + tap, :D]

    def bd(self):
        return self.small()[5:6, :LANES]


def sigmoid(values):
    return 1.0 / (1.0 + jnp.exp(-values))


GELU_A = 0.7978845608028654
GELU_B = 0.044715


def gelu_parts(values):
    square = values * values
    tanh = jnp.tanh(GELU_A * values * (1.0 + GELU_B * square))
    return square, tanh


def fill_bias(bias, wide):
    bias[:, :HALF] = jnp.full((HALF, HALF), 0.0, f32) + jnp.where(wide, 0.0, NEG)
    causal = row_iota(HALF, HALF) >= lane_iota(HALF, HALF)
    bias[:, HALF:] = jnp.where(causal, 0.0, NEG)


def decay_factors(cum, cumt, bias, head):
    row = cumt[pl.ds(head, 1), :]
    lanes = lane_iota(1, LANES)
    column = jnp.sum(jnp.where(lanes == head, cum[...], 0.0), axis=1, keepdims=True)
    first = jnp.exp(column[:HALF] - row[:, :HALF] + bias[:, HALF:])
    second = jnp.exp(column[HALF:] - row + bias[...])
    return first, second


def head_norm(values, lanes):
    square = values * values
    low = jnp.sum(jnp.where(lanes < HEAD_DIM, square, 0.0), axis=1, keepdims=True)
    high = jnp.sum(jnp.where(lanes < HEAD_DIM, 0.0, square), axis=1, keepdims=True)
    return jnp.where(lanes < HEAD_DIM, low, high) * (1.0 / HEAD_DIM)


def fill_decay(dp, bd, cum, cumt):
    raw = dp[...] + bd
    log_decay = (jnp.minimum(raw, 0.0) - jnp.log1p(jnp.exp(-jnp.abs(raw)))) * (1.0 / 16.0)
    high, middle, low = split_three(log_decay)
    causal = jnp.where(row_iota(ROWS, ROWS) >= lane_iota(ROWS, ROWS), 1.0, 0.0).astype(bf16)
    cum[...] = mm(causal, high) + mm(causal, middle) + mm(causal, low)
    cumt[...] = jnp.transpose(cum[...])


def columns(index, first=0):
    return slice(index * PAIR + first, index * PAIR + first + PAIR)


def attn_forward_body(k):
    flip = k.layer == 1
    wide = k.wide
    x = k.x()
    k.mods()

    def first(i, carry):
        rows = pl.ds(pl.multiple_of(i * HALF, HALF), HALF)
        slot = k.slot(i)
        normal, _ = normalise(x[rows, :].astype(f32))
        k.inner[rows, :] = (normal * (1.0 + k.share(slot, 1)) + k.share(slot, 0)).astype(bf16)
        return carry

    lax.fori_loop(0, 2, first, 0)
    w_qk = k.w_qk()
    w_vgd = k.w_vgd()

    def project(i, carry):
        start = i * HALF
        rows = pl.ds(start, HALF)
        if flip:
            part = mm(order_matrix(start, HALF, wide, True), k.inner[...]).astype(bf16)
        else:
            part = k.inner[rows, :]
        k.ordered[rows, :] = part
        k.qkvg[rows, : 2 * D] = mm(part, w_qk[...])
        k.qkvg[rows, 2 * D :] = mm(part, w_vgd[:, : 2 * D])
        k.dp[rows, :] = mm(part, w_vgd[:, 2 * D :])
        return carry

    lax.fori_loop(0, 2, project, 0)
    k.small()
    for name in ("ordered", "qkvg", "dp"):
        k.push(name)
    fill_decay(k.dp, k.bd(), k.cum, k.cumt)
    fill_bias(k.bias, wide)

    vpad = k.vpad
    vpad[0:8, :] = jnp.zeros((8, D), f32)
    vpad[8 : 8 + ROWS, :] = k.qkvg[:, 2 * D : 3 * D]
    position = row_iota(ROWS, 1) & jnp.where(wide, ROWS - 1, HALF - 1)
    one = jnp.where(position >= 1, vpad[7 : 7 + ROWS, :], 0.0)
    two = jnp.where(position >= 2, vpad[6 : 6 + ROWS, :], 0.0)
    k.vc[...] = k.ck(0) * vpad[8 : 8 + ROWS, :] + k.ck(1) * one + k.ck(2) * two
    for name in ("cum", "cumt", "vc"):
        k.push(name)

    def pair(p, carry):
        lanes = lane_iota(1, PAIR)
        queries = cat_left(k.qkvg[:, columns(p)] * SCALE)
        keys = k.qkvg[:, columns(p, D)]
        value_high, value_low = split(k.vc[:, columns(p)])
        values = jnp.concatenate([value_high, value_low], axis=1)
        parts = []
        for e in range(2):
            key_cat = cat_right(jnp.where((lanes // HEAD_DIM) == e, keys, 0.0))
            first, second = decay_factors(k.cum, k.cumt, k.bias, 2 * p + e)
            first = first * mm_t(queries[:HALF], key_cat[:HALF])
            second = second * mm_t(queries[HALF:], key_cat)
            parts.append(
                jnp.concatenate(
                    [
                        mm_near(first, values[:HALF], value_high[:HALF]),
                        mm_near(second, values, value_high),
                    ],
                    axis=0,
                )
            )
        total = jnp.where(lanes < HEAD_DIM, parts[0], parts[1])
        k.o[:, columns(p)] = total
        gate = k.qkvg[:, columns(p, 3 * D)]
        normed = total * lax.rsqrt(head_norm(total, lanes) + 1.0)
        mixed = (normed * (gate * sigmoid(gate))).astype(bf16)
        if flip:
            k.inner[:, columns(p)] = mixed
        else:
            k.gated[:, columns(p)] = mixed
        return carry

    for p in range(PAIRS):
        pair(p, 0)
    k.push("o")
    if flip:

        def back(i, carry):
            start = i * HALF
            k.gated[pl.ds(start, HALF), :] = mm(
                order_matrix(start, HALF, wide, False), k.inner[...]
            ).astype(bf16)
            return carry

        lax.fori_loop(0, 2, back, 0)


def ffn_forward_body(k):
    gated, x = k.gated(), k.x()
    k.mods(), k.small()

    def tile(i, carry):
        start = i * HALF
        rows = pl.ds(start, HALF)
        slot = k.slot(i)
        grown = mm(gated[rows, :], k.wo()[...])
        k.branch[rows, :] = grown
        middle = x[rows, :].astype(f32) + k.share(slot, 2) * grown
        normal, _ = normalise(middle)
        inner = (normal * (1.0 + k.share(slot, 4)) + k.share(slot, 3)).astype(bf16)
        up = mm(inner, k.wu()[...]) + k.bu()
        _, tanh = gelu_parts(up)
        hidden = (0.5 * up * (1.0 + tanh)).astype(bf16)
        low = mm(hidden, k.wn()[...])
        k.down[rows, :] = low
        result = middle + k.share(slot, 5) * (low + k.bn())
        live = (row_iota(HALF, 1) + start) < k.live_rows
        k.out[rows, :] = jnp.where(live, result, 0.0).astype(bf16)
        return carry

    for i in range(2):
        tile(i, 0)
    if k.layer == 1:
        k.sent[...] = jnp.where(k.section == 0, k.out[...].astype(f32), x[...].astype(f32)).astype(bf16)


def ffn_backward_body(k):
    gmod, gbu, gbn = k.gmod, k.gbu, k.gbn
    gmod[...] = jnp.zeros(gmod.shape, f32)
    gbu[...] = jnp.zeros(gbu.shape, f32)
    gbn[...] = jnp.zeros(gbn.shape, f32)
    k.mods(), k.small()
    x, grad, branch, down = k.x(), k.grad(), k.branch(), k.down()

    def tile(i, carry):
        start = i * HALF
        rows = pl.ds(start, HALF)
        slot = k.slot(i)

        def add(part, values):
            where = (pl.ds(slot, 1), slice((part - 2) * D, (part - 1) * D))
            gmod[where] = gmod[where] + jnp.sum(values, axis=0, keepdims=True)

        grown = branch[rows, :]
        middle = x[rows, :].astype(f32) + k.share(slot, 2) * grown
        normal, rate = normalise(middle)
        inner = (normal * (1.0 + k.share(slot, 4)) + k.share(slot, 3)).astype(bf16)
        k.inner_s[rows, :] = inner
        live = (row_iota(HALF, 1) + start) < k.live_rows
        above = jnp.where(live, grad[rows, :].astype(f32), 0.0)
        add(5, above * (down[rows, :] + k.bn()))
        grad_down = above * k.share(slot, 5)
        gbn[...] = gbn[...] + jnp.sum(grad_down, axis=0, keepdims=True)
        down_low = grad_down.astype(bf16)
        k.down_s[rows, :] = down_low
        up = mm(inner, k.wu()[...]) + k.bu()
        square, tanh = gelu_parts(up)
        half = 0.5 * (1.0 + tanh)
        k.hidden_s[rows, :] = (up * half).astype(bf16)
        slope = half + 0.5 * up * (1.0 - tanh * tanh) * (
            GELU_A * (1.0 + 3.0 * GELU_B * square)
        )
        grad_up = mm_t(down_low, k.wn()[...]) * slope
        gbu[...] = gbu[...] + jnp.sum(grad_up, axis=0, keepdims=True)
        up_low = grad_up.astype(bf16)
        k.up_s[rows, :] = up_low
        grad_inner = mm_t(up_low, k.wu()[...])
        add(3, grad_inner)
        add(4, grad_inner * normal)
        grad_middle = above + normalise_back(
            normal, rate, grad_inner * (1.0 + k.share(slot, 4))
        )
        k.mid_grad[rows, :] = grad_middle
        add(2, grad_middle * grown)
        k.branch_low[rows, :] = (grad_middle * k.share(slot, 2)).astype(bf16)
        return carry

    for i in range(2):
        tile(i, 0)
    k.push("mid_grad")
    k.push("branch_low")

    def weights(j, carry):
        part = pl.ds(pl.multiple_of(j * HALF, HALF), HALF)
        hidden_t = jnp.transpose(k.hidden_s[:, part].astype(f32)).astype(bf16)
        k.gwn[part, :] = mm(hidden_t, k.down_s[...])
        return carry

    lax.fori_loop(0, FF // HALF, weights, 0)
    inner_t = jnp.transpose(k.inner_s[...].astype(f32)).astype(bf16)
    if k.packed:
        devices, shard, _ = k.keep.shape

        def halves(j, carry):
            for kept, own in ((k.keep, c_section), (k.sent, 1 - c_section)):
                columns = pl.ds(pl.multiple_of(j * HALF + own * (FF // 2), HALF), HALF)
                here = pl.ds(pl.multiple_of(j * HALF, HALF), HALF)
                part = mm(inner_t, k.up_s[:, columns]).reshape(devices, shard, HALF)
                kept[:, :, here] = part.astype(kept.dtype)
            return carry

        c_section = k.section
        lax.fori_loop(0, FF // 2 // HALF, halves, 0)

        def owner(r, carry):
            for kept, own in ((k.keep, c_section), (k.sent, 1 - c_section)):
                for piece in range(2):
                    start = pl.multiple_of((4 * r + 2 * own + piece) * shard, 8)
                    rows = k.gwn[pl.ds(start, shard), :]
                    at = FF // 2 + piece * D
                    kept[r, :, at : at + D] = rows.astype(kept.dtype)
            return carry

        lax.fori_loop(0, devices, owner, 0)
        k.push("keep")
        k.push("sent")
    else:
        k.gwu[...] = mm(inner_t, k.up_s[...])
    gated = k.gated()
    k.gwo[...] = mm(jnp.transpose(gated[...].astype(f32)).astype(bf16), k.branch_low[...])

    short = jnp.concatenate([gbn[...], jnp.zeros((1, FF - D), f32)], axis=1)
    k.sums[...] = jnp.concatenate(
        [gmod[0:SLOTS, :], gbu[...], short, jnp.zeros((4, FF), f32)], axis=0
    )


def mixer_backward_body(k):
    flip = k.layer == 1
    wide = k.wide
    mixed_s, low, dv_s, rows_s, cols_s = k.mixed_s, k.low, k.dv_s, k.rows_s, k.cols_s
    fill_bias(k.bias, wide)
    branch_low, wo = k.branch_low(), k.wo()

    def first(i, carry):
        start = i * HALF
        rows = pl.ds(start, HALF)
        if flip:
            part = mm(order_matrix(start, HALF, wide, True), branch_low[...]).astype(bf16)
        else:
            part = branch_low[rows, :]
        mixed_s[rows, :] = mm_t(part, wo[...])
        return carry

    lax.fori_loop(0, 2, first, 0)
    rows_s[...] = jnp.zeros(rows_s.shape, f32)
    cols_s[...] = jnp.zeros(cols_s.shape, f32)
    qkvg, vc, cum, cumt, o = k.qkvg(), k.vc(), k.cum(), k.cumt(), k.o()
    k.small()

    def pair(p, carry):
        lanes = lane_iota(1, PAIR)
        total = o[:, columns(p)]
        gate = qkvg[:, columns(p, 3 * D)]
        above = mixed_s[:, columns(p)]
        rate = lax.rsqrt(head_norm(total, lanes) + 1.0)
        sig = sigmoid(gate)
        grad_gate = above * (total * rate) * (sig * (1.0 + gate * (1.0 - sig)))
        low[:, columns(p, 3 * D)] = grad_gate.astype(bf16)
        grad_normed = above * (gate * sig)
        product = grad_normed * total
        inside = jnp.where(
            lanes < HEAD_DIM,
            jnp.sum(jnp.where(lanes < HEAD_DIM, product, 0.0), axis=1, keepdims=True),
            jnp.sum(jnp.where(lanes < HEAD_DIM, 0.0, product), axis=1, keepdims=True),
        ) * (1.0 / HEAD_DIM)
        grad_o = rate * grad_normed - total * (rate * rate * rate) * inside

        queries = qkvg[:, columns(p)] * SCALE
        keys = qkvg[:, columns(p, D)]
        values = vc[:, columns(p)]
        query_cat = cat_left(queries)
        grad_cat = cat_left(grad_o)
        key_high, key_low = split(keys)
        key_pair = jnp.concatenate([key_high, key_low], axis=1)
        query_t = jnp.transpose(queries)
        grad_t = jnp.transpose(grad_o)
        grad_q = []
        grad_k = []
        grad_v = []
        for e in range(2):
            mine = (lanes // HEAD_DIM) == e
            head = 2 * p + e
            key_cat = cat_right(jnp.where(mine, keys, 0.0))
            value_cat = cat_right(jnp.where(mine, values, 0.0))
            first, second = decay_factors(cum, cumt, k.bias, head)
            raw_first = mm_t(query_cat[:HALF], key_cat[:HALF])
            raw_second = mm_t(query_cat[HALF:], key_cat)
            grad_first = first * mm_t(grad_cat[:HALF], value_cat[:HALF])
            grad_second = second * mm_t(grad_cat[HALF:], value_cat)
            score_first = raw_first * first
            score_second = raw_second * second
            pull_first = grad_first * raw_first
            pull_second = grad_second * raw_second
            here = lanes == head
            rows_s[:HALF, :] = rows_s[:HALF, :] + jnp.where(
                here, jnp.sum(pull_first, axis=1, keepdims=True), 0.0
            )
            rows_s[HALF:, :] = rows_s[HALF:, :] + jnp.where(
                here, jnp.sum(pull_second, axis=1, keepdims=True), 0.0
            )
            low_cols = jnp.sum(pull_second, axis=0, keepdims=True)
            cols_s[pl.ds(head, 1), :HALF] = low_cols[:, :HALF] + jnp.sum(
                pull_first, axis=0, keepdims=True
            )
            cols_s[pl.ds(head, 1), HALF:] = low_cols[:, HALF:]
            grad_q.append(
                jnp.concatenate(
                    [
                        mm_near(grad_first, key_pair[:HALF], key_high[:HALF]),
                        mm_near(grad_second, key_pair, key_high),
                    ],
                    axis=0,
                )
            )

            def turned(source_t, block_first, block_second):
                high, low = split(source_t[e * HEAD_DIM : (e + 1) * HEAD_DIM, :])
                both = jnp.concatenate([high, low], axis=0)
                first_high, first_low = split(block_first)
                second_high, second_low = split(block_second)
                one = mm(both[:, :HALF], first_high)
                one = one[:HEAD_DIM] + one[HEAD_DIM:] + mm(high[:, :HALF], first_low)
                two = mm(both[:, HALF:], second_high)
                two = two[:HEAD_DIM] + two[HEAD_DIM:] + mm(high[:, HALF:], second_low)
                return jnp.concatenate([two[:, :HALF] + one, two[:, HALF:]], axis=1)

            grad_k.append(turned(query_t, grad_first, grad_second))
            grad_v.append(turned(grad_t, score_first, score_second))
        query_grad = jnp.where(lanes < HEAD_DIM, grad_q[0], grad_q[1]) * SCALE
        low[:, columns(p)] = query_grad.astype(bf16)
        low[:, columns(p, D)] = jnp.transpose(jnp.concatenate(grad_k, axis=0)).astype(bf16)
        dv_s[:ROWS, columns(p)] = jnp.transpose(jnp.concatenate(grad_v, axis=0))
        return carry

    for p in range(PAIRS):
        pair(p, 0)

    pulled = rows_s[...] - jnp.transpose(cols_s[...])
    high, middle, rest = split_three(pulled)
    upper_first = jnp.concatenate(
        [
            jnp.where(row_iota(HALF, HALF) <= lane_iota(HALF, HALF), 1.0, 0.0),
            jnp.full((HALF, HALF), 0.0, f32) + jnp.where(wide, 1.0, 0.0),
        ],
        axis=1,
    ).astype(bf16)
    upper_second = upper_first[:, :HALF]
    later = jnp.concatenate(
        [
            mm(upper_first, high) + mm(upper_first, middle) + mm(upper_first, rest),
            mm(upper_second, high[HALF:]) + mm(upper_second, middle[HALF:])
            + mm(upper_second, rest[HALF:]),
        ],
        axis=0,
    )
    grad_dp = later * (1.0 / 16.0) * sigmoid(-(k.dp()[...] + k.bd()))
    grad_bd = jnp.sum(grad_dp, axis=0, keepdims=True)
    low[:, QKVG:] = grad_dp.astype(bf16)

    dv_s[ROWS:, :] = jnp.zeros((8, D), f32)
    position = row_iota(ROWS, 1) & jnp.where(wide, ROWS - 1, HALF - 1)
    last = jnp.where(wide, ROWS - 1, HALF - 1)
    here = dv_s[0:ROWS, :]
    one = jnp.where(position <= last - 1, dv_s[1 : 1 + ROWS, :], 0.0)
    two = jnp.where(position <= last - 2, dv_s[2 : 2 + ROWS, :], 0.0)
    value = qkvg[:, 2 * D : 3 * D]
    low[:, 2 * D : 3 * D] = (k.ck(0) * here + k.ck(1) * one + k.ck(2) * two).astype(bf16)
    k.push("low")

    taps = [jnp.sum(rows * value, axis=0, keepdims=True) for rows in (here, one, two)]
    rest = jnp.concatenate([grad_bd, jnp.zeros((1, D - LANES), f32)], axis=1)
    k.sums[...] = jnp.concatenate([*taps, rest, jnp.zeros((4, D), f32)], axis=0)

    ordered_t = jnp.transpose(k.ordered()[...].astype(f32)).astype(bf16)
    gwo = k.gwo()
    gw = k.gw

    def weights(j, carry):
        part = pl.ds(pl.multiple_of(j * HALF, HALF), HALF)
        gw[:, part] = mm(ordered_t, low[:, part])
        return carry

    lax.fori_loop(0, QKVG // HALF, weights, 0)
    gw[:, QKVG : QKVG + D] = gwo[...]
    gw[:, QKVG + D :] = mm(ordered_t, low[:, QKVG:])

    def halves(j, carry):
        here = pl.ds(pl.multiple_of(j * HALF, HALF), HALF)
        keep = pl.ds(pl.multiple_of(j * HALF + k.section * GROUP, HALF), HALF)
        send = pl.ds(pl.multiple_of(j * HALF + (1 - k.section) * GROUP, HALF), HALF)
        k.gw_keep[:, here] = gw[:, keep]
        k.gw_send[:, here] = gw[:, send].astype(bf16)
        return carry

    lax.fori_loop(0, GROUP // HALF, halves, 0)


def input_backward_body(k):
    flip = k.layer == 1
    wide = k.wide
    gmod, mixed_s, perm_s = k.gmod, k.mixed_s, k.perm_s
    gmod[...] = jnp.zeros(gmod.shape, f32)
    low, w_qk, w_vgd = k.low(), k.w_qk(), k.w_vgd()

    def inner_grad(i, carry):
        rows = pl.ds(pl.multiple_of(i * HALF, HALF), HALF)
        mixed_s[rows, :] = mm_t(low[rows, : 2 * D], w_qk[...]) + mm_t(
            low[rows, 2 * D :], w_vgd[...]
        )
        return carry

    lax.fori_loop(0, 2, inner_grad, 0)
    if flip:
        high, middle, rest = split_three(mixed_s[...])
        perm_s[:, :D] = high
        perm_s[:, D : 2 * D] = middle
        perm_s[:, 2 * D :] = rest
    x, mid_grad = k.x(), k.mid_grad()
    k.mods()

    def tile(i, carry):
        start = i * HALF
        rows = pl.ds(start, HALF)
        slot = k.slot(i)
        if flip:
            three = mm(order_matrix(start, HALF, wide, False), perm_s[...])
            grad = three[:, :D] + three[:, D : 2 * D] + three[:, 2 * D :]
        else:
            grad = mixed_s[rows, :]
        normal, rate = normalise(x[rows, :].astype(f32))
        where = (pl.ds(slot, 1), slice(0, D))
        gmod[where] = gmod[where] + jnp.sum(grad, axis=0, keepdims=True)
        where = (pl.ds(slot, 1), slice(D, 2 * D))
        gmod[where] = gmod[where] + jnp.sum(grad * normal, axis=0, keepdims=True)
        total = mid_grad[rows, :] + normalise_back(normal, rate, grad * (1.0 + k.share(slot, 1)))
        k.gx[rows, :] = total
        k.gx_low[rows, :] = total.astype(bf16)
        return carry

    for i in range(2):
        tile(i, 0)
    k.push("gx_low")
    k.push("gx")
    ffn, mixer = k.ffn_sums(), k.mixer_sums()
    k.mod_low[...] = jnp.concatenate([gmod[...], ffn[...]], axis=1).astype(bf16)
    if k.layer == 0:
        first = k.section == 0
        k.gx_send[...] = jnp.where(first, k.gx_two()[...], k.gx[...])
        one, two = k.mod_low[...].astype(f32), k.mod_two()[...].astype(f32)
        k.mod_mine[...] = jnp.where(first, one, two).astype(bf16)
        k.mod_send[...] = jnp.where(first, two, one).astype(bf16)
    half = 2 * D
    rest = ffn[0:1, :] + ffn[1:2, :]
    k.sums[...] = jnp.concatenate(
        [
            gmod[0:1, :] + gmod[1:2, :],
            rest[:, :half],
            rest[:, half:],
            ffn[2:3, :half],
            ffn[2:3, half:],
            jnp.concatenate([ffn[3:4, :D], mixer[0:1, :]], axis=1),
            jnp.concatenate([mixer[1:2, :], mixer[2:3, :]], axis=1),
            jnp.concatenate([mixer[3:4, :], jnp.zeros((1, D), f32)], axis=1),
        ],
        axis=0,
    )


ANY = pl.BlockSpec(memory_space=pl.ANY)
VMEM = pl.BlockSpec(memory_space=pltpu.VMEM)
HBM = pl.BlockSpec(memory_space=pltpu.HBM)


def call(body, layer, layouts, ins, outs, scratch, flops, packed=None, after=()):
    arrays = []
    counts = []
    kept = []
    places = []
    for kind, given, part in ins.values():
        places.extend([ANY] * 2 if kind == "own" else [HBM])
        given = given if kind == "own" else (given,)
        arrays.extend(given)
        counts.append(len(given))
        rows, wide = given[0].shape[-2:]
        start, stop = part or (0, wide)
        kept.append(pltpu.VMEM((rows, stop - start), given[0].dtype))

    def kernel(*refs):
        refs = list(refs)
        take = lambda count: [refs.pop(0) for _ in range(count)]
        (layouts_ref,) = take(1)
        sources = [take(count) for count in counts]
        take(len(after))
        targets = take(len(outs))
        buffers = take(len(ins))
        results = take(len(outs))
        rest = take(len(scratch))
        in_sems, out_sems = refs
        k = Kernel(layer, layouts_ref)
        k.packed = packed
        for number, (name, (kind, _, part)) in enumerate(ins.items()):
            given = sources[number]
            if part is not None:
                given = [ref.at[:, part[0] : part[1]] for ref in given]
            setattr(k, name, k.load(kind, given, buffers[number], in_sems.at[number]))
        k.results = {}
        for number, name in enumerate(outs):
            setattr(k, name, results[number])
            k.results[name] = (results[number], targets[number], out_sems.at[number])
        for name, ref in zip(scratch, rest):
            setattr(k, name, ref)
        body(k)
        k.finish()

    return pl.pallas_call(
        kernel,
        out_shape=[jax.ShapeDtypeStruct(shape, kind) for shape, kind, _ in outs.values()],
        in_specs=[pl.BlockSpec(memory_space=pltpu.SMEM)] + places + [ANY] * len(after),
        out_specs=[HBM if for_kernel else ANY for _, _, for_kernel in outs.values()],
        scratch_shapes=kept
        + [pltpu.VMEM(shape, kind) for shape, kind, _ in outs.values()]
        + [pltpu.VMEM(shape, kind) for shape, kind in scratch.values()]
        + [pltpu.SemaphoreType.DMA((len(ins),)), pltpu.SemaphoreType.DMA((len(outs),))],
        compiler_params=pltpu.CompilerParams(vmem_limit_bytes=56 * 1024 * 1024),
        cost_estimate=pl.CostEstimate(flops=flops, bytes_accessed=4 << 20, transcendentals=0),
    )(layouts, *arrays, *after)


def own(pair, part=None):
    return ("own", pair, part)


def plain(array):
    return ("plain", array, None)


def micro(array):
    return ("micro", array, None)


AT_UP = (0, FF)
AT_OUT = (FF, FF + D)


def attn_forward(layer, layouts, x, mods, small, qk, vgd):
    return call(
        attn_forward_body,
        layer,
        layouts,
        dict(
            x=micro(x),
            mods=own(mods),
            w_qk=own(qk),
            w_vgd=own(vgd),
            small=own(small),
        ),
        dict(
            ordered=((ROWS, D), bf16, True),
            qkvg=((ROWS, QKVG), f32, True),
            dp=((ROWS, LANES), f32, True),
            vc=((ROWS, D), f32, True),
            cum=((ROWS, LANES), f32, True),
            cumt=((LANES, ROWS), f32, True),
            o=((ROWS, D), f32, True),
            gated=((ROWS, D), bf16, True),
        ),
        dict(
            inner=((ROWS, D), bf16),
            vpad=((ROWS + 8, D), f32),
            bias=((HALF, ROWS), f32),
        ),
        4 * 10**9,
    )


def ffn_forward(layer, layouts, x, mods, small, gated, upo, down):
    return call(
        ffn_forward_body,
        layer,
        layouts,
        dict(
            gated=plain(gated),
            x=micro(x),
            wo=own(upo, AT_OUT),
            mods=own(mods),
            small=own(small),
            wu=own(upo, AT_UP),
            wn=own(down),
        ),
        dict(
            out=((ROWS, D), bf16, True),
            branch=((ROWS, D), f32, True),
            down=((ROWS, D), f32, True),
            **({"sent": ((ROWS, D), bf16, False)} if layer == 1 else {}),
        ),
        {},
        3 * 10**9,
    )


def ffn_backward(
    layer, layouts, x, mods, small, gated, branch, down_raw, grad, upo, down, devices, after=()
):
    shard = D // devices
    in_kernel = shard % 8 == 0
    if in_kernel:
        sums = dict(
            keep=((devices, shard, FF), f32, True),
            sent=((devices, shard, FF), bf16, False),
        )
    else:
        sums = dict(gwu=((D, FF), f32, False), gwn=((FF, D), f32, False))
    return call(
        ffn_backward_body,
        layer,
        layouts,
        dict(
            mods=own(mods),
            small=own(small),
            x=micro(x),
            grad=micro(grad),
            branch=plain(branch),
            down=plain(down_raw),
            wu=own(upo, AT_UP),
            wn=own(down),
            gated=plain(gated),
        ),
        dict(
            mid_grad=((ROWS, D), f32, True),
            branch_low=((ROWS, D), bf16, True),
            gwo=((D, D), f32, True),
            sums=((8, FF), f32, True),
            **sums,
        ),
        dict(
            **({"gwn": ((FF, D), f32)} if in_kernel else {}),
            hidden_s=((ROWS, FF), bf16),
            inner_s=((ROWS, D), bf16),
            up_s=((ROWS, FF), bf16),
            down_s=((ROWS, D), bf16),
            gmod=((8, FF), f32),
            gbu=((1, FF), f32),
            gbn=((1, D), f32),
        ),
        5 * 10**9,
        packed=in_kernel,
        after=after,
    )


def mixer_backward(layer, layouts, small, saved, branch_low, gwo, upo, after=()):
    ordered, qkvg, dp, vc, cum, cumt, o = saved
    return call(
        mixer_backward_body,
        layer,
        layouts,
        dict(
            branch_low=plain(branch_low),
            wo=own(upo, AT_OUT),
            qkvg=plain(qkvg),
            vc=plain(vc),
            cum=plain(cum),
            cumt=plain(cumt),
            o=plain(o),
            small=own(small),
            dp=plain(dp),
            ordered=plain(ordered),
            gwo=plain(gwo),
        ),
        dict(
            low=((ROWS, QKVG + LANES), bf16, True),
            gw_keep=((D, GROUP), f32, True),
            gw_send=((D, GROUP), bf16, False),
            sums=((8, D), f32, True),
        ),
        dict(
            mixed_s=((ROWS, D), f32),
            dv_s=((ROWS + 8, D), f32),
            rows_s=((ROWS, LANES), f32),
            cols_s=((LANES, ROWS), f32),
            bias=((HALF, ROWS), f32),
            gw=((D, 2 * GROUP), f32),
        ),
        7 * 10**9,
        after=after,
    )


def input_backward(
    layer, layouts, x, mods, low, mid_grad, ffn_sums, mixer_sums, qk, vgd, two=None, after=()
):
    extra_in, extra_out = {}, {}
    if two is not None:
        extra_in = dict(gx_two=plain(two[0]), mod_two=plain(two[1]))
        extra_out = dict(
            gx_send=((ROWS, D), f32, False),
            mod_mine=((8, 6 * D), bf16, False),
            mod_send=((8, 6 * D), bf16, False),
        )
    return call(
        input_backward_body,
        layer,
        layouts,
        dict(
            low=plain(low),
            w_qk=own(qk),
            w_vgd=own(vgd),
            x=micro(x),
            mid_grad=plain(mid_grad),
            mods=own(mods),
            ffn_sums=plain(ffn_sums),
            mixer_sums=plain(mixer_sums),
            **extra_in,
        ),
        dict(
            gx=((ROWS, D), f32, True),
            gx_low=((ROWS, D), bf16, True),
            mod_low=((8, 6 * D), bf16, True),
            sums=((8, 2 * D), f32, False),
            **extra_out,
        ),
        dict(
            mixed_s=((ROWS, D), f32),
            perm_s=((ROWS, 3 * D), bf16),
            gmod=((8, 2 * D), f32),
        ),
        2 * 10**9,
        after=after,
    )


def small_kernel(b_up, b_down, taps, b_decay, packed):
    packed[...] = jnp.zeros(packed.shape, f32)
    packed[0:1, :] = b_up[...]
    packed[1:2, :D] = b_down[...]
    packed[2:5, :D] = taps[0]
    packed[5:6, :HEADS] = b_decay[...]


def pack_small(b_up, b_down, taps, b_decay):
    return pl.pallas_call(
        small_kernel,
        out_shape=jax.ShapeDtypeStruct((8, FF), f32),
        in_specs=[VMEM] * 4,
        out_specs=VMEM,
    )(b_up, b_down, taps, b_decay)


def pack_kernel(
    w_query, w_key, w_value, w_gate, w_out, w_decay, w_up, conditions, qk, vgd, upo, lifted
):
    qk[:, :D] = w_query[0]
    qk[:, D:] = w_key[0]
    vgd[:, :D] = w_value[0]
    vgd[:, D : 2 * D] = w_gate[0]
    place = jnp.where(row_iota(HEADS, LANES) == lane_iota(HEADS, LANES), 1.0, 0.0).astype(bf16)
    turned = lax.dot_general(
        w_decay[0], place, (((0,), (0,)), ((), ())), preferred_element_type=f32
    )
    vgd[:, 2 * D :] = turned.astype(bf16)
    upo[:, :FF] = w_up[0]
    upo[:, FF:] = w_out[0]
    values = jnp.concatenate([conditions[m].astype(f32) for m in range(MICRO)], axis=0)
    lifted[0] = (values * sigmoid(values)).astype(bf16)


def pack(*weights):
    shard = weights[0].shape[1]
    widths = (2 * D, 2 * D + LANES, FF + D)
    return pl.pallas_call(
        pack_kernel,
        out_shape=[jax.ShapeDtypeStruct((shard, width), bf16) for width in widths]
        + [jax.ShapeDtypeStruct((1, MICRO * SLOTS, D), bf16)],
        in_specs=[VMEM] * len(weights),
        out_specs=[VMEM] * (len(widths) + 1),
    )(*weights)


def join_kernel(bits, waits, *refs):
    count = len(bits)
    held, came, out = refs[:count], refs[count : 2 * count], refs[2 * count + waits :]
    for i, bit in enumerate(bits):
        mine = (lax.axis_index("row") >> bit) & 1
        out[i][:, mine] = held[i][...]
        out[i][:, 1 - mine] = came[i][...]


def join(held, came, bits, after=()):
    def parts(array, bit):
        axis = axis_of(bit)
        above = 1
        for size in array.shape[:axis]:
            above *= size
        return array.reshape((above, -1) + array.shape[-2:])

    split_held = [parts(array, bit) for array, bit in zip(held, bits)]
    split_came = [parts(array, bit) for array, bit in zip(came, bits)]
    out = pl.pallas_call(
        functools.partial(join_kernel, bits, len(after)),
        out_shape=[
            jax.ShapeDtypeStruct(array.shape[:1] + (2,) + array.shape[1:], array.dtype)
            for array in split_held
        ],
        in_specs=[VMEM] * (2 * len(held)) + [ANY] * len(after),
        out_specs=[VMEM] * len(held),
        compiler_params=pltpu.CompilerParams(vmem_limit_bytes=8 * 1024 * 1024),
        cost_estimate=pl.CostEstimate(flops=10**6, bytes_accessed=10**6, transcendentals=0),
    )(*split_held, *split_came, *after)
    joined = []
    for array, result, bit in zip(held, out, bits):
        shape = list(array.shape)
        shape[axis_of(bit)] = 2
        joined.append(result.reshape(shape))
    return joined


def lifted_kernel(mine, came, ada, out, kept, sem):
    copy = pltpu.make_async_copy(ada, kept, sem)
    copy.start()
    first = lax.axis_index("section") == 0
    pair = mine[0:SLOTS, :].astype(f32), came[0:SLOTS, :].astype(f32)
    grad = jnp.concatenate(
        [jnp.where(first, pair[0], pair[1]), jnp.where(first, pair[1], pair[0])], axis=0
    ).astype(bf16)
    copy.wait()
    out[...] = mm_t(grad, kept[...])


def lifted_grads(mine, came, ada):
    return pl.pallas_call(
        lifted_kernel,
        out_shape=jax.ShapeDtypeStruct((MICRO * SLOTS, D), f32),
        in_specs=[VMEM, VMEM, ANY],
        out_specs=VMEM,
        scratch_shapes=[pltpu.VMEM((D, 6 * D), bf16), pltpu.SemaphoreType.DMA],
        compiler_params=pltpu.CompilerParams(vmem_limit_bytes=16 * 1024 * 1024),
        cost_estimate=pl.CostEstimate(flops=10**9, bytes_accessed=2 << 20, transcendentals=0),
    )(mine, came, ada)


def term_kernel(*refs):
    *terms, stays, goes = refs
    stays[...] = sum(ref[:, 0] for ref in terms)
    goes[...] = sum(ref[:, 1] for ref in terms)


def term_step(below, *terms):
    tail = terms[0].shape[1:]
    above = terms[0].shape[0] // (2 * below)
    shape = jax.ShapeDtypeStruct((above, below) + tail, f32)
    out = pl.pallas_call(
        term_kernel,
        out_shape=[shape] * 2,
        in_specs=[VMEM] * len(terms),
        out_specs=[VMEM] * 2,
        compiler_params=pltpu.CompilerParams(vmem_limit_bytes=8 * 1024 * 1024),
        cost_estimate=pl.CostEstimate(flops=10**6, bytes_accessed=10**6, transcendentals=0),
    )(*[term.reshape((above, 2, below) + tail) for term in terms])
    return [array.reshape((above * below,) + tail) for array in out]


def step_kernel(bit, widths, counts, waits, *refs):
    mine = (lax.axis_index("row") >> bit) & 1
    count, many = len(widths), len(counts)
    refs = list(refs)
    take = lambda number: [refs.pop(0) for _ in range(number)]
    sources = take(count + many)
    take(waits)
    targets = take(count + 1)
    buffers = take(count + many)
    results = take(count + 1)
    in_sems, out_sems = refs
    arrive = [
        pltpu.make_async_copy(source, buffer, in_sems.at[i])
        for i, (source, buffer) in enumerate(zip(sources, buffers))
    ]
    leave = [
        pltpu.make_async_copy(result, target, out_sems.at[i])
        for i, (result, target) in enumerate(zip(results, targets))
    ]
    for copy in arrive:
        copy.start()
    kept, came = buffers[:count], buffers[count:]
    places = [(j, i) for j, number in enumerate(counts) for i in range(number)]
    goes = results[count]
    at = 0
    for i in range(count):
        j, place = places[i]
        arrive[i].wait()
        if place == 0:
            arrive[count + j].wait()
        start = sum(widths[i - place : i])
        columns = slice(start, start + widths[i])
        total = kept[i][:, 1 - mine] + came[j][:, 1 - mine, :, :, columns].astype(f32)
        goes[:, :, :, at : at + widths[i]] = total.astype(bf16)
        at += widths[i]
    leave[count].start()
    for i in range(count):
        j, place = places[i]
        start = sum(widths[i - place : i])
        columns = slice(start, start + widths[i])
        results[i][...] = kept[i][:, mine] + came[j][:, mine, :, :, columns].astype(f32)
        leave[i].start()
    for copy in leave:
        copy.wait()


def step(kept, came, bit, below=1, after=()):
    blocks, rows = kept[0].shape[0] // 2, kept[0].shape[1]
    above = blocks // below
    paired = lambda array: array.reshape((above, 2, below) + array.shape[1:])
    widths = [array.shape[2] for array in kept]
    size = sum(array.size for array in kept)
    arrays = [paired(array) for array in kept] + [paired(array) for array, _ in came]
    shapes = [((above, below, rows, width), f32) for width in widths]
    shapes.append(((above, below, rows, sum(widths)), bf16))
    out = pl.pallas_call(
        functools.partial(step_kernel, bit, widths, [count for _, count in came], len(after)),
        out_shape=[jax.ShapeDtypeStruct(shape, kind) for shape, kind in shapes],
        in_specs=[HBM] * len(kept) + [ANY] * (len(came) + len(after)),
        out_specs=[HBM] * len(kept) + [ANY],
        scratch_shapes=[pltpu.VMEM(array.shape, array.dtype) for array in arrays]
        + [pltpu.VMEM(shape, kind) for shape, kind in shapes]
        + [pltpu.SemaphoreType.DMA((len(arrays),)), pltpu.SemaphoreType.DMA((len(shapes),))],
        compiler_params=pltpu.CompilerParams(vmem_limit_bytes=10 * 1024 * 1024),
        cost_estimate=pl.CostEstimate(flops=size, bytes_accessed=8 * size, transcendentals=0),
    )(*arrays, *after)
    count = len(kept)
    flat_blocks = [array.reshape((blocks,) + array.shape[2:]) for array in out]
    return flat_blocks[:count], flat_blocks[count]


def misc_step_kernel(held, arrived, out):
    size = held.shape[0] - SUMS
    out[:size, :] = held[:size, :]
    out[size : 2 * size, :] = arrived[:size, :]
    high, low = split(misc_sums(held, arrived))
    out[2 * size : 2 * size + SUMS // 2, :] = high
    out[2 * size + SUMS // 2 :, :] = low


def misc_step(held, arrived):
    return pl.pallas_call(
        misc_step_kernel,
        out_shape=jax.ShapeDtypeStruct((2 * held.shape[0] - SUMS, 2 * D), bf16),
        in_specs=[VMEM] * 2,
        out_specs=VMEM,
        cost_estimate=pl.CostEstimate(flops=10**5, bytes_accessed=10**5, transcendentals=0),
    )(held, arrived)


def misc_sums(*refs):
    size = refs[0].shape[0] - SUMS
    parts = [ref[size:, :].astype(f32) for ref in refs]
    return sum(part[: SUMS // 2] + part[SUMS // 2 :] for part in parts)


SUMS = 32
OWN = 16


def misc_kernel(mod_one, mod_two, sums_one, sums_two, out):
    rows = []
    for mod in (mod_one, mod_two):
        for slot in range(SLOTS):
            for i in range(3):
                part = mod[slot : slot + 1, i * 2 * D : (i + 1) * 2 * D]
                rows.append(part.astype(f32))
        rows.append(jnp.zeros((OWN // 2 - 3 * SLOTS, 2 * D), f32))
    sums = jnp.concatenate([sums_one[...], sums_two[...]], axis=0)
    rows.extend(part.astype(f32) for part in split(sums))
    out[...] = jnp.concatenate(rows, axis=0).astype(bf16)


def pack_misc(mod_one, mod_two, sums_one, sums_two):
    return pl.pallas_call(
        misc_kernel,
        out_shape=jax.ShapeDtypeStruct((OWN + SUMS, 2 * D), bf16),
        in_specs=[VMEM] * 4,
        out_specs=VMEM,
    )(mod_one, mod_two, sums_one, sums_two)


def finish_kernel(widths, counts, waits, *refs):
    count = len(widths)
    kept, refs = refs[:count], refs[count:]
    came, refs = refs[: len(counts)], refs[len(counts) :]
    lifted, misc, misc_came = refs[:3]
    mine, other, small_mine, small_other = refs[3 + waits :]
    places = [(ref, i) for ref, many in zip(came, counts) for i in range(many)]
    added = []
    for i in range(count):
        ref, place = places[i]
        start = sum(widths[i - place : i])
        added.append(kept[i][0] + ref[0, :, start : start + widths[i]].astype(f32))
    a1, f1, f2, a2 = added
    size = misc.shape[0] - SUMS
    rows = jnp.concatenate([misc[:size, :], misc_came[:size, :]], axis=0)
    rows = rows.astype(f32).reshape(-1, OWN, 2 * D)

    def ada(first):
        columns = []
        for i in range(3):
            both = [rows[:, first + 3 * slot + i, :] for slot in range(SLOTS)]
            columns.append(mm(lifted[...], jnp.concatenate(both, axis=0).astype(bf16)))
        return jnp.concatenate(columns, axis=1)

    first = lax.axis_index("section") == 0
    at = 0
    for one, two in ((a1, a2), (f1, f2), (ada(0), ada(OWN // 2))):
        columns = slice(at, at + one.shape[1])
        mine[:, columns] = jnp.where(first, one, two)
        other[:, columns] = jnp.where(first, two, one)
        at += one.shape[1]
    total = misc_sums(misc, misc_came)
    one, two = total[0:8, :], total[8:16, :]
    small_mine[...] = jnp.where(first, one, two)
    small_other[...] = jnp.where(first, two, one)


def finish(kept, came, lifted, misc, misc_came, after):
    widths = [array.shape[2] for array in kept]
    shard = kept[0].shape[1]
    wide = GROUP + FF + 6 * D
    arrays = [array for array, _ in came]
    shapes = [(shard, wide)] * 2 + [(8, 2 * D)] * 2
    return pl.pallas_call(
        functools.partial(finish_kernel, widths, [count for _, count in came], len(after)),
        out_shape=[jax.ShapeDtypeStruct(shape, f32) for shape in shapes],
        in_specs=[VMEM] * (len(kept) + len(came) + 3) + [ANY] * len(after),
        out_specs=[VMEM] * 4,
        compiler_params=pltpu.CompilerParams(vmem_limit_bytes=8 * 1024 * 1024),
    )(*kept, *arrays, lifted, misc, misc_came, *after)


def output_kernel(mine, other, small_mine, small_other, *outs):
    first = lax.axis_index("section") == 0

    def halves(start, width):
        columns = slice(start, start + width)
        pair = mine[:, columns], other[:, columns]
        return jnp.where(first, pair[0], pair[1]), jnp.where(first, pair[1], pair[0])

    attn = halves(0, GROUP)
    cut = GROUP - 2 * D
    outs[0][...] = attn[0][:, :D]
    outs[1][...] = attn[0][:, D : 2 * D]
    outs[2][:, :cut] = attn[0][:, 2 * D :]
    outs[2][:, cut:] = attn[1][:, : D - cut]
    outs[3][...] = attn[1][:, D - cut : 2 * D - cut]
    outs[4][...] = attn[1][:, 2 * D - cut : 3 * D - cut]
    decay = jnp.transpose(attn[1][:, 3 * D - cut :])
    for head in range(HEADS):
        outs[5][head] = decay[head : head + 1, :]
    up = halves(GROUP, FF // 2)
    outs[6][:, : FF // 2] = up[0]
    outs[6][:, FF // 2 :] = up[1]
    for piece in range(2):
        down = halves(GROUP + FF // 2 + piece * D, D)
        outs[7][piece] = down[0]
        outs[7][2 + piece] = down[1]
    outs[8][...] = mine[:, GROUP + FF :] + other[:, GROUP + FF :]
    small = small_mine[...] + small_other[...]
    half = 2 * D
    for i in range(3):
        outs[9][:, i * half : (i + 1) * half] = small[i : i + 1, :]
    for i in range(2):
        outs[10][:, i * half : (i + 1) * half] = small[3 + i : 4 + i, :]
    outs[11][...] = small[5:6, :D]
    outs[12][0] = small[5:6, D:]
    outs[12][1] = small[6:7, :D]
    outs[12][2] = small[6:7, D:]
    outs[13][...] = small[7:8, :HEADS]


def outputs(mine, other, small_mine, small_other):
    shard = mine.shape[0]
    shapes = (
        [(shard, D)] * 5
        + [(HEADS, 1, shard), (shard, FF), (4, shard, D), (shard, 6 * D)]
        + [(1, 6 * D), (1, FF), (1, D), (3, 1, D), (1, HEADS)]
    )
    return pl.pallas_call(
        output_kernel,
        out_shape=[jax.ShapeDtypeStruct(shape, f32) for shape in shapes],
        in_specs=[VMEM] * 4,
        out_specs=[VMEM] * len(shapes),
    )(mine, other, small_mine, small_other)


def both_kernel(one, two, came, out, kept, sems):
    section = lax.axis_index("section")

    def move(mine, layer):
        arrive = [
            pltpu.make_async_copy(mine, kept.at[layer], sems.at[0]),
            pltpu.make_async_copy(came, kept.at[1 - layer], sems.at[1]),
        ]
        leave = [
            pltpu.make_async_copy(kept.at[layer], out.at[layer], sems.at[2]),
            pltpu.make_async_copy(kept.at[1 - layer], out.at[1 - layer], sems.at[3]),
        ]
        for copy in arrive:
            copy.start()
        for copy, after in zip(arrive, leave):
            copy.wait()
            after.start()
        for copy in leave:
            copy.wait()

    @pl.when(section == 0)
    def _():
        move(one, 0)

    @pl.when(section == 1)
    def _():
        move(two, 1)


def both_micros(one, two, came):
    return pl.pallas_call(
        both_kernel,
        out_shape=jax.ShapeDtypeStruct((MICRO,) + one.shape, one.dtype),
        in_specs=[ANY] * 3,
        out_specs=ANY,
        scratch_shapes=[
            pltpu.VMEM((MICRO,) + one.shape, one.dtype),
            pltpu.SemaphoreType.DMA((4,)),
        ],
    )(one, two, came)


def swap(values):
    return lax.ppermute(values, "section", [(0, 1), (1, 0)])


def row_bits():
    bits = lax.axis_size("row").bit_length() - 1
    third = bits // 3
    return (
        tuple(range(third)),
        tuple(range(third, 2 * third)),
        tuple(range(2 * third, bits)),
    )


def partner(values, bit):
    size = lax.axis_size("row")
    return lax.ppermute(values, "row", [(i, i ^ (1 << bit)) for i in range(size)])


def axis_of(bit):
    return lax.axis_size("row").bit_length() - 2 - bit


def bit_of(bit):
    return (lax.axis_index("row") >> bit) & 1


def single(values):
    return values.reshape((1,) * (lax.axis_size("row").bit_length() - 1) + values.shape)


def gather_steps(along_x, along_y, along_z):
    steps = [(bit, bit) for bit in reversed(along_z)]
    return steps + list(zip(along_x + along_y, along_y + along_x))


def flat(held):
    return held.reshape(-1, held.shape[-1])


def lock(*arrays):
    return lax.optimization_barrier(arrays)


def on_device(
    tokens, conditions, output_grad, layouts,
    w_ada, b_ada, w_query, w_key, w_value, w_gate, w_out, w_decay, b_decay, conv_kernel,
    w_up, b_up, w_down, b_down,
):
    section = lax.axis_index("section")
    devices = lax.axis_size("row")
    shard = w_query.shape[1]
    along_x, along_y, along_z = row_bits()

    def both(values):
        return values, swap(values)

    qk, vgd, upo, lifted = pack(
        w_query, w_key, w_value, w_gate, w_out, w_decay.transpose(0, 2, 1), w_up, conditions
    )
    small = pack_small(b_up, b_down, conv_kernel, b_decay)
    steps = gather_steps(along_x, along_y, along_z)
    lag = len(along_z)
    order = tuple(reversed(along_z)) + along_x + along_y
    term_bits = along_x + along_y + along_z
    spans = len(steps) + lag - 4
    bounds = [(len(term_bits) * i + spans // 2) // spans for i in range(spans + 1)]
    term_bits = [term_bits[bounds[i] : bounds[i + 1]] for i in range(spans)]
    left = list(order)
    groups = [[single(qk), single(vgd)], [single(upo), single(w_down[0])]]
    for place in range(len(steps) + lag):
        numbers = [g for g in range(2) if 0 <= place - g * lag < len(steps)]
        bits = [bit for g in numbers for bit in steps[place - g * lag]]
        held = [array for g in numbers for array in groups[g]]
        came = [partner(array, bit) for array, bit in zip(held, bits)]
        if place < 2:
            after = (small,)
        elif place == 2:
            for bit in order:
                lifted = jnp.concatenate([lifted, partner(lifted, bit)], axis=0)
            after = (lifted,)
        elif place < 3 + spans:
            if place == 3:
                lifted_cut = lax.dynamic_slice_in_dim(
                    lifted, lax.axis_index("row") * shard, shard, 2
                )
                product = mm(lifted_cut.reshape(devices * MICRO * SLOTS, shard), w_ada[0])
                terms = (product.reshape(devices, MICRO * SLOTS, 6 * D),)
            for bit in term_bits[place - 3]:
                stays, goes = term_step(1 << left.index(bit), *terms)
                left.remove(bit)
                terms = (stays, partner(goes, bit))
            after = (terms[1],)
        else:
            mods = both(sum(term[0] for term in terms) + b_ada[0])
            smalls = both(small)
            x = tokens
            *saved, gated = attn_forward(0, layouts, x, mods, smalls, qk, vgd)
            after = (gated,)
        held = join(held, came, bits, after)
        for g in numbers:
            groups[g], held = held[:2], held[2:]
        if place == len(steps) - 1:
            qk, vgd = [both(flat(array)) for array in groups[0]]
    upo, down = [both(flat(array)) for array in groups[1]]
    kept = []
    acts = []
    for l in range(2):
        if l:
            *saved, gated = attn_forward(l, layouts, x, mods, smalls, qk, vgd)
        out, branch, down_raw, *acts_sent = ffn_forward(
            l, layouts, x, mods, smalls, gated, upo, down
        )
        kept.append((x, saved, gated, branch, down_raw))
        acts.append(out)
        x = out[None]

    late, _ = lock(w_ada[0], acts[0])
    ada_all = lax.all_gather(late, "row", axis=0, tiled=True)

    def ffn_step(l, grad, after=()):
        x, saved, gated, branch, down_raw = kept[l]
        mid_grad, branch_low, gwo, sums, *terms = ffn_backward(
            l, layouts, x, mods, smalls, gated, branch, down_raw, grad, upo, down, devices, after
        )
        if terms[0].ndim == 2:
            up_sum = terms[0].reshape(devices, shard, 2, FF // 2)
            down_sum = terms[1].reshape(devices, 2, 2, shard, D)
            terms = []
            for own in (section, 1 - section):
                up_half = lax.dynamic_index_in_dim(up_sum, own, 2, keepdims=False)
                down_half = lax.dynamic_index_in_dim(down_sum, own, 1, keepdims=False)
                terms.append(
                    jnp.concatenate([up_half, down_half[:, 0], down_half[:, 1]], axis=2)
                )
            terms[1] = terms[1].astype(bf16)
        return [branch_low, gwo], mid_grad, terms[0], terms[1], sums

    def mixer_step(l, carried, after=()):
        low, keep, sent, sums = mixer_backward(
            l, layouts, smalls, kept[l][1], *carried, upo, after
        )
        by_row = lambda array: array.reshape(devices, shard, GROUP)
        return low, by_row(keep), by_row(sent), sums

    def input_step(l, low, mid_grad, ffn_sums, mixer_sums, two=None, after=()):
        x = kept[l][0]
        return input_backward(
            l, layouts, x, mods, low, mid_grad, ffn_sums, mixer_sums, qk, vgd, two, after
        )

    def run(keep, came, bits, below=1, after=()):
        for bit in bits[:-1]:
            keep, sent = step(keep, came, bit, below, after)
            came = [(partner(sent, bit), len(keep))]
        return step(keep, came, bits[-1], below, after)

    def grown(mod, bits):
        for bit in bits:
            mod = misc_step(mod, partner(mod, bit))
        return mod

    x_bits, y_bits, z_bits = along_x, along_y, along_z
    lifted = lifted_cut.reshape(devices, MICRO, SLOTS, shard)
    lifted = lax.dynamic_index_in_dim(lifted, section, 1, keepdims=False)
    lifted = lifted.transpose(2, 1, 0).reshape(shard, SLOTS * devices)

    carried, mid_grad, f2_keep, f2_sent, f2_sums = ffn_step(1, output_grad)
    *carried, f2_sent, acts_sent, lifted = lock(*carried, f2_sent, acts_sent[0], lifted)
    f2_came = swap(f2_sent)
    acts_came = swap(acts_sent)
    low, a2_keep, a2_sent, m2_sums = mixer_step(1, carried)
    low, a2_sent, f2_came, acts_came = lock(low, a2_sent, f2_came, acts_came)
    a2_came = swap(a2_sent)
    gx_two, grad, mod_low_two, sums_two = input_step(1, low, mid_grad, f2_sums, m2_sums)
    grad, a2_came = lock(grad, a2_came)
    f2_keep, f2_sent = run([f2_keep], [(f2_came, 1)], x_bits)
    a2_keep, a2_sent = run([a2_keep], [(a2_came, 1)], y_bits, 1 << len(x_bits))
    grad, f2_sent, a2_sent = lock(grad, f2_sent, a2_sent)
    f2_came = partner(f2_sent, x_bits[-1])
    a2_came = partner(a2_sent, y_bits[-1])

    carried, mid_grad, f1_keep, f1_sent, f1_sums = ffn_step(0, grad[None])
    *carried, f1_sent, f2_came, a2_came = lock(*carried, f1_sent, f2_came, a2_came)
    f1_came = swap(f1_sent)
    f2_keep, f2_sent = run(f2_keep, [(f2_came, 1)], y_bits)
    a2_keep, a2_sent = run(a2_keep, [(a2_came, 1)], x_bits)
    f1_keep, f1_sent = run([f1_keep], [(f1_came, 1)], x_bits)
    *carried, f2_sent, a2_sent, f1_sent = lock(*carried, f2_sent, a2_sent, f1_sent)
    f1_came = partner(f1_sent, x_bits[-1])
    a2_came = partner(a2_sent, x_bits[-1])
    f2_came = partner(f2_sent, y_bits[-1])
    low, a1_keep, a1_sent, m1_sums = mixer_step(0, carried)
    low, a1_sent, f2_came, a2_came, f1_came, ada_all = lock(
        low, a1_sent, f2_came, a2_came, f1_came, ada_all
    )
    a1_came = swap(a1_sent)
    two_keep, two_sent = run(f2_keep + a2_keep, [(f2_came, 1), (a2_came, 1)], z_bits[:1])
    f1_keep, f1_sent = run(f1_keep, [(f1_came, 1)], y_bits)
    a1_keep, a1_sent = run([a1_keep], [(a1_came, 1)], x_bits)
    low, two_sent, f1_sent, a1_sent = lock(low, two_sent, f1_sent, a1_sent)
    a1_came = partner(a1_sent, x_bits[-1])
    f1_came = partner(f1_sent, y_bits[-1])
    two_came = partner(two_sent, z_bits[0])
    gx_one, _, mod_low_one, sums_one, gx_sent, mod_mine, mod_sent = input_step(
        0, low, mid_grad, f1_sums, m1_sums, (gx_two, mod_low_two)
    )
    misc = pack_misc(mod_low_one, mod_low_two, sums_one, sums_two)
    misc, a1_came, two_came, f1_came, gx_sent, mod_sent = lock(
        misc, a1_came, two_came, f1_came, gx_sent, mod_sent
    )

    a1_keep, a1_sent = run(a1_keep, [(a1_came, 1)], y_bits)
    a1_sent, misc = lock(a1_sent, misc)
    a1_came = partner(a1_sent, y_bits[-1])
    misc = grown(misc, tuple(reversed(z_bits))[:-1])
    gx_came = swap(gx_sent)
    mod_came = swap(mod_sent)
    keep, came = a1_keep + f1_keep, [(a1_came, 1), (f1_came, 1)]
    for place, bit in enumerate(z_bits):
        if place == 1:
            keep, came = keep + two_keep, came + [(two_came, 2)]
        keep, sent = step(keep, came, bit)
        if place == len(z_bits) - 1:
            sent, misc, gx_came, mod_came = lock(sent, misc, gx_came, mod_came)
        elif place == 0:
            sent, misc = lock(sent, misc)
        came = [(partner(sent, bit), len(keep))]
        if place == 0:
            misc = grown(misc, z_bits[:1] + (x_bits + y_bits)[:-1])
    misc_came = partner(misc, y_bits[-1])
    gx_out = both_micros(gx_one, gx_two, gx_came)
    acts_out = both_micros(acts[0], acts[1], acts_came)
    grad_lifted = lifted_grads(mod_mine, mod_came, ada_all)
    lifted_came = swap(grad_lifted)
    mine, other, small_mine, small_other = finish(
        keep, came, lifted, misc, misc_came, (gx_out, acts_out, lifted_came)
    )
    came, small_came = swap(other), swap(small_other)
    (
        g_query, g_key, g_value, g_gate, g_out, g_decay, g_up, g_down, g_ada,
        g_b_ada, g_b_up, g_b_down, g_conv, g_b_decay,
    ) = outputs(mine, came, small_mine, small_came)

    grad_lifted = (grad_lifted + lifted_came).reshape(MICRO, SLOTS, D)
    _, pull_silu = jax.vjp(jax.nn.silu, conditions.astype(f32))
    (cond_grads,) = pull_silu(grad_lifted)

    return (
        acts_out[None],
        gx_out[None],
        cond_grads,
        g_ada[None],
        g_b_ada,
        g_query[None],
        g_key[None],
        g_value[None],
        g_gate[None],
        g_out[None],
        g_decay.transpose(1, 2, 0),
        g_b_decay,
        g_conv.transpose(1, 0, 2),
        g_up[None],
        g_b_up,
        g_down.reshape(1, FF // devices, D),
        g_b_down,
    )


def solution(mesh):
    rows = P(None, "row", None)
    mats = P("section", "row", None)
    vector = P("section", None)
    in_specs = (
        rows, rows, rows, P(None, "row"),
        mats, vector, mats, mats, mats, mats, mats, mats, vector, P("section", None, None),
        mats, vector, mats, vector,
    )
    blocks = P("section", None, "row", None)
    out_specs = (
        blocks, blocks, rows,
        mats, vector, mats, mats, mats, mats, mats, mats, vector, P("section", None, None),
        mats, vector, mats, vector,
    )
    return jax.shard_map(
        on_device, mesh=mesh, in_specs=in_specs, out_specs=out_specs, check_vma=False
    )
```

profile of v0, /device:TPU:0, one launch (start us, length us, event | category | flops | bytes accessed | tf_op | source)
XLA Modules:
  0.0 285.0 jit_solution(2979841468044272249)
XLA Ops:
  9.1 4.0 %collective-permute-start = (bf16[1,4,384]{2,1,0:T(4,128)(2,1)}, bf16[1,4,384]{2,1,0:T(4,128)(2,1)S(1)}, u32[]{:S(2)}, u32[]{:S(2)}) collective-permute-start(bf16[1,4,384]{2,1,0:T(4,128)(2,1)} %get-tuple-element.192), channel_id=1, source_target_pairs={{0,8},{1,9},{2,10},{3,11},{4,12},{5,13},{6,14},{7,15},{8,0},{9,1},... | collective-permute-start | bytes 9224 | tf_op jit(solution)/shard_map/ppermute | solution.py:1369
  13.2 2.9 %collective-permute-start.10 = (bf16[1,1,1,1,24,896]{5,4,3,2,1,0:T(8,128)(2,1)}, bf16[1,1,1,1,24,896]{5,4,3,2,1,0:T(8,128)(2,1)S(1)}, u32[]{:S(2)}, u32[]{:S(2)}) collective-permute-start(bf16[1,1,1,1,24,896]{5,4,3,2,1,0:T(8,128)(2,1)} %bitcast.229), channel_id=1, source_target_pairs={{0,8},{1,9},{2,10},{3,11},{4,12},{5,13},{6,14},{7,15},{8,0},{9,1},... | collective-permute-start | bytes 129032 | tf_op jit(solution)/shard_map/ppermute | solution.py:1369
  26.0 2.2 collective-permute-done.2
  35.1 2.2 collective-permute-done.11
  44.0 2.6 collective-permute-start.16
  46.6 5.2 %collective-permute-done.16 = bf16[1,1,1,1,96,384]{5,4,3,2,1,0:T(8,128)(2,1)S(1)} collective-permute-done((bf16[1,1,1,1,96,384]{5,4,3,2,1,0:T(8,128)(2,1)S(1)}, bf16[1,1,1,1,96,384]{5,4,3,2,1,0:T(8,128)(2,1)S(1)}, u32[]{:S(2)}, u32[]{:S(2)}) %collective-permute-start.16) | collective-permute-done | bytes 73760 | tf_op jit(solution)/shard_map/ppermute | solution.py:1369
  57.4 5.3 %collective-permute-done.20 = bf16[2,1,1,1,96,384]{5,4,0,3,2,1:T(8,128)(2,1)S(1)} collective-permute-done((bf16[2,1,1,1,96,384]{5,4,0,3,2,1:T(8,128)(2,1)S(1)}, bf16[2,1,1,1,96,384]{5,4,0,3,2,1:T(8,128)(2,1)S(1)}, u32[]{:S(2)}, u32[]{:S(2)}) %collective-permute-start.20) | collective-permute-done | bytes 147488 | tf_op jit(solution)/shard_map/ppermute | solution.py:1369
  65.7 2.3 collective-permute-start.25
  68.8 3.7 %collective-permute-done.6 = f32[2,4,2304]{2,1,0:T(4,128)S(1)} collective-permute-done((f32[2,4,2304]{2,1,0:T(4,128)S(1)}, f32[2,4,2304]{2,1,0:T(4,128)S(1)}, u32[]{:S(2)}, u32[]{:S(2)}) %collective-permute-start.6) | collective-permute-done | bytes 73760 | tf_op jit(solution)/shard_map/ppermute | solution.py:1369
  74.2 3.6 %collective-permute-done.7.refs_4_ = f32[1,4,2304]{2,1,0:T(4,128)S(1)} collective-permute-done((f32[1,4,2304]{2,1,0:T(4,128)S(1)}, f32[1,4,2304]{2,1,0:T(4,128)S(1)}, u32[]{:S(2)}, u32[]{:S(2)}) %collective-permute-start.7) | collective-permute-done | bytes 36896 | tf_op jit(solution)/shard_map/ppermute | solution.py:1369
  81.9 9.1 %shard_map.315 = (bf16[512,384]{1,0:T(8,128)(2,1)}, f32[512,1536]{1,0:T(8,128)}, f32[512,128]{1,0:T(8,128)}, f32[512,384]{1,0:T(8,128)}, f32[512,128]{1,0:T(8,12...) custom-call(s32[2,1]{1,0:T(2,128)} %copy.48.refs_0_, bf16[2,512,384]{2,1,0:T(8,128)(2,1)} %refs_6_.3, ...), custom_call_target="tpu_custom_call" | custom-call | flops 4000000000 | bytes 4194304 | tf_op jit(solution)/shard_map/pallas_call | solution.py:735
  91.0 2.8 collective-permute-done.27
  93.8 3.1 %collective-permute-done.26 = bf16[2,2,1,2,24,1920]{5,4,3,1,0,2:T(8,128)(2,1)S(1)} collective-permute-done((bf16[2,2,1,2,24,1920]{5,4,3,1,0,2:T(8,128)(2,1)S(1)}, bf16[2,2,1,2,24,1920]{5,4,3,1,0,2:T(8,128)(2,1)S(1)}, u32[]{:S(2)}, u32[]{:S(2)}) %collective-permute-start.26) | collective-permute-done | bytes 737312 | tf_op jit(solution)/shard_map/ppermute | solution.py:1369
  100.1 4.6 %collective-permute-done.29.refs_12_ = bf16[1536,384]{1,0:T(8,128)(2,1)S(1)} collective-permute-done((bf16[1536,384]{1,0:T(8,128)(2,1)}, bf16[1536,384]{1,0:T(8,128)(2,1)S(1)}, u32[]{:S(2)}, u32[]{:S(2)}) %collective-permute-start.29) | collective-permute-done | bytes 1179680 | tf_op jit(solution)/shard_map/ppermute | solution.py:1354
  106.9 6.6 %shard_map.318 = (bf16[512,384]{1,0:T(8,128)(2,1)}, f32[512,384]{1,0:T(8,128)}, f32[512,384]{1,0:T(8,128)}) custom-call(s32[2,1]{1,0:T(2,128)} %copy.48.refs_0_, bf16[512,384]{1,0:T(8,128)(2,1)} %get-tuple-element.214.refs_4_.refs_1_.refs_13_, bf16[2,512,384]{2,1,0:T(8,128)(2,1)} %refs_6_.3, bf16[384,1920]{1,0:T(8,128)(2,1)} %bitcast.67.refs_3_.refs_9_.refs_2_, ...), custom_call_target="tpu_custom_call" | custom-call | flops 3000000000 | bytes 4194304 | tf_op jit(solution)/shard_map/pallas_call | solution.py:735
  113.4 9.8 %shard_map.319 = (bf16[512,384]{1,0:T(8,128)(2,1)}, f32[512,1536]{1,0:T(8,128)}, f32[512,128]{1,0:T(8,128)}, f32[512,384]{1,0:T(8,128)}, f32[512,128]{1,0:T(8,12...) custom-call(s32[2,1]{1,0:T(2,128)} %copy.48.refs_0_, bf16[1,512,384]{2,1,0:T(8,128)(2,1)} %bitcast.247, ...), custom_call_target="tpu_custom_call" | custom-call | flops 4000000000 | bytes 4194304 | tf_op jit(solution)/shard_map/pallas_call | solution.py:735
  123.3 6.8 %shard_map.320 = (bf16[512,384]{1,0:T(8,128)(2,1)}, f32[512,384]{1,0:T(8,128)}, f32[512,384]{1,0:T(8,128)}, bf16[512,384]{1,0:T(8,128)(2,1)}) custom-call(s32[2,1]{1,0:T(2,128)} %copy.48.refs_0_, bf16[512,384]{1,0:T(8,128)(2,1)} %get-tuple-element.222.refs_1_.refs_13_, bf16[1,512,384]{2,1,0:T(8,128)(2,1)} %bitcast.248, ...), custom_call_target="tpu_custom_call" | custom-call | flops 3000000000 | bytes 4194304 | tf_op jit(solution)/shard_map/pallas_call | solution.py:735
  130.1 13.2 %shard_map.321 = (f32[512,384]{1,0:T(8,128)}, bf16[512,384]{1,0:T(8,128)(2,1)}, f32[384,384]{1,0:T(8,128)}, f32[8,1536]{1,0:T(8,128)}, f32[16,24,1536]{2,1,0:T(8,128)}, /*index=5*/bf16[16,24,1536]{2,1,0:T(8,128)(2,1)}) custom-call(s32[2,1]{1,0:T(2,128)} %copy.48.refs_0_, f32[4,2304]{1,0:T(4,128)} %copy-done.25, f32[4,2304]{1,0:T(4,128)} %copy-done.32, ...), custom_call_target="tpu_custom_call" | custom-call | flops 5000000000 | bytes 4194304 | tf_op jit(solution)/shard_map/pallas_call | solution.py:735
  143.9 15.4 %shard_map.322 = (bf16[512,1664]{1,0:T(8,128)(2,1)}, f32[384,1024]{1,0:T(8,128)}, bf16[384,1024]{1,0:T(8,128)(2,1)}, f32[8,384]{1,0:T(8,128)}) custom-call(s32[2,1]{1,0:T(2,128)} %copy.48.refs_0_, bf16[512,384]{1,0:T(8,128)(2,1)} %get-tuple-element.230.refs_1_, bf16[384,1920]{1,0:T(8,128)(2,1)} %bitcast.67.refs_3_.refs_9_.refs_2_, ...), custom_call_target="tpu_custom_call" | custom-call | flops 7000000000 | bytes 4194304 | tf_op jit(solution)/shard_map/pallas_call | solution.py:735
  160.6 6.8 %shard_map.324 = (f32[512,384]{1,0:T(8,128)}, bf16[512,384]{1,0:T(8,128)(2,1)}, bf16[8,2304]{1,0:T(8,128)(2,1)}, f32[8,768]{1,0:T(8,128)}) custom-call(s32[2,1]{1,0:T(2,128)} %copy.48.refs_0_, bf16[512,1664]{1,0:T(8,128)(2,1)} %get-tuple-element.244.refs_1_, bf16[384,768]{1,0:T(8,128)(2,1)} %bitcast.53.refs_4_.refs_2_, ...), custom_call_target="tpu_custom_call" | custom-call | flops 2000000000 | bytes 4194304 | tf_op jit(solution)/shard_map/pallas_call | solution.py:735
  169.4 13.0 %shard_map.327 = (f32[512,384]{1,0:T(8,128)}, bf16[512,384]{1,0:T(8,128)(2,1)}, f32[384,384]{1,0:T(8,128)}, f32[8,1536]{1,0:T(8,128)}, f32[16,24,1536]{2,1,0:T(8,128)}, /*index=5*/bf16[16,24,1536]{2,1,0:T(8,128)(2,1)}) custom-call(s32[2,1]{1,0:T(2,128)} %copy.48.refs_0_, f32[4,2304]{1,0:T(4,128)} %copy-done.25, f32[4,2304]{1,0:T(4,128)} %copy-done.32, ...), custom_call_target="tpu_custom_call" | custom-call | flops 5000000000 | bytes 4194304 | tf_op jit(solution)/shard_map/pallas_call | solution.py:735
  182.4 2.1 collective-permute-done.33
  192.6 15.3 %shard_map.331 = (bf16[512,1664]{1,0:T(8,128)(2,1)}, f32[384,1024]{1,0:T(8,128)}, bf16[384,1024]{1,0:T(8,128)(2,1)}, f32[8,384]{1,0:T(8,128)}) custom-call(s32[2,1]{1,0:T(2,128)} %copy.48.refs_0_, bf16[512,384]{1,0:T(8,128)(2,1)} %get-tuple-element.276.refs_1_, bf16[384,1920]{1,0:T(8,128)(2,1)} %bitcast.67.refs_3_.refs_9_.refs_2_, ...), custom_call_target="tpu_custom_call" | custom-call | flops 7000000000 | bytes 4194304 | tf_op jit(solution)/shard_map/pallas_call | solution.py:735
  208.6 3.2 %collective-permute-done.38 = bf16[8,24,1536]{2,1,0:T(8,128)(2,1)S(1)} collective-permute-done((bf16[8,24,1536]{2,1,0:T(8,128)(2,1)}, bf16[8,24,1536]{2,1,0:T(8,128)(2,1)S(1)}, u32[]{:S(2)}, u32[]{:S(2)}) %collective-permute-start.38) | collective-permute-done | bytes 589856 | tf_op jit(solution)/shard_map/ppermute | solution.py:1369
  219.5 5.8 %shard_map.335 = (f32[512,384]{1,0:T(8,128)}, bf16[512,384]{1,0:T(8,128)(2,1)}, bf16[8,2304]{1,0:T(8,128)(2,1)}, f32[8,768]{1,0:T(8,128)}, f32[512,384]{1,0:T(8,...) custom-call(s32[2,1]{1,0:T(2,128)} %copy.48.refs_0_, bf16[512,1664]{1,0:T(8,128)(2,1)} %get-tuple-element.303.refs_1_, ...), custom_call_target="tpu_custom_call" | custom-call | flops 2000000000 | bytes 4194304 | tf_op jit(solution)/shard_map/pallas_call | solution.py:735
  229.8 2.4 collective-permute-start.44
  232.2 4.7 %collective-permute-done.44.arrived = bf16[48,768]{1,0:T(8,128)(2,1)S(1)} collective-permute-done((bf16[48,768]{1,0:T(8,128)(2,1)}, bf16[48,768]{1,0:T(8,128)(2,1)S(1)}, u32[]{:S(2)}, u32[]{:S(2)}) %collective-permute-start.44) | collective-permute-done | bytes 73760 | tf_op jit(solution)/shard_map/ppermute | solution.py:1369
  242.6 3.8 %collective-permute-done.46.arrived = bf16[64,768]{1,0:T(8,128)(2,1)S(1)} collective-permute-done((bf16[64,768]{1,0:T(8,128)(2,1)}, bf16[64,768]{1,0:T(8,128)(2,1)S(1)}, u32[]{:S(2)}, u32[]{:S(2)}) %collective-permute-start.46) | collective-permute-done | bytes 98336 | tf_op jit(solution)/shard_map/ppermute | solution.py:1369
  249.3 4.8 %collective-permute-done.47.arrived = bf16[96,768]{1,0:T(8,128)(2,1)S(1)} collective-permute-done((bf16[96,768]{1,0:T(8,128)(2,1)}, bf16[96,768]{1,0:T(8,128)(2,1)S(1)}, u32[]{:S(2)}, u32[]{:S(2)}) %collective-permute-start.47) | collective-permute-done | bytes 147488 | tf_op jit(solution)/shard_map/ppermute | solution.py:1369
  256.5 2.4 shard_map.340
  265.9 2.4 shard_map.343.refs_8_
  275.9 2.1 shard_map.346
  (213 shorter events, 96.0 us)
Async XLA Ops:
  7.2 200.7 %all-gather.2.cloned.1.call-start = ((), (), s32[]{:S(2)}) async-start(), calls=%async_computation | async-start | bytes 1880064 | tf_op jit(solution)/shard_map/all_gather | solution.py:1471
  9.1 10.3 %collective-permute-start = (bf16[1,4,384]{2,1,0:T(4,128)(2,1)}, bf16[1,4,384]{2,1,0:T(4,128)(2,1)S(1)}, u32[]{:S(2)}, u32[]{:S(2)}) collective-permute-start(bf16[1,4,384]{2,1,0:T(4,128)(2,1)} %get-tuple-element.192), channel_id=1, source_target_pairs={{0,8},{1,9},{2,10},{3,11},{4,12},{5,13},{6,14},{7,15},{8,0},{9,1},... | collective-permute-start | bytes 9224 | tf_op jit(solution)/shard_map/ppermute | solution.py:1369
  13.1 17.4 %collective-permute-start.9 = (bf16[1,1,1,1,24,768]{5,4,3,2,1,0:T(8,128)(2,1)}, bf16[1,1,1,1,24,768]{5,4,3,2,1,0:T(8,128)(2,1)S(1)}, u32[]{:S(2)}, u32[]{:S(2)}) collective-permute-start(bf16[1,1,1,1,24,768]{5,4,3,2,1,0:T(8,128)(2,1)} %bitcast.232), channel_id=1, source_target_pairs={{0,8},{1,9},{2,10},{3,11},{4,12},{5,13},{6,14},{7,15},{8,0},{9,1},... | collective-permute-start | bytes 110600 | tf_op jit(solution)/shard_map/ppermute | solution.py:1369
  13.2 17.3 %collective-permute-start.10 = (bf16[1,1,1,1,24,896]{5,4,3,2,1,0:T(8,128)(2,1)}, bf16[1,1,1,1,24,896]{5,4,3,2,1,0:T(8,128)(2,1)S(1)}, u32[]{:S(2)}, u32[]{:S(2)}) collective-permute-start(bf16[1,1,1,1,24,896]{5,4,3,2,1,0:T(8,128)(2,1)} %bitcast.229), channel_id=1, source_target_pairs={{0,8},{1,9},{2,10},{3,11},{4,12},{5,13},{6,14},{7,15},{8,0},{9,1},... | collective-permute-start | bytes 129032 | tf_op jit(solution)/shard_map/ppermute | solution.py:1369
  39.9 12.0 %collective-permute-start.13 = (bf16[2,2,1,1,24,768]{5,4,1,0,3,2:T(8,128)(2,1)S(1)}, bf16[2,2,1,1,24,768]{5,4,1,0,3,2:T(8,128)(2,1)S(1)}, u32[]{:S(2)}, u32[]{:S(2)}) collective-permute-start(bf16[2,2,1,1,24,768]{5,4,1,0,3,2:T(8,128)(2,1)S(1)} %bitcast.210), channel_id=1, source_target_pairs={{0,1},{1,0},{2,3},{3,2},{4,5},{5,4},{6,7},{7,6},{8,9},{9,8},{10,11... | collective-permute-start | bytes 442376 | tf_op jit(solution)/shard_map/ppermute | solution.py:1369
  41.4 10.4 %collective-permute-start.14 = (bf16[2,2,1,1,24,896]{5,4,1,0,3,2:T(8,128)(2,1)S(1)}, bf16[2,2,1,1,24,896]{5,4,1,0,3,2:T(8,128)(2,1)S(1)}, u32[]{:S(2)}, u32[]{:S(2)}) collective-permute-start(bf16[2,2,1,1,24,896]{5,4,1,0,3,2:T(8,128)(2,1)S(1)} %bitcast.201), channel_id=1, source_target_pairs={{0,2},{1,3},{2,0},{3,1},{4,6},{5,7},{6,4},{7,5},{8,10},{9,11},{10,... | collective-permute-start | bytes 516104 | tf_op jit(solution)/shard_map/ppermute | solution.py:1369
  43.1 13.7 %collective-permute-start.4 = (f32[8,4,2304]{2,1,0:T(4,128)S(1)}, f32[8,4,2304]{2,1,0:T(4,128)S(1)}, u32[]{:S(2)}, u32[]{:S(2)}) collective-permute-start(f32[8,4,2304]{2,1,0:T(4,128)S(1)} %bitcast.238), channel_id=1, source_target_pairs={{0,1},{1,0},{2,3},{3,2},{4,5},{5,4},{6,7},{7,6},{8,9},{9,8},{10,11... | collective-permute-start | bytes 884744 | tf_op jit(solution)/shard_map/ppermute | solution.py:1369
  43.7 8.1 %collective-permute-start.15 = (bf16[1,1,1,1,24,1920]{5,4,3,2,1,0:T(8,128)(2,1)S(1)}, bf16[1,1,1,1,24,1920]{5,4,3,2,1,0:T(8,128)(2,1)S(1)}, u32[]{:S(2)}, u32[]{:S(2)}) collective-permute-start(bf16[1,1,1,1,24,1920]{5,4,3,2,1,0:T(8,128)(2,1)S(1)} %bitcast.215), channel_id=1, source_target_pairs={{0,8},{1,9},{2,10},{3,11},{4,12},{5,13},{6,14},{7,15},{8,0},{9,1},... | collective-permute-start | bytes 276488 | tf_op jit(solution)/shard_map/ppermute | solution.py:1369
  51.9 12.3 %collective-permute-start.18 = (bf16[2,2,2,1,24,896]{5,4,2,1,0,3:T(8,128)(2,1)S(1)}, bf16[2,2,2,1,24,896]{5,4,2,1,0,3:T(8,128)(2,1)S(1)}, u32[]{:S(2)}, u32[]{:S(2)}) collective-permute-start(bf16[2,2,2,1,24,896]{5,4,2,1,0,3:T(8,128)(2,1)S(1)} %bitcast.177), channel_id=1, source_target_pairs={{0,1},{1,0},{2,3},{3,2},{4,5},{5,4},{6,7},{7,6},{8,9},{9,8},{10,11... | collective-permute-start | bytes 1032200 | tf_op jit(solution)/shard_map/ppermute | solution.py:1369
  53.2 11.1 %collective-permute-start.17 = (bf16[2,2,1,2,24,768]{5,4,3,1,0,2:T(8,128)(2,1)S(1)}, bf16[2,2,1,2,24,768]{5,4,3,1,0,2:T(8,128)(2,1)S(1)}, u32[]{:S(2)}, u32[]{:S(2)}) collective-permute-start(bf16[2,2,1,2,24,768]{5,4,3,1,0,2:T(8,128)(2,1)S(1)} %bitcast.186), channel_id=1, source_target_pairs={{0,2},{1,3},{2,0},{3,1},{4,6},{5,7},{6,4},{7,5},{8,10},{9,11},{10,... | collective-permute-start | bytes 884744 | tf_op jit(solution)/shard_map/ppermute | solution.py:1369
  54.7 7.9 %collective-permute-start.19 = (bf16[2,1,1,1,24,1920]{5,4,0,3,2,1:T(8,128)(2,1)S(1)}, bf16[2,1,1,1,24,1920]{5,4,0,3,2,1:T(8,128)(2,1)S(1)}, u32[]{:S(2)}, u32[]{:S(2)}) collective-permute-start(bf16[2,1,1,1,24,1920]{5,4,0,3,2,1:T(8,128)(2,1)S(1)} %bitcast.198), channel_id=1, source_target_pairs={{0,4},{1,5},{2,6},{3,7},{4,0},{5,1},{6,2},{7,3},{8,12},{9,13},{10,... | collective-permute-start | bytes 552968 | tf_op jit(solution)/shard_map/ppermute | solution.py:1369
  65.5 12.3 %collective-permute-start.24 = (bf16[2,2,1,1,24,1920]{5,4,1,0,3,2:T(8,128)(2,1)S(1)}, bf16[2,2,1,1,24,1920]{5,4,1,0,3,2:T(8,128)(2,1)S(1)}, u32[]{:S(2)}, u32[]{:S(2)}) collective-permute-start(bf16[2,2,1,1,24,1920]{5,4,1,0,3,2:T(8,128)(2,1)S(1)} %bitcast.174), channel_id=1, source_target_pairs={{0,1},{1,0},{2,3},{3,2},{4,5},{5,4},{6,7},{7,6},{8,9},{9,8},{10,11... | collective-permute-start | bytes 1105928 | tf_op jit(solution)/shard_map/ppermute | solution.py:1369
  65.7 12.1 %collective-permute-start.25 = (bf16[2,2,1,1,96,384]{5,4,1,0,3,2:T(8,128)(2,1)S(1)}, bf16[2,2,1,1,96,384]{5,4,1,0,3,2:T(8,128)(2,1)S(1)}, u32[]{:S(2)}, u32[]{:S(2)}) collective-permute-start(bf16[2,2,1,1,96,384]{5,4,1,0,3,2:T(8,128)(2,1)S(1)} %bitcast.184), channel_id=1, source_target_pairs={{0,2},{1,3},{2,0},{3,1},{4,6},{5,7},{6,4},{7,5},{8,10},{9,11},{10,... | collective-permute-start | bytes 884744 | tf_op jit(solution)/shard_map/ppermute | solution.py:1369
  77.9 19.0 %collective-permute-start.26 = (bf16[2,2,1,2,24,1920]{5,4,3,1,0,2:T(8,128)(2,1)S(1)}, bf16[2,2,1,2,24,1920]{5,4,3,1,0,2:T(8,128)(2,1)S(1)}, u32[]{:S(2)}, u32[]{:S(2)}) collective-permute-start(bf16[2,2,1,2,24,1920]{5,4,3,1,0,2:T(8,128)(2,1)S(1)} %bitcast.159), channel_id=1, source_target_pairs={{0,2},{1,3},{2,0},{3,1},{4,6},{5,7},{6,4},{7,5},{8,10},{9,11},{10,... | collective-permute-start | bytes 2211848 | tf_op jit(solution)/shard_map/ppermute | solution.py:1369
  78.0 15.8 %collective-permute-start.27 = (bf16[2,2,2,1,96,384]{5,4,2,1,0,3:T(8,128)(2,1)S(1)}, bf16[2,2,2,1,96,384]{5,4,2,1,0,3:T(8,128)(2,1)S(1)}, u32[]{:S(2)}, u32[]{:S(2)}) collective-permute-start(bf16[2,2,2,1,96,384]{5,4,2,1,0,3:T(8,128)(2,1)S(1)} %bitcast.167), channel_id=1, source_target_pairs={{0,1},{1,0},{2,3},{3,2},{4,5},{5,4},{6,7},{7,6},{8,9},{9,8},{10,11... | collective-permute-start | bytes 1769480 | tf_op jit(solution)/shard_map/ppermute | solution.py:1369
  143.3 16.1 %collective-permute-start.30 = (bf16[16,24,1536]{2,1,0:T(8,128)(2,1)}, bf16[16,24,1536]{2,1,0:T(8,128)(2,1)S(1)}, u32[]{:S(2)}, u32[]{:S(2)}) collective-permute-start(bf16[16,24,1536]{2,1,0:T(8,128)(2,1)} %get-tuple-element.241), channel_id=1, source_target_pairs={{0,16},{16,0},{1,17},{17,1},{2,18},{18,2},{3,19},{19,3},{4,20},{20... | collective-permute-start | bytes 3538952 | tf_op jit(solution)/shard_map/ppermute | solution.py:1354
  143.4 15.9 %collective-permute-start.31 = (bf16[512,384]{1,0:T(8,128)(2,1)}, bf16[512,384]{1,0:T(8,128)(2,1)}, u32[]{:S(2)}, u32[]{:S(2)}) collective-permute-start(bf16[512,384]{1,0:T(8,128)(2,1)} %get-tuple-element.242), channel_id=1, source_target_pairs={{0,16},{16,0},{1,17},{17,1},{2,18},{18,2},{3,19},{19,3},{4,20},{20... | collective-permute-start | bytes 1179656 | tf_op jit(solution)/shard_map/ppermute | solution.py:1354
  159.4 8.0 %collective-permute-start.32 = (bf16[16,24,1024]{2,1,0:T(8,128)(2,1)}, bf16[16,24,1024]{2,1,0:T(8,128)(2,1)S(1)}, u32[]{:S(2)}, u32[]{:S(2)}) collective-permute-start(bf16[16,24,1024]{2,1,0:T(8,128)(2,1)} %bitcast.256), channel_id=1, source_target_pairs={{0,16},{16,0},{1,17},{17,1},{2,18},{18,2},{3,19},{19,3},{4,20},{20... | collective-permute-start | bytes 2359304 | tf_op jit(solution)/shard_map/ppermute | solution.py:1354
  168.0 16.5 %collective-permute-start.33 = (bf16[8,24,1536]{2,1,0:T(8,128)(2,1)S(1)}, bf16[8,24,1536]{2,1,0:T(8,128)(2,1)S(1)}, u32[]{:S(2)}, u32[]{:S(2)}) collective-permute-start(bf16[8,24,1536]{2,1,0:T(8,128)(2,1)S(1)} %bitcast.235), channel_id=1, source_target_pairs={{0,1},{1,0},{2,3},{3,2},{4,5},{5,4},{6,7},{7,6},{8,9},{9,8},{10,11... | collective-permute-start | bytes 1769480 | tf_op jit(solution)/shard_map/ppermute | solution.py:1369
  169.1 13.3 %collective-permute-start.34 = (bf16[8,24,1024]{2,1,0:T(8,128)(2,1)S(1)}, bf16[8,24,1024]{2,1,0:T(8,128)(2,1)S(1)}, u32[]{:S(2)}, u32[]{:S(2)}) collective-permute-start(bf16[8,24,1024]{2,1,0:T(8,128)(2,1)S(1)} %bitcast.237), channel_id=1, source_target_pairs={{0,2},{1,3},{2,0},{3,1},{4,6},{5,7},{6,4},{7,5},{8,10},{9,11},{10,... | collective-permute-start | bytes 1179656 | tf_op jit(solution)/shard_map/ppermute | solution.py:1369
  189.0 19.6 %collective-permute-start.36 = (bf16[4,24,1536]{2,1,0:T(8,128)(2,1)}, bf16[4,24,1536]{2,1,0:T(8,128)(2,1)S(1)}, u32[]{:S(2)}, u32[]{:S(2)}) collective-permute-start(bf16[4,24,1536]{2,1,0:T(8,128)(2,1)} %bitcast.85), channel_id=1, source_target_pairs={{0,2},{1,3},{2,0},{3,1},{4,6},{5,7},{6,4},{7,5},{8,10},{9,11},{10,... | collective-permute-start | bytes 884744 | tf_op jit(solution)/shard_map/ppermute | solution.py:1369
  190.5 17.3 %collective-permute-start.37 = (bf16[4,24,1024]{2,1,0:T(8,128)(2,1)S(1)}, bf16[4,24,1024]{2,1,0:T(8,128)(2,1)S(1)}, u32[]{:S(2)}, u32[]{:S(2)}) collective-permute-start(bf16[4,24,1024]{2,1,0:T(8,128)(2,1)S(1)} %bitcast.241), channel_id=1, source_target_pairs={{0,1},{1,0},{2,3},{3,2},{4,5},{5,4},{6,7},{7,6},{8,9},{9,8},{10,11... | collective-permute-start | bytes 589832 | tf_op jit(solution)/shard_map/ppermute | solution.py:1369
  191.1 20.6 %collective-permute-start.38 = (bf16[8,24,1536]{2,1,0:T(8,128)(2,1)}, bf16[8,24,1536]{2,1,0:T(8,128)(2,1)S(1)}, u32[]{:S(2)}, u32[]{:S(2)}) collective-permute-start(bf16[8,24,1536]{2,1,0:T(8,128)(2,1)} %bitcast.91), channel_id=1, source_target_pairs={{0,1},{1,0},{2,3},{3,2},{4,5},{5,4},{6,7},{7,6},{8,9},{9,8},{10,11... | collective-permute-start | bytes 1769480 | tf_op jit(solution)/shard_map/ppermute | solution.py:1369
  215.9 11.6 %collective-permute-start.40 = (bf16[8,24,1024]{2,1,0:T(8,128)(2,1)S(1)}, bf16[8,24,1024]{2,1,0:T(8,128)(2,1)S(1)}, u32[]{:S(2)}, u32[]{:S(2)}) collective-permute-start(bf16[8,24,1024]{2,1,0:T(8,128)(2,1)S(1)} %bitcast.236), channel_id=1, source_target_pairs={{0,1},{1,0},{2,3},{3,2},{4,5},{5,4},{6,7},{7,6},{8,9},{9,8},{10,11... | collective-permute-start | bytes 1179656 | tf_op jit(solution)/shard_map/ppermute | solution.py:1369
  216.3 10.5 %collective-permute-start.42 = (bf16[4,24,1536]{2,1,0:T(8,128)(2,1)}, bf16[4,24,1536]{2,1,0:T(8,128)(2,1)S(1)}, u32[]{:S(2)}, u32[]{:S(2)}) collective-permute-start(bf16[4,24,1536]{2,1,0:T(8,128)(2,1)} %bitcast.100), channel_id=1, source_target_pairs={{0,2},{1,3},{2,0},{3,1},{4,6},{5,7},{6,4},{7,5},{8,10},{9,11},{10,... | collective-permute-start | bytes 884744 | tf_op jit(solution)/shard_map/ppermute | solution.py:1369
  218.0 8.8 %collective-permute-start.41 = (bf16[2,24,2560]{2,1,0:T(8,128)(2,1)}, bf16[2,24,2560]{2,1,0:T(8,128)(2,1)S(1)}, u32[]{:S(2)}, u32[]{:S(2)}) collective-permute-start(bf16[2,24,2560]{2,1,0:T(8,128)(2,1)} %bitcast.97), channel_id=1, source_target_pairs={{0,4},{1,5},{2,6},{3,7},{4,0},{5,1},{6,2},{7,3},{8,12},{9,13},{10,... | collective-permute-start | bytes 737288 | tf_op jit(solution)/shard_map/ppermute | solution.py:1369
  227.5 31.4 %collective-permute-start.48 = (f32[512,384]{1,0:T(8,128)}, f32[512,384]{1,0:T(8,128)}, u32[]{:S(2)}, u32[]{:S(2)}) collective-permute-start(f32[512,384]{1,0:T(8,128)} %get-tuple-element.336), channel_id=1, source_target_pairs={{0,16},{16,0},{1,17},{17,1},{2,18},{18,2},{3,19},{19,3},{4,20},{20... | collective-permute-start | bytes 2359304 | tf_op jit(solution)/shard_map/ppermute | solution.py:1354
  228.3 10.8 %collective-permute-start.43 = (bf16[4,24,1024]{2,1,0:T(8,128)(2,1)S(1)}, bf16[4,24,1024]{2,1,0:T(8,128)(2,1)S(1)}, u32[]{:S(2)}, u32[]{:S(2)}) collective-permute-start(bf16[4,24,1024]{2,1,0:T(8,128)(2,1)S(1)} %bitcast.242), channel_id=1, source_target_pairs={{0,2},{1,3},{2,0},{3,1},{4,6},{5,7},{6,4},{7,5},{8,10},{9,11},{10,... | collective-permute-start | bytes 589832 | tf_op jit(solution)/shard_map/ppermute | solution.py:1369
  241.2 15.3 %collective-permute-start.45 = (bf16[2,24,2560]{2,1,0:T(8,128)(2,1)S(1)}, bf16[2,24,2560]{2,1,0:T(8,128)(2,1)S(1)}, u32[]{:S(2)}, u32[]{:S(2)}) collective-permute-start(bf16[2,24,2560]{2,1,0:T(8,128)(2,1)S(1)} %bitcast.240), channel_id=1, source_target_pairs={{0,4},{1,5},{2,6},{3,7},{4,0},{5,1},{6,2},{7,3},{8,12},{9,13},{10,... | collective-permute-start | bytes 737288 | tf_op jit(solution)/shard_map/ppermute | solution.py:1369
  249.3 9.6 %collective-permute-start.49 = (bf16[8,2304]{1,0:T(8,128)(2,1)S(1)}, bf16[8,2304]{1,0:T(8,128)(2,1)S(1)}, u32[]{:S(2)}, u32[]{:S(2)}) collective-permute-start(bf16[8,2304]{1,0:T(8,128)(2,1)S(1)} %copy-done.33), channel_id=1, source_target_pairs={{0,16},{16,0},{1,17},{17,1},{2,18},{18,2},{3,19},{19,3},{4,20},{20... | collective-permute-start | bytes 110600 | tf_op jit(solution)/shard_map/ppermute | solution.py:1354
  258.9 11.0 %collective-permute-start.51 = (bf16[1,24,5120]{2,1,0:T(8,128)(2,1)S(1)}, bf16[1,24,5120]{2,1,0:T(8,128)(2,1)S(1)}, u32[]{:S(2)}, u32[]{:S(2)}) collective-permute-start(bf16[1,24,5120]{2,1,0:T(8,128)(2,1)S(1)} %bitcast.239), channel_id=1, source_target_pairs={{0,8},{1,9},{2,10},{3,11},{4,12},{5,13},{6,14},{7,15},{8,0},{9,1},... | collective-permute-start | bytes 737288 | tf_op jit(solution)/shard_map/ppermute | solution.py:1369
  260.8 9.2 %collective-permute-start.52 = (bf16[160,768]{1,0:T(8,128)(2,1)}, bf16[160,768]{1,0:T(8,128)(2,1)S(1)}, u32[]{:S(2)}, u32[]{:S(2)}) collective-permute-start(bf16[160,768]{1,0:T(8,128)(2,1)} %shard_map.342.refs_6_), channel_id=1, source_target_pairs={{0,2},{1,3},{2,0},{3,1},{4,6},{5,7},{6,4},{7,5},{8,10},{9,11},{10,... | collective-permute-start | bytes 737288 | tf_op jit(solution)/shard_map/ppermute | solution.py:1369
  (59 other events, 337.8 us)
Sparse Core Ops, SparseCore 0:
  144.0 60.9 all-gather.1
where the time goes:
time: 289 us; the launch traced here: 285 us
  Pallas kernels  135 us (47%)
  waiting for transfers between devices  61.2 us (21%)
  starting transfers between devices  50.6 us (18%)
  local copies, waits for them, and re-layouts  19.2 us (7%)
  between operations  14.8 us (5%)
    pallas_call x10, Pallas kernels, call(): pl.pallas_call(kernel, out_shape=[jax.ShapeDtypeStruct(shape, kind) for s...  102 us
    ppermute x39, waiting for transfers between devices, partner(): return lax.ppermute(values, 'row', [(i, i ^ 1 << bit) for i in range(size)])  54.4 us
    ppermute x39, starting transfers between devices, partner(): return lax.ppermute(values, 'row', [(i, i ^ 1 << bit) for i in range(size)])  47.8 us
    unnamed x76, local copies, waits for them, and re-layouts  19 us
    pallas_call x11, Pallas kernels, step(): pl.pallas_call(functools.partial(step_kernel, bit, widths, [count for _,...  12.8 us
    ppermute x16, waiting for transfers between devices, swap(): return lax.ppermute(values, 'section', [(0, 1), (1, 0)])  6.74 us
  transfers between devices with their start and end apart: 56, of which 22 were waited for; matrix products, arithmetic and copies ran while one was open for 2% of the time, Pallas kernels for 32%

commit v1 on v0

--- a/solution.py
+++ b/solution.py
@@ -1205,8 +1205,8 @@
     count = len(widths)
     kept, refs = refs[:count], refs[count:]
     came, refs = refs[: len(counts)], refs[len(counts) :]
-    lifted, misc, misc_came = refs[:3]
-    mine, other, small_mine, small_other = refs[3 + waits :]
+    lifted, *parts = refs[:5]
+    mine, other, small_mine, small_other = refs[5 + waits :]
     places = [(ref, i) for ref, many in zip(came, counts) for i in range(many)]
     added = []
     for i in range(count):
@@ -1214,8 +1214,8 @@
         start = sum(widths[i - place : i])
         added.append(kept[i][0] + ref[0, :, start : start + widths[i]].astype(f32))
     a1, f1, f2, a2 = added
-    size = misc.shape[0] - SUMS
-    rows = jnp.concatenate([misc[:size, :], misc_came[:size, :]], axis=0)
+    size = parts[0].shape[0] - SUMS
+    rows = jnp.concatenate([part[:size, :] for part in parts], axis=0)
     rows = rows.astype(f32).reshape(-1, OWN, 2 * D)
 
     def ada(first):
@@ -1232,13 +1232,13 @@
         mine[:, columns] = jnp.where(first, one, two)
         other[:, columns] = jnp.where(first, two, one)
         at += one.shape[1]
-    total = misc_sums(misc, misc_came)
+    total = misc_sums(*parts)
     one, two = total[0:8, :], total[8:16, :]
     small_mine[...] = jnp.where(first, one, two)
     small_other[...] = jnp.where(first, two, one)
 
 
-def finish(kept, came, lifted, misc, misc_came, after):
+def finish(kept, came, lifted, parts, after):
     widths = [array.shape[2] for array in kept]
     shard = kept[0].shape[1]
     wide = GROUP + FF + 6 * D
@@ -1247,10 +1247,10 @@
     return pl.pallas_call(
         functools.partial(finish_kernel, widths, [count for _, count in came], len(after)),
         out_shape=[jax.ShapeDtypeStruct(shape, f32) for shape in shapes],
-        in_specs=[VMEM] * (len(kept) + len(came) + 3) + [ANY] * len(after),
+        in_specs=[VMEM] * (len(kept) + len(came) + 5) + [ANY] * len(after),
         out_specs=[VMEM] * 4,
         compiler_params=pltpu.CompilerParams(vmem_limit_bytes=8 * 1024 * 1024),
-    )(*kept, *arrays, lifted, misc, misc_came, *after)
+    )(*kept, *arrays, lifted, *parts, *after)
 
 
 def output_kernel(mine, other, small_mine, small_other, *outs):
@@ -1308,8 +1308,9 @@
     )(mine, other, small_mine, small_other)
 
 
-def both_kernel(one, two, came, out, kept, sems):
+def both_kernel(one, two, came, out, mark, kept, sems):
     section = lax.axis_index("section")
+    mark[...] = jnp.zeros(mark.shape, f32)
 
     def move(mine, layer):
         arrive = [
@@ -1340,9 +1341,12 @@
 def both_micros(one, two, came):
     return pl.pallas_call(
         both_kernel,
-        out_shape=jax.ShapeDtypeStruct((MICRO,) + one.shape, one.dtype),
+        out_shape=[
+            jax.ShapeDtypeStruct((MICRO,) + one.shape, one.dtype),
+            jax.ShapeDtypeStruct((8, LANES), f32),
+        ],
         in_specs=[ANY] * 3,
-        out_specs=ANY,
+        out_specs=[ANY, VMEM],
         scratch_shapes=[
             pltpu.VMEM((MICRO,) + one.shape, one.dtype),
             pltpu.SemaphoreType.DMA((4,)),
@@ -1364,9 +1368,13 @@
     )
 
 
+def across(values, flips):
+    size = lax.axis_size("row")
+    return lax.ppermute(values, "row", [(i, i ^ flips) for i in range(size)])
+
+
 def partner(values, bit):
-    size = lax.axis_size("row")
-    return lax.ppermute(values, "row", [(i, i ^ (1 << bit)) for i in range(size)])
+    return across(values, 1 << bit)
 
 
 def axis_of(bit):
@@ -1412,49 +1420,43 @@
     )
     small = pack_small(b_up, b_down, conv_kernel, b_decay)
     steps = gather_steps(along_x, along_y, along_z)
-    lag = len(along_z)
-    order = tuple(reversed(along_z)) + along_x + along_y
+    order = tuple(reversed(along_z)) + along_x[:-1] + along_y[:-1] + along_x[-1:] + along_y[-1:]
     term_bits = along_x + along_y + along_z
-    spans = len(steps) + lag - 4
-    bounds = [(len(term_bits) * i + spans // 2) // spans for i in range(spans + 1)]
+    spans = len(steps) - 2
+    bounds = [len(term_bits) * i // spans for i in range(spans + 1)]
     term_bits = [term_bits[bounds[i] : bounds[i + 1]] for i in range(spans)]
     left = list(order)
-    groups = [[single(qk), single(vgd)], [single(upo), single(w_down[0])]]
-    for place in range(len(steps) + lag):
-        numbers = [g for g in range(2) if 0 <= place - g * lag < len(steps)]
-        bits = [bit for g in numbers for bit in steps[place - g * lag]]
-        held = [array for g in numbers for array in groups[g]]
+    held = [single(array) for array in (qk, vgd, upo, w_down[0])]
+    for place, pair in enumerate(steps):
+        bits = pair + pair
         came = [partner(array, bit) for array, bit in zip(held, bits)]
-        if place < 2:
-            after = (small,)
-        elif place == 2:
+        after = (small,)
+        if place == 1:
             for bit in order:
                 lifted = jnp.concatenate([lifted, partner(lifted, bit)], axis=0)
             after = (lifted,)
-        elif place < 3 + spans:
-            if place == 3:
-                lifted_cut = lax.dynamic_slice_in_dim(
-                    lifted, lax.axis_index("row") * shard, shard, 2
-                )
-                product = mm(lifted_cut.reshape(devices * MICRO * SLOTS, shard), w_ada[0])
-                terms = (product.reshape(devices, MICRO * SLOTS, 6 * D),)
-            for bit in term_bits[place - 3]:
+        if place == 2:
+            lifted_cut = lax.dynamic_slice_in_dim(
+                lifted, lax.axis_index("row") * shard, shard, 2
+            )
+            product = mm(lifted_cut.reshape(devices * MICRO * SLOTS, shard), w_ada[0])
+            terms = (product.reshape(devices, MICRO * SLOTS, 6 * D),)
+        if place >= 2:
+            for bit in term_bits[place - 2]:
                 stays, goes = term_step(1 << left.index(bit), *terms)
                 left.remove(bit)
                 terms = (stays, partner(goes, bit))
             after = (terms[1],)
+        if place < len(steps) - 1:
+            held = join(held, came, bits, after)
         else:
+            qk, vgd = [both(flat(array)) for array in join(held[:2], came[:2], bits[:2])]
             mods = both(sum(term[0] for term in terms) + b_ada[0])
             smalls = both(small)
             x = tokens
             *saved, gated = attn_forward(0, layouts, x, mods, smalls, qk, vgd)
-            after = (gated,)
-        held = join(held, came, bits, after)
-        for g in numbers:
-            groups[g], held = held[:2], held[2:]
-        if place == len(steps) - 1:
-            qk, vgd = [both(flat(array)) for array in groups[0]]
-    upo, down = [both(flat(array)) for array in groups[1]]
+            held = join(held[2:], came[2:], bits[2:], (gated,))
+    upo, down = [both(flat(array)) for array in held]
     kept = []
     acts = []
     for l in range(2):
@@ -1579,14 +1581,15 @@
             sent, misc = lock(sent, misc)
         came = [(partner(sent, bit), len(keep))]
         if place == 0:
-            misc = grown(misc, z_bits[:1] + (x_bits + y_bits)[:-1])
-    misc_came = partner(misc, y_bits[-1])
-    gx_out = both_micros(gx_one, gx_two, gx_came)
-    acts_out = both_micros(acts[0], acts[1], acts_came)
+            misc = grown(misc, z_bits[:1] + x_bits[:-1] + y_bits[:-1])
+    last = (1 << x_bits[-1], 1 << y_bits[-1])
+    parts = [misc] + [across(misc, flips) for flips in (last[0], last[1], last[0] + last[1])]
+    gx_out, gx_mark = both_micros(gx_one, gx_two, gx_came)
+    acts_out, acts_mark = both_micros(acts[0], acts[1], acts_came)
     grad_lifted = lifted_grads(mod_mine, mod_came, ada_all)
     lifted_came = swap(grad_lifted)
     mine, other, small_mine, small_other = finish(
-        keep, came, lifted, misc, misc_came, (gx_out, acts_out, lifted_came)
+        keep, came, lifted, parts, (gx_mark, acts_mark, lifted_came)
     )
     came, small_came = swap(other), swap(small_other)
     (

time: 289 us -> 285 us (0.986)
  waiting for transfers between devices: 61.2 us -> 48.3 us
  starting transfers between devices: 50.6 us -> 57.1 us
    ppermute x39 -> x40, waiting for transfers between devices: 54.4 us -> 39.8 us  [across(): return lax.ppermute(values, 'row', [(i, i ^ flips) for i in range(size)])]
    ppermute x39 -> x40, starting transfers between devices: 47.8 us -> 54.5 us  [across(): return lax.ppermute(values, 'row', [(i, i ^ flips) for i in range(size)])]
    unnamed x76 -> x84, local copies, waits for them, and re-layouts: 19 us -> 21.4 us
  transfers between devices with their start and end apart: 56 -> 57, of which waited for: 22 -> 19; matrix products, arithmetic and copies ran while one was open for 2% -> 2% of each run, Pallas kernels for 32% -> 33%
where the time goes in v1:
time: 285 us; the launch traced here: 281 us
  Pallas kernels  135 us (47%)
  starting transfers between devices  57.1 us (20%)
  waiting for transfers between devices  48.3 us (17%)
  local copies, waits for them, and re-layouts  21.6 us (8%)
  between operations  14.9 us (5%)
    pallas_call x10, Pallas kernels, call(): pl.pallas_call(kernel, out_shape=[jax.ShapeDtypeStruct(shape, kind) for s...  102 us
    ppermute x40, starting transfers between devices, across(): return lax.ppermute(values, 'row', [(i, i ^ flips) for i in range(size)])  54.5 us
    ppermute x40, waiting for transfers between devices, across(): return lax.ppermute(values, 'row', [(i, i ^ flips) for i in range(size)])  39.8 us
    unnamed x84, local copies, waits for them, and re-layouts  21.4 us
    pallas_call x11, Pallas kernels, step(): pl.pallas_call(functools.partial(step_kernel, bit, widths, [count for _,...  12.9 us
    ppermute x16, waiting for transfers between devices, swap(): return lax.ppermute(values, 'section', [(0, 1), (1, 0)])  8.46 us
  transfers between devices with their start and end apart: 57, of which 19 were waited for; matrix products, arithmetic and copies ran while one was open for 2% of the time, Pallas kernels for 33%

profile of v1, /device:TPU:0, one launch (start us, length us, event | category | flops | bytes accessed | tf_op | source)
XLA Modules:
  0.0 280.8 jit_solution(5813987878064613993)
XLA Ops:
  7.2 1.8 shard_map.305
  9.1 4.0 %collective-permute-start = (bf16[1,4,384]{2,1,0:T(4,128)(2,1)}, bf16[1,4,384]{2,1,0:T(4,128)(2,1)S(1)}, u32[]{:S(2)}, u32[]{:S(2)}) collective-permute-start(bf16[1,4,384]{2,1,0:T(4,128)(2,1)} %get-tuple-element.196), channel_id=1, source_target_pairs={{0,8},{1,9},{2,10},{3,11},{4,12},{5,13},{6,14},{7,15},{8,0},{9,1},... | collective-permute-start | bytes 9224 | tf_op jit(solution)/shard_map/ppermute | solution.py:1373
  13.2 2.9 %collective-permute-start.10 = (bf16[1,1,1,1,24,896]{5,4,3,2,1,0:T(8,128)(2,1)}, bf16[1,1,1,1,24,896]{5,4,3,2,1,0:T(8,128)(2,1)S(1)}, u32[]{:S(2)}, u32[]{:S(2)}) collective-permute-start(bf16[1,1,1,1,24,896]{5,4,3,2,1,0:T(8,128)(2,1)} %bitcast.227), channel_id=1, source_target_pairs={{0,8},{1,9},{2,10},{3,11},{4,12},{5,13},{6,14},{7,15},{8,0},{9,1},... | collective-permute-start | bytes 129032 | tf_op jit(solution)/shard_map/ppermute | solution.py:1373
  16.1 2.9 %collective-permute-start.12 = (bf16[1,1,1,1,96,384]{5,4,3,2,1,0:T(8,128)(2,1)}, bf16[1,1,1,1,96,384]{5,4,3,2,1,0:T(8,128)(2,1)S(1)}, u32[]{:S(2)}, u32[]{:S(2)}) collective-permute-start(bf16[1,1,1,1,96,384]{5,4,3,2,1,0:T(8,128)(2,1)} %bitcast.224), channel_id=1, source_target_pairs={{0,8},{1,9},{2,10},{3,11},{4,12},{5,13},{6,14},{7,15},{8,0},{9,1},... | collective-permute-start | bytes 221192 | tf_op jit(solution)/shard_map/ppermute | solution.py:1373
  24.6 2.6 collective-permute-done.1
  29.4 2.2 collective-permute-done.2
  33.9 2.3 collective-permute-done.3
  47.4 2.4 collective-permute-done.16
  56.9 7.0 %collective-permute-done.17 = bf16[2,2,1,1,24,768]{5,4,1,0,3,2:T(8,128)(2,1)S(1)} collective-permute-done((bf16[2,2,1,1,24,768]{5,4,1,0,3,2:T(8,128)(2,1)S(1)}, bf16[2,2,1,1,24,768]{5,4,1,0,3,2:T(8,128)(2,1)S(1)}, u32[]{:S(2)}, u32[]{:S(2)}) %collective-permute-start.17) | collective-permute-done | bytes 147488 | tf_op jit(solution)/shard_map/ppermute | solution.py:1373
  68.3 3.3 %collective-permute-done.6 = f32[2,4,2304]{2,1,0:T(4,128)S(1)} collective-permute-done((f32[2,4,2304]{2,1,0:T(4,128)S(1)}, f32[2,4,2304]{2,1,0:T(4,128)S(1)}, u32[]{:S(2)}, u32[]{:S(2)}) %collective-permute-start.6) | collective-permute-done | bytes 73760 | tf_op jit(solution)/shard_map/ppermute | solution.py:1373
  82.2 9.1 %shard_map.315 = (bf16[512,384]{1,0:T(8,128)(2,1)}, f32[512,1536]{1,0:T(8,128)}, f32[512,128]{1,0:T(8,128)}, f32[512,384]{1,0:T(8,128)}, f32[512,128]{1,0:T(8,12...) custom-call(s32[2,1]{1,0:T(2,128)} %copy.48.refs_0_, bf16[2,512,384]{2,1,0:T(8,128)(2,1)} %refs_6_.3, ...), custom_call_target="tpu_custom_call" | custom-call | flops 4000000000 | bytes 4194304 | tf_op jit(solution)/shard_map/pallas_call | solution.py:735
  94.6 4.6 %collective-permute-done.29.refs_12_ = bf16[1536,384]{1,0:T(8,128)(2,1)S(1)} collective-permute-done((bf16[1536,384]{1,0:T(8,128)(2,1)}, bf16[1536,384]{1,0:T(8,128)(2,1)S(1)}, u32[]{:S(2)}, u32[]{:S(2)}) %collective-permute-start.29) | collective-permute-done | bytes 1179680 | tf_op jit(solution)/shard_map/ppermute | solution.py:1358
  101.4 6.5 %shard_map.317 = (bf16[512,384]{1,0:T(8,128)(2,1)}, f32[512,384]{1,0:T(8,128)}, f32[512,384]{1,0:T(8,128)}) custom-call(s32[2,1]{1,0:T(2,128)} %copy.48.refs_0_, bf16[512,384]{1,0:T(8,128)(2,1)} %get-tuple-element.220.refs_4_.refs_1_.refs_13_, bf16[2,512,384]{2,1,0:T(8,128)(2,1)} %refs_6_.3, bf16[384,1920]{1,0:T(8,128)(2,1)} %bitcast.67.refs_3_.refs_9_.refs_2_, ...), custom_call_target="tpu_custom_call" | custom-call | flops 3000000000 | bytes 4194304 | tf_op jit(solution)/shard_map/pallas_call | solution.py:735
  107.9 9.8 %shard_map.318 = (bf16[512,384]{1,0:T(8,128)(2,1)}, f32[512,1536]{1,0:T(8,128)}, f32[512,128]{1,0:T(8,128)}, f32[512,384]{1,0:T(8,128)}, f32[512,128]{1,0:T(8,12...) custom-call(s32[2,1]{1,0:T(2,128)} %copy.48.refs_0_, bf16[1,512,384]{2,1,0:T(8,128)(2,1)} %bitcast.245, ...), custom_call_target="tpu_custom_call" | custom-call | flops 4000000000 | bytes 4194304 | tf_op jit(solution)/shard_map/pallas_call | solution.py:735
  117.7 6.8 %shard_map.319 = (bf16[512,384]{1,0:T(8,128)(2,1)}, f32[512,384]{1,0:T(8,128)}, f32[512,384]{1,0:T(8,128)}, bf16[512,384]{1,0:T(8,128)(2,1)}) custom-call(s32[2,1]{1,0:T(2,128)} %copy.48.refs_0_, bf16[512,384]{1,0:T(8,128)(2,1)} %get-tuple-element.226.refs_1_.refs_13_, bf16[1,512,384]{2,1,0:T(8,128)(2,1)} %bitcast.246, ...), custom_call_target="tpu_custom_call" | custom-call | flops 3000000000 | bytes 4194304 | tf_op jit(solution)/shard_map/pallas_call | solution.py:735
  124.6 13.4 %shard_map.320 = (f32[512,384]{1,0:T(8,128)}, bf16[512,384]{1,0:T(8,128)(2,1)}, f32[384,384]{1,0:T(8,128)}, f32[8,1536]{1,0:T(8,128)}, f32[16,24,1536]{2,1,0:T(8,128)}, /*index=5*/bf16[16,24,1536]{2,1,0:T(8,128)(2,1)}) custom-call(s32[2,1]{1,0:T(2,128)} %copy.48.refs_0_, f32[4,2304]{1,0:T(4,128)} %copy-done.28, f32[4,2304]{1,0:T(4,128)} %copy-done.36, ...), custom_call_target="tpu_custom_call" | custom-call | flops 5000000000 | bytes 4194304 | tf_op jit(solution)/shard_map/pallas_call | solution.py:735
  138.5 15.5 %shard_map.321 = (bf16[512,1664]{1,0:T(8,128)(2,1)}, f32[384,1024]{1,0:T(8,128)}, bf16[384,1024]{1,0:T(8,128)(2,1)}, f32[8,384]{1,0:T(8,128)}) custom-call(s32[2,1]{1,0:T(2,128)} %copy.48.refs_0_, bf16[512,384]{1,0:T(8,128)(2,1)} %get-tuple-element.234.refs_1_, bf16[384,1920]{1,0:T(8,128)(2,1)} %bitcast.67.refs_3_.refs_9_.refs_2_, ...), custom_call_target="tpu_custom_call" | custom-call | flops 7000000000 | bytes 4194304 | tf_op jit(solution)/shard_map/pallas_call | solution.py:735
  155.8 6.8 %shard_map.323 = (f32[512,384]{1,0:T(8,128)}, bf16[512,384]{1,0:T(8,128)(2,1)}, bf16[8,2304]{1,0:T(8,128)(2,1)}, f32[8,768]{1,0:T(8,128)}) custom-call(s32[2,1]{1,0:T(2,128)} %copy.48.refs_0_, bf16[512,1664]{1,0:T(8,128)(2,1)} %get-tuple-element.249.refs_1_, bf16[384,768]{1,0:T(8,128)(2,1)} %bitcast.59.refs_4_.refs_2_, ...), custom_call_target="tpu_custom_call" | custom-call | flops 2000000000 | bytes 4194304 | tf_op jit(solution)/shard_map/pallas_call | solution.py:735
  165.5 13.0 %shard_map.326 = (f32[512,384]{1,0:T(8,128)}, bf16[512,384]{1,0:T(8,128)(2,1)}, f32[384,384]{1,0:T(8,128)}, f32[8,1536]{1,0:T(8,128)}, f32[16,24,1536]{2,1,0:T(8,128)}, /*index=5*/bf16[16,24,1536]{2,1,0:T(8,128)(2,1)}) custom-call(s32[2,1]{1,0:T(2,128)} %copy.48.refs_0_, f32[4,2304]{1,0:T(4,128)} %copy-done.28, f32[4,2304]{1,0:T(4,128)} %copy-done.36, ...), custom_call_target="tpu_custom_call" | custom-call | flops 5000000000 | bytes 4194304 | tf_op jit(solution)/shard_map/pallas_call | solution.py:735
  178.6 3.1 %collective-permute-done.33 = bf16[8,24,1536]{2,1,0:T(8,128)(2,1)S(1)} collective-permute-done((bf16[8,24,1536]{2,1,0:T(8,128)(2,1)S(1)}, bf16[8,24,1536]{2,1,0:T(8,128)(2,1)S(1)}, u32[]{:S(2)}, u32[]{:S(2)}) %collective-permute-start.33) | collective-permute-done | bytes 589856 | tf_op jit(solution)/shard_map/ppermute | solution.py:1373
  189.7 15.2 %shard_map.330 = (bf16[512,1664]{1,0:T(8,128)(2,1)}, f32[384,1024]{1,0:T(8,128)}, bf16[384,1024]{1,0:T(8,128)(2,1)}, f32[8,384]{1,0:T(8,128)}) custom-call(s32[2,1]{1,0:T(2,128)} %copy.48.refs_0_, bf16[512,384]{1,0:T(8,128)(2,1)} %get-tuple-element.281.refs_1_, bf16[384,1920]{1,0:T(8,128)(2,1)} %bitcast.67.refs_3_.refs_9_.refs_2_, ...), custom_call_target="tpu_custom_call" | custom-call | flops 7000000000 | bytes 4194304 | tf_op jit(solution)/shard_map/pallas_call | solution.py:735
  205.7 3.1 %collective-permute-done.38 = bf16[8,24,1536]{2,1,0:T(8,128)(2,1)S(1)} collective-permute-done((bf16[8,24,1536]{2,1,0:T(8,128)(2,1)}, bf16[8,24,1536]{2,1,0:T(8,128)(2,1)S(1)}, u32[]{:S(2)}, u32[]{:S(2)}) %collective-permute-start.38) | collective-permute-done | bytes 589856 | tf_op jit(solution)/shard_map/ppermute | solution.py:1373
  216.5 5.8 %shard_map.334 = (f32[512,384]{1,0:T(8,128)}, bf16[512,384]{1,0:T(8,128)(2,1)}, bf16[8,2304]{1,0:T(8,128)(2,1)}, f32[8,768]{1,0:T(8,128)}, f32[512,384]{1,0:T(8,...) custom-call(s32[2,1]{1,0:T(2,128)} %copy.48.refs_0_, bf16[512,1664]{1,0:T(8,128)(2,1)} %get-tuple-element.308.refs_1_, ...), custom_call_target="tpu_custom_call" | custom-call | flops 2000000000 | bytes 4194304 | tf_op jit(solution)/shard_map/pallas_call | solution.py:735
  226.9 2.4 collective-permute-start.44
  229.3 4.7 %collective-permute-done.44.arrived = bf16[48,768]{1,0:T(8,128)(2,1)S(1)} collective-permute-done((bf16[48,768]{1,0:T(8,128)(2,1)}, bf16[48,768]{1,0:T(8,128)(2,1)S(1)}, u32[]{:S(2)}, u32[]{:S(2)}) %collective-permute-start.44) | collective-permute-done | bytes 73760 | tf_op jit(solution)/shard_map/ppermute | solution.py:1373
  239.7 6.8 %collective-permute-done.46.arrived = bf16[64,768]{1,0:T(8,128)(2,1)S(1)} collective-permute-done((bf16[64,768]{1,0:T(8,128)(2,1)}, bf16[64,768]{1,0:T(8,128)(2,1)S(1)}, u32[]{:S(2)}, u32[]{:S(2)}) %collective-permute-start.46) | collective-permute-done | bytes 98336 | tf_op jit(solution)/shard_map/ppermute | solution.py:1373
  248.8 2.4 shard_map.339
  251.2 3.3 %collective-permute-start.50 = (bf16[1,24,5120]{2,1,0:T(8,128)(2,1)S(1)}, bf16[1,24,5120]{2,1,0:T(8,128)(2,1)S(1)}, u32[]{:S(2)}, u32[]{:S(2)}) collective-permute-start(bf16[1,24,5120]{2,1,0:T(8,128)(2,1)S(1)} %bitcast.237), channel_id=1, source_target_pairs={{0,8},{1,9},{2,10},{3,11},{4,12},{5,13},{6,14},{7,15},{8,0},{9,1},... | collective-permute-start | bytes 737288 | tf_op jit(solution)/shard_map/ppermute | solution.py:1373
  255.5 2.6 collective-permute-start.53
  260.7 2.5 shard_map.322
  263.3 2.9 %shard_map.341 = (f32[2,512,384]{2,1,0:T(8,128)}, f32[8,128]{1,0:T(8,128)}) custom-call(f32[512,384]{1,0:T(8,128)} %get-tuple-element.314.one, f32[512,384]{1,0:T(8,128)} %get-tuple-element.312.refs_12_.two, f32[512,384]{1,0:T(8,128)} %collective-permute-done.47.came), custom_call_target="tpu_custom_call" | custom-call | tf_op jit(solution)/shard_map/pallas_call | solution.py:1342
  271.6 2.1 shard_map.344
  (221 shorter events, 92.0 us)
Async XLA Ops:
  7.2 197.8 %all-gather.2.cloned.1.call-start = ((), (), s32[]{:S(2)}) async-start(), calls=%async_computation | async-start | bytes 1880064 | tf_op jit(solution)/shard_map/all_gather | solution.py:1473
  9.1 13.2 %collective-permute-start = (bf16[1,4,384]{2,1,0:T(4,128)(2,1)}, bf16[1,4,384]{2,1,0:T(4,128)(2,1)S(1)}, u32[]{:S(2)}, u32[]{:S(2)}) collective-permute-start(bf16[1,4,384]{2,1,0:T(4,128)(2,1)} %get-tuple-element.196), channel_id=1, source_target_pairs={{0,8},{1,9},{2,10},{3,11},{4,12},{5,13},{6,14},{7,15},{8,0},{9,1},... | collective-permute-start | bytes 9224 | tf_op jit(solution)/shard_map/ppermute | solution.py:1373
  13.1 23.3 %collective-permute-start.9 = (bf16[1,1,1,1,24,768]{5,4,3,2,1,0:T(8,128)(2,1)}, bf16[1,1,1,1,24,768]{5,4,3,2,1,0:T(8,128)(2,1)S(1)}, u32[]{:S(2)}, u32[]{:S(2)}) collective-permute-start(bf16[1,1,1,1,24,768]{5,4,3,2,1,0:T(8,128)(2,1)} %bitcast.230), channel_id=1, source_target_pairs={{0,8},{1,9},{2,10},{3,11},{4,12},{5,13},{6,14},{7,15},{8,0},{9,1},... | collective-permute-start | bytes 110600 | tf_op jit(solution)/shard_map/ppermute | solution.py:1373
  13.2 23.2 %collective-permute-start.10 = (bf16[1,1,1,1,24,896]{5,4,3,2,1,0:T(8,128)(2,1)}, bf16[1,1,1,1,24,896]{5,4,3,2,1,0:T(8,128)(2,1)S(1)}, u32[]{:S(2)}, u32[]{:S(2)}) collective-permute-start(bf16[1,1,1,1,24,896]{5,4,3,2,1,0:T(8,128)(2,1)} %bitcast.227), channel_id=1, source_target_pairs={{0,8},{1,9},{2,10},{3,11},{4,12},{5,13},{6,14},{7,15},{8,0},{9,1},... | collective-permute-start | bytes 129032 | tf_op jit(solution)/shard_map/ppermute | solution.py:1373
  16.0 20.4 %collective-permute-start.11 = (bf16[1,1,1,1,24,1920]{5,4,3,2,1,0:T(8,128)(2,1)}, bf16[1,1,1,1,24,1920]{5,4,3,2,1,0:T(8,128)(2,1)S(1)}, u32[]{:S(2)}, u32[]{:S(2)}) collective-permute-start(bf16[1,1,1,1,24,1920]{5,4,3,2,1,0:T(8,128)(2,1)} %bitcast.213), channel_id=1, source_target_pairs={{0,8},{1,9},{2,10},{3,11},{4,12},{5,13},{6,14},{7,15},{8,0},{9,1},... | collective-permute-start | bytes 276488 | tf_op jit(solution)/shard_map/ppermute | solution.py:1373
  16.1 20.3 %collective-permute-start.12 = (bf16[1,1,1,1,96,384]{5,4,3,2,1,0:T(8,128)(2,1)}, bf16[1,1,1,1,96,384]{5,4,3,2,1,0:T(8,128)(2,1)S(1)}, u32[]{:S(2)}, u32[]{:S(2)}) collective-permute-start(bf16[1,1,1,1,96,384]{5,4,3,2,1,0:T(8,128)(2,1)} %bitcast.224), channel_id=1, source_target_pairs={{0,8},{1,9},{2,10},{3,11},{4,12},{5,13},{6,14},{7,15},{8,0},{9,1},... | collective-permute-start | bytes 221192 | tf_op jit(solution)/shard_map/ppermute | solution.py:1373
  45.9 9.4 %collective-permute-start.4 = (f32[8,4,2304]{2,1,0:T(4,128)S(1)}, f32[8,4,2304]{2,1,0:T(4,128)S(1)}, u32[]{:S(2)}, u32[]{:S(2)}) collective-permute-start(f32[8,4,2304]{2,1,0:T(4,128)S(1)} %bitcast.236), channel_id=1, source_target_pairs={{0,1},{1,0},{2,3},{3,2},{4,5},{5,4},{6,7},{7,6},{8,9},{9,8},{10,11... | collective-permute-start | bytes 884744 | tf_op jit(solution)/shard_map/ppermute | solution.py:1373
  49.9 14.3 %collective-permute-start.19 = (bf16[2,2,1,1,24,1920]{5,4,1,0,3,2:T(8,128)(2,1)S(1)}, bf16[2,2,1,1,24,1920]{5,4,1,0,3,2:T(8,128)(2,1)S(1)}, u32[]{:S(2)}, u32[]{:S(2)}) collective-permute-start(bf16[2,2,1,1,24,1920]{5,4,1,0,3,2:T(8,128)(2,1)S(1)} %bitcast.172), channel_id=1, source_target_pairs={{0,1},{1,0},{2,3},{3,2},{4,5},{5,4},{6,7},{7,6},{8,9},{9,8},{10,11... | collective-permute-start | bytes 1105928 | tf_op jit(solution)/shard_map/ppermute | solution.py:1373
  51.4 12.8 %collective-permute-start.20 = (bf16[2,2,1,1,96,384]{5,4,1,0,3,2:T(8,128)(2,1)S(1)}, bf16[2,2,1,1,96,384]{5,4,1,0,3,2:T(8,128)(2,1)S(1)}, u32[]{:S(2)}, u32[]{:S(2)}) collective-permute-start(bf16[2,2,1,1,96,384]{5,4,1,0,3,2:T(8,128)(2,1)S(1)} %bitcast.185), channel_id=1, source_target_pairs={{0,2},{1,3},{2,0},{3,1},{4,6},{5,7},{6,4},{7,5},{8,10},{9,11},{10,... | collective-permute-start | bytes 884744 | tf_op jit(solution)/shard_map/ppermute | solution.py:1373
  52.9 10.9 %collective-permute-start.18 = (bf16[2,2,1,1,24,896]{5,4,1,0,3,2:T(8,128)(2,1)S(1)}, bf16[2,2,1,1,24,896]{5,4,1,0,3,2:T(8,128)(2,1)S(1)}, u32[]{:S(2)}, u32[]{:S(2)}) collective-permute-start(bf16[2,2,1,1,24,896]{5,4,1,0,3,2:T(8,128)(2,1)S(1)} %bitcast.199), channel_id=1, source_target_pairs={{0,2},{1,3},{2,0},{3,1},{4,6},{5,7},{6,4},{7,5},{8,10},{9,11},{10,... | collective-permute-start | bytes 516104 | tf_op jit(solution)/shard_map/ppermute | solution.py:1373
  53.5 10.4 %collective-permute-start.17 = (bf16[2,2,1,1,24,768]{5,4,1,0,3,2:T(8,128)(2,1)S(1)}, bf16[2,2,1,1,24,768]{5,4,1,0,3,2:T(8,128)(2,1)S(1)}, u32[]{:S(2)}, u32[]{:S(2)}) collective-permute-start(bf16[2,2,1,1,24,768]{5,4,1,0,3,2:T(8,128)(2,1)S(1)} %bitcast.202), channel_id=1, source_target_pairs={{0,1},{1,0},{2,3},{3,2},{4,5},{5,4},{6,7},{7,6},{8,9},{9,8},{10,11... | collective-permute-start | bytes 442376 | tf_op jit(solution)/shard_map/ppermute | solution.py:1373
  55.3 8.9 %collective-permute-start.5 = (f32[4,4,2304]{2,1,0:T(4,128)S(1)}, f32[4,4,2304]{2,1,0:T(4,128)S(1)}, u32[]{:S(2)}, u32[]{:S(2)}) collective-permute-start(f32[4,4,2304]{2,1,0:T(4,128)S(1)} %bitcast.241), channel_id=1, source_target_pairs={{0,2},{1,3},{2,0},{3,1},{4,6},{5,7},{6,4},{7,5},{8,10},{9,11},{10,... | collective-permute-start | bytes 442376 | tf_op jit(solution)/shard_map/ppermute | solution.py:1373
  64.4 10.3 %collective-permute-start.22 = (bf16[2,2,2,1,24,896]{5,4,2,1,0,3:T(8,128)(2,1)S(1)}, bf16[2,2,2,1,24,896]{5,4,2,1,0,3:T(8,128)(2,1)S(1)}, u32[]{:S(2)}, u32[]{:S(2)}) collective-permute-start(bf16[2,2,2,1,24,896]{5,4,2,1,0,3:T(8,128)(2,1)S(1)} %bitcast.175), channel_id=1, source_target_pairs={{0,1},{1,0},{2,3},{3,2},{4,5},{5,4},{6,7},{7,6},{8,9},{9,8},{10,11... | collective-permute-start | bytes 1032200 | tf_op jit(solution)/shard_map/ppermute | solution.py:1373
  72.2 19.2 %collective-permute-start.26 = (bf16[2,2,1,2,24,1920]{5,4,3,1,0,2:T(8,128)(2,1)S(1)}, bf16[2,2,1,2,24,1920]{5,4,3,1,0,2:T(8,128)(2,1)S(1)}, u32[]{:S(2)}, u32[]{:S(2)}) collective-permute-start(bf16[2,2,1,2,24,1920]{5,4,3,1,0,2:T(8,128)(2,1)S(1)} %bitcast.157), channel_id=1, source_target_pairs={{0,2},{1,3},{2,0},{3,1},{4,6},{5,7},{6,4},{7,5},{8,10},{9,11},{10,... | collective-permute-start | bytes 2211848 | tf_op jit(solution)/shard_map/ppermute | solution.py:1373
  73.5 17.9 %collective-permute-start.27 = (bf16[2,2,2,1,96,384]{5,4,2,1,0,3:T(8,128)(2,1)S(1)}, bf16[2,2,2,1,96,384]{5,4,2,1,0,3:T(8,128)(2,1)S(1)}, u32[]{:S(2)}, u32[]{:S(2)}) collective-permute-start(bf16[2,2,2,1,96,384]{5,4,2,1,0,3:T(8,128)(2,1)S(1)} %bitcast.163), channel_id=1, source_target_pairs={{0,1},{1,0},{2,3},{3,2},{4,5},{5,4},{6,7},{7,6},{8,9},{9,8},{10,11... | collective-permute-start | bytes 1769480 | tf_op jit(solution)/shard_map/ppermute | solution.py:1373
  137.9 16.1 %collective-permute-start.30 = (bf16[16,24,1536]{2,1,0:T(8,128)(2,1)}, bf16[16,24,1536]{2,1,0:T(8,128)(2,1)S(1)}, u32[]{:S(2)}, u32[]{:S(2)}) collective-permute-start(bf16[16,24,1536]{2,1,0:T(8,128)(2,1)} %get-tuple-element.245), channel_id=1, source_target_pairs={{0,16},{16,0},{1,17},{17,1},{2,18},{18,2},{3,19},{19,3},{4,20},{20... | collective-permute-start | bytes 3538952 | tf_op jit(solution)/shard_map/ppermute | solution.py:1358
  138.1 15.9 %collective-permute-start.31 = (bf16[512,384]{1,0:T(8,128)(2,1)S(1)}, bf16[512,384]{1,0:T(8,128)(2,1)S(1)}, u32[]{:S(2)}, u32[]{:S(2)}) collective-permute-start(bf16[512,384]{1,0:T(8,128)(2,1)S(1)} %copy-done.35), channel_id=1, source_target_pairs={{0,16},{16,0},{1,17},{17,1},{2,18},{18,2},{3,19},{19,3},{4,20},{20... | collective-permute-start | bytes 1179656 | tf_op jit(solution)/shard_map/ppermute | solution.py:1358
  163.3 18.4 %collective-permute-start.33 = (bf16[8,24,1536]{2,1,0:T(8,128)(2,1)S(1)}, bf16[8,24,1536]{2,1,0:T(8,128)(2,1)S(1)}, u32[]{:S(2)}, u32[]{:S(2)}) collective-permute-start(bf16[8,24,1536]{2,1,0:T(8,128)(2,1)S(1)} %bitcast.233), channel_id=1, source_target_pairs={{0,1},{1,0},{2,3},{3,2},{4,5},{5,4},{6,7},{7,6},{8,9},{9,8},{10,11... | collective-permute-start | bytes 1769480 | tf_op jit(solution)/shard_map/ppermute | solution.py:1373
  164.3 14.2 %collective-permute-start.34 = (bf16[8,24,1024]{2,1,0:T(8,128)(2,1)S(1)}, bf16[8,24,1024]{2,1,0:T(8,128)(2,1)S(1)}, u32[]{:S(2)}, u32[]{:S(2)}) collective-permute-start(bf16[8,24,1024]{2,1,0:T(8,128)(2,1)S(1)} %bitcast.235), channel_id=1, source_target_pairs={{0,2},{1,3},{2,0},{3,1},{4,6},{5,7},{6,4},{7,5},{8,10},{9,11},{10,... | collective-permute-start | bytes 1179656 | tf_op jit(solution)/shard_map/ppermute | solution.py:1373
  186.1 19.5 %collective-permute-start.36 = (bf16[4,24,1536]{2,1,0:T(8,128)(2,1)}, bf16[4,24,1536]{2,1,0:T(8,128)(2,1)S(1)}, u32[]{:S(2)}, u32[]{:S(2)}) collective-permute-start(bf16[4,24,1536]{2,1,0:T(8,128)(2,1)} %bitcast.85), channel_id=1, source_target_pairs={{0,2},{1,3},{2,0},{3,1},{4,6},{5,7},{6,4},{7,5},{8,10},{9,11},{10,... | collective-permute-start | bytes 884744 | tf_op jit(solution)/shard_map/ppermute | solution.py:1373
  187.7 17.3 %collective-permute-start.37 = (bf16[4,24,1024]{2,1,0:T(8,128)(2,1)S(1)}, bf16[4,24,1024]{2,1,0:T(8,128)(2,1)S(1)}, u32[]{:S(2)}, u32[]{:S(2)}) collective-permute-start(bf16[4,24,1024]{2,1,0:T(8,128)(2,1)S(1)} %bitcast.239), channel_id=1, source_target_pairs={{0,1},{1,0},{2,3},{3,2},{4,5},{5,4},{6,7},{7,6},{8,9},{9,8},{10,11... | collective-permute-start | bytes 589832 | tf_op jit(solution)/shard_map/ppermute | solution.py:1373
  188.2 20.5 %collective-permute-start.38 = (bf16[8,24,1536]{2,1,0:T(8,128)(2,1)}, bf16[8,24,1536]{2,1,0:T(8,128)(2,1)S(1)}, u32[]{:S(2)}, u32[]{:S(2)}) collective-permute-start(bf16[8,24,1536]{2,1,0:T(8,128)(2,1)} %bitcast.91), channel_id=1, source_target_pairs={{0,1},{1,0},{2,3},{3,2},{4,5},{5,4},{6,7},{7,6},{8,9},{9,8},{10,11... | collective-permute-start | bytes 1769480 | tf_op jit(solution)/shard_map/ppermute | solution.py:1373
  212.9 11.6 %collective-permute-start.40 = (bf16[8,24,1024]{2,1,0:T(8,128)(2,1)S(1)}, bf16[8,24,1024]{2,1,0:T(8,128)(2,1)S(1)}, u32[]{:S(2)}, u32[]{:S(2)}) collective-permute-start(bf16[8,24,1024]{2,1,0:T(8,128)(2,1)S(1)} %bitcast.234), channel_id=1, source_target_pairs={{0,1},{1,0},{2,3},{3,2},{4,5},{5,4},{6,7},{7,6},{8,9},{9,8},{10,11... | collective-permute-start | bytes 1179656 | tf_op jit(solution)/shard_map/ppermute | solution.py:1373
  213.3 10.5 %collective-permute-start.42 = (bf16[4,24,1536]{2,1,0:T(8,128)(2,1)}, bf16[4,24,1536]{2,1,0:T(8,128)(2,1)S(1)}, u32[]{:S(2)}, u32[]{:S(2)}) collective-permute-start(bf16[4,24,1536]{2,1,0:T(8,128)(2,1)} %bitcast.100), channel_id=1, source_target_pairs={{0,2},{1,3},{2,0},{3,1},{4,6},{5,7},{6,4},{7,5},{8,10},{9,11},{10,... | collective-permute-start | bytes 884744 | tf_op jit(solution)/shard_map/ppermute | solution.py:1373
  224.5 26.7 %collective-permute-start.47 = (f32[512,384]{1,0:T(8,128)}, f32[512,384]{1,0:T(8,128)}, u32[]{:S(2)}, u32[]{:S(2)}) collective-permute-start(f32[512,384]{1,0:T(8,128)} %get-tuple-element.341), channel_id=1, source_target_pairs={{0,16},{16,0},{1,17},{17,1},{2,18},{18,2},{3,19},{19,3},{4,20},{20... | collective-permute-start | bytes 2359304 | tf_op jit(solution)/shard_map/ppermute | solution.py:1358
  225.4 10.8 %collective-permute-start.43 = (bf16[4,24,1024]{2,1,0:T(8,128)(2,1)S(1)}, bf16[4,24,1024]{2,1,0:T(8,128)(2,1)S(1)}, u32[]{:S(2)}, u32[]{:S(2)}) collective-permute-start(bf16[4,24,1024]{2,1,0:T(8,128)(2,1)S(1)} %bitcast.240), channel_id=1, source_target_pairs={{0,2},{1,3},{2,0},{3,1},{4,6},{5,7},{6,4},{7,5},{8,10},{9,11},{10,... | collective-permute-start | bytes 589832 | tf_op jit(solution)/shard_map/ppermute | solution.py:1373
  237.6 11.2 %collective-permute-start.45 = (bf16[2,24,2560]{2,1,0:T(8,128)(2,1)S(1)}, bf16[2,24,2560]{2,1,0:T(8,128)(2,1)S(1)}, u32[]{:S(2)}, u32[]{:S(2)}) collective-permute-start(bf16[2,24,2560]{2,1,0:T(8,128)(2,1)S(1)} %bitcast.238), channel_id=1, source_target_pairs={{0,4},{1,5},{2,6},{3,7},{4,0},{5,1},{6,2},{7,3},{8,12},{9,13},{10,... | collective-permute-start | bytes 737288 | tf_op jit(solution)/shard_map/ppermute | solution.py:1373
  239.7 11.5 %collective-permute-start.48 = (bf16[8,2304]{1,0:T(8,128)(2,1)S(1)}, bf16[8,2304]{1,0:T(8,128)(2,1)S(1)}, u32[]{:S(2)}, u32[]{:S(2)}) collective-permute-start(bf16[8,2304]{1,0:T(8,128)(2,1)S(1)} %copy-done.37), channel_id=1, source_target_pairs={{0,16},{16,0},{1,17},{17,1},{2,18},{18,2},{3,19},{19,3},{4,20},{20... | collective-permute-start | bytes 110600 | tf_op jit(solution)/shard_map/ppermute | solution.py:1358
  251.2 15.0 %collective-permute-start.50 = (bf16[1,24,5120]{2,1,0:T(8,128)(2,1)S(1)}, bf16[1,24,5120]{2,1,0:T(8,128)(2,1)S(1)}, u32[]{:S(2)}, u32[]{:S(2)}) collective-permute-start(bf16[1,24,5120]{2,1,0:T(8,128)(2,1)S(1)} %bitcast.237), channel_id=1, source_target_pairs={{0,8},{1,9},{2,10},{3,11},{4,12},{5,13},{6,14},{7,15},{8,0},{9,1},... | collective-permute-start | bytes 737288 | tf_op jit(solution)/shard_map/ppermute | solution.py:1373
  254.6 11.6 %collective-permute-start.51 = (bf16[96,768]{1,0:T(8,128)(2,1)}, bf16[96,768]{1,0:T(8,128)(2,1)S(1)}, u32[]{:S(2)}, u32[]{:S(2)}) collective-permute-start(bf16[96,768]{1,0:T(8,128)(2,1)} %shard_map.340.refs_6_), channel_id=1, source_target_pairs={{0,1},{1,0},{2,3},{3,2},{4,5},{5,4},{6,7},{7,6},{8,9},{9,8},{10,11... | collective-permute-start | bytes 442376 | tf_op jit(solution)/shard_map/ppermute | solution.py:1373
  255.1 11.1 %collective-permute-start.52 = (bf16[96,768]{1,0:T(8,128)(2,1)}, bf16[96,768]{1,0:T(8,128)(2,1)S(1)}, u32[]{:S(2)}, u32[]{:S(2)}) collective-permute-start(bf16[96,768]{1,0:T(8,128)(2,1)} %shard_map.340.refs_6_), channel_id=1, source_target_pairs={{0,2},{1,3},{2,0},{3,1},{4,6},{5,7},{6,4},{7,5},{8,10},{9,11},{10,... | collective-permute-start | bytes 442376 | tf_op jit(solution)/shard_map/ppermute | solution.py:1373
  255.5 10.8 %collective-permute-start.53 = (bf16[96,768]{1,0:T(8,128)(2,1)}, bf16[96,768]{1,0:T(8,128)(2,1)S(1)}, u32[]{:S(2)}, u32[]{:S(2)}) collective-permute-start(bf16[96,768]{1,0:T(8,128)(2,1)} %shard_map.340.refs_6_), channel_id=1, source_target_pairs={{0,3},{1,2},{2,1},{3,0},{4,7},{5,6},{6,5},{7,4},{8,11},{9,10},{10,... | collective-permute-start | bytes 442376 | tf_op jit(solution)/shard_map/ppermute | solution.py:1373
  (64 other events, 305.1 us)
Sparse Core Ops, SparseCore 0:
  138.7 62.7 all-gather.1

commit v2 on v1

--- a/solution.py
+++ b/solution.py
@@ -963,11 +963,13 @@
         out_shape=jax.ShapeDtypeStruct((8, FF), f32),
         in_specs=[VMEM] * 4,
         out_specs=VMEM,
+        compiler_params=pltpu.CompilerParams(vmem_limit_bytes=8 * 1024 * 1024),
     )(b_up, b_down, taps, b_decay)
 
 
 def pack_kernel(
-    w_query, w_key, w_value, w_gate, w_out, w_decay, w_up, conditions, qk, vgd, upo, lifted
+    w_query, w_key, w_value, w_gate, w_out, w_decay, w_up, w_down, w_ada, conditions,
+    qk, vgd, upo, down, ada, lifted,
 ):
     qk[:, :D] = w_query[0]
     qk[:, D:] = w_key[0]
@@ -980,19 +982,22 @@
     vgd[:, 2 * D :] = turned.astype(bf16)
     upo[:, :FF] = w_up[0]
     upo[:, FF:] = w_out[0]
+    down[...] = w_down[0]
+    ada[...] = w_ada[0]
     values = jnp.concatenate([conditions[m].astype(f32) for m in range(MICRO)], axis=0)
     lifted[0] = (values * sigmoid(values)).astype(bf16)
 
 
 def pack(*weights):
     shard = weights[0].shape[1]
-    widths = (2 * D, 2 * D + LANES, FF + D)
+    shapes = [(shard, width) for width in (2 * D, 2 * D + LANES, FF + D)]
+    shapes += [weights[7].shape[1:], weights[8].shape[1:], (1, MICRO * SLOTS, D)]
     return pl.pallas_call(
         pack_kernel,
-        out_shape=[jax.ShapeDtypeStruct((shard, width), bf16) for width in widths]
-        + [jax.ShapeDtypeStruct((1, MICRO * SLOTS, D), bf16)],
+        out_shape=[jax.ShapeDtypeStruct(shape, bf16) for shape in shapes],
         in_specs=[VMEM] * len(weights),
-        out_specs=[VMEM] * (len(widths) + 1),
+        out_specs=[VMEM] * len(shapes),
+        compiler_params=pltpu.CompilerParams(vmem_limit_bytes=8 * 1024 * 1024),
     )(*weights)
 
 
@@ -1165,6 +1170,7 @@
         out_shape=jax.ShapeDtypeStruct((2 * held.shape[0] - SUMS, 2 * D), bf16),
         in_specs=[VMEM] * 2,
         out_specs=VMEM,
+        compiler_params=pltpu.CompilerParams(vmem_limit_bytes=8 * 1024 * 1024),
         cost_estimate=pl.CostEstimate(flops=10**5, bytes_accessed=10**5, transcendentals=0),
     )(held, arrived)
 
@@ -1179,34 +1185,39 @@
 OWN = 16
 
 
-def misc_kernel(mod_one, mod_two, sums_one, sums_two, out):
+def misc_kernel(conditions, mod_one, mod_two, sums_one, sums_two, out):
+    values = conditions[...].astype(f32)
+    values = jnp.where(lax.axis_index("section") == 0, values[:SLOTS], values[SLOTS:])
+    lifted = values * sigmoid(values)
+    spare = [jnp.concatenate([lifted[0:1], lifted[1:2]], axis=1), jnp.zeros((1, 2 * D), f32)]
     rows = []
     for mod in (mod_one, mod_two):
         for slot in range(SLOTS):
             for i in range(3):
                 part = mod[slot : slot + 1, i * 2 * D : (i + 1) * 2 * D]
                 rows.append(part.astype(f32))
-        rows.append(jnp.zeros((OWN // 2 - 3 * SLOTS, 2 * D), f32))
+        rows.extend(spare)
     sums = jnp.concatenate([sums_one[...], sums_two[...]], axis=0)
     rows.extend(part.astype(f32) for part in split(sums))
     out[...] = jnp.concatenate(rows, axis=0).astype(bf16)
 
 
-def pack_misc(mod_one, mod_two, sums_one, sums_two):
+def pack_misc(conditions, mod_one, mod_two, sums_one, sums_two):
     return pl.pallas_call(
         misc_kernel,
         out_shape=jax.ShapeDtypeStruct((OWN + SUMS, 2 * D), bf16),
-        in_specs=[VMEM] * 4,
+        in_specs=[VMEM] * 5,
         out_specs=VMEM,
-    )(mod_one, mod_two, sums_one, sums_two)
+        compiler_params=pltpu.CompilerParams(vmem_limit_bytes=8 * 1024 * 1024),
+    )(conditions, mod_one, mod_two, sums_one, sums_two)
 
 
 def finish_kernel(widths, counts, waits, *refs):
     count = len(widths)
     kept, refs = refs[:count], refs[count:]
     came, refs = refs[: len(counts)], refs[len(counts) :]
-    lifted, *parts = refs[:5]
-    mine, other, small_mine, small_other = refs[5 + waits :]
+    parts = refs[:4]
+    mine, other, small_mine, small_other = refs[4 + waits :]
     places = [(ref, i) for ref, many in zip(came, counts) for i in range(many)]
     added = []
     for i in range(count):
@@ -1217,12 +1228,17 @@
     size = parts[0].shape[0] - SUMS
     rows = jnp.concatenate([part[:size, :] for part in parts], axis=0)
     rows = rows.astype(f32).reshape(-1, OWN, 2 * D)
+    shard = mine.shape[0]
+    chosen = lane_iota(shard, D) == row_iota(shard, D) + lax.axis_index("row") * shard
+    chosen = jnp.where(chosen, 1.0, 0.0).astype(bf16)
+    features = [rows[:, 6, slot * D : (slot + 1) * D].astype(bf16) for slot in range(SLOTS)]
+    lifted = jnp.concatenate([mm_t(chosen, part) for part in features], axis=1).astype(bf16)
 
     def ada(first):
         columns = []
         for i in range(3):
             both = [rows[:, first + 3 * slot + i, :] for slot in range(SLOTS)]
-            columns.append(mm(lifted[...], jnp.concatenate(both, axis=0).astype(bf16)))
+            columns.append(mm(lifted, jnp.concatenate(both, axis=0).astype(bf16)))
         return jnp.concatenate(columns, axis=1)
 
     first = lax.axis_index("section") == 0
@@ -1238,7 +1254,7 @@
     small_other[...] = jnp.where(first, two, one)
 
 
-def finish(kept, came, lifted, parts, after):
+def finish(kept, came, parts, after):
     widths = [array.shape[2] for array in kept]
     shard = kept[0].shape[1]
     wide = GROUP + FF + 6 * D
@@ -1247,10 +1263,10 @@
     return pl.pallas_call(
         functools.partial(finish_kernel, widths, [count for _, count in came], len(after)),
         out_shape=[jax.ShapeDtypeStruct(shape, f32) for shape in shapes],
-        in_specs=[VMEM] * (len(kept) + len(came) + 5) + [ANY] * len(after),
+        in_specs=[VMEM] * (len(kept) + len(came) + 4) + [ANY] * len(after),
         out_specs=[VMEM] * 4,
         compiler_params=pltpu.CompilerParams(vmem_limit_bytes=8 * 1024 * 1024),
-    )(*kept, *arrays, lifted, *parts, *after)
+    )(*kept, *arrays, *parts, *after)
 
 
 def output_kernel(mine, other, small_mine, small_other, *outs):
@@ -1305,6 +1321,7 @@
         out_shape=[jax.ShapeDtypeStruct(shape, f32) for shape in shapes],
         in_specs=[VMEM] * 4,
         out_specs=[VMEM] * len(shapes),
+        compiler_params=pltpu.CompilerParams(vmem_limit_bytes=8 * 1024 * 1024),
     )(mine, other, small_mine, small_other)
 
 
@@ -1351,6 +1368,7 @@
             pltpu.VMEM((MICRO,) + one.shape, one.dtype),
             pltpu.SemaphoreType.DMA((4,)),
         ],
+        compiler_params=pltpu.CompilerParams(vmem_limit_bytes=8 * 1024 * 1024),
     )(one, two, came)
 
 
@@ -1415,34 +1433,35 @@
     def both(values):
         return values, swap(values)
 
-    qk, vgd, upo, lifted = pack(
-        w_query, w_key, w_value, w_gate, w_out, w_decay.transpose(0, 2, 1), w_up, conditions
+    qk, vgd, upo, down, ada, lifted = pack(
+        w_query, w_key, w_value, w_gate, w_out, w_decay.transpose(0, 2, 1), w_up, w_down, w_ada,
+        conditions,
     )
     small = pack_small(b_up, b_down, conv_kernel, b_decay)
+    conds = conditions.reshape(MICRO * SLOTS, D)
     steps = gather_steps(along_x, along_y, along_z)
-    order = tuple(reversed(along_z)) + along_x[:-1] + along_y[:-1] + along_x[-1:] + along_y[-1:]
-    term_bits = along_x + along_y + along_z
-    spans = len(steps) - 2
-    bounds = [len(term_bits) * i // spans for i in range(spans + 1)]
-    term_bits = [term_bits[bounds[i] : bounds[i + 1]] for i in range(spans)]
-    left = list(order)
-    held = [single(array) for array in (qk, vgd, upo, w_down[0])]
+    lag = len(along_z)
+    plane = along_x + along_y
+    bounds = [len(plane) * i // lag for i in range(lag + 1)]
+    held = [single(array) for array in (qk, vgd, upo, down)]
+    ada = single(ada)
     for place, pair in enumerate(steps):
         bits = pair + pair
         came = [partner(array, bit) for array, bit in zip(held, bits)]
-        after = (small,)
-        if place == 1:
-            for bit in order:
-                lifted = jnp.concatenate([lifted, partner(lifted, bit)], axis=0)
-            after = (lifted,)
-        if place == 2:
-            lifted_cut = lax.dynamic_slice_in_dim(
-                lifted, lax.axis_index("row") * shard, shard, 2
-            )
-            product = mm(lifted_cut.reshape(devices * MICRO * SLOTS, shard), w_ada[0])
-            terms = (product.reshape(devices, MICRO * SLOTS, 6 * D),)
-        if place >= 2:
-            for bit in term_bits[place - 2]:
+        after = ()
+        if place < lag:
+            lifted = jnp.concatenate([lifted, partner(lifted, pair[0])], axis=0)
+            for bit in plane[bounds[place] : bounds[place + 1]]:
+                (ada,) = join([ada], [partner(ada, bit)], (bit,))
+            after = (small, lifted, ada)
+        if place == lag:
+            left = list(reversed(along_z))
+            rows = D >> lag
+            line = (lax.axis_index("row") >> len(plane)) * rows
+            lifted = lax.dynamic_slice_in_dim(lifted, line, rows, 2)
+            product = mm(lifted.reshape(-1, rows), flat(ada))
+            terms = (product.reshape(1 << lag, MICRO * SLOTS, 6 * D),)
+            for bit in along_z:
                 stays, goes = term_step(1 << left.index(bit), *terms)
                 left.remove(bit)
                 terms = (stays, partner(goes, bit))
@@ -1515,12 +1534,8 @@
         return mod
 
     x_bits, y_bits, z_bits = along_x, along_y, along_z
-    lifted = lifted_cut.reshape(devices, MICRO, SLOTS, shard)
-    lifted = lax.dynamic_index_in_dim(lifted, section, 1, keepdims=False)
-    lifted = lifted.transpose(2, 1, 0).reshape(shard, SLOTS * devices)
-
     carried, mid_grad, f2_keep, f2_sent, f2_sums = ffn_step(1, output_grad)
-    *carried, f2_sent, acts_sent, lifted = lock(*carried, f2_sent, acts_sent[0], lifted)
+    *carried, f2_sent, acts_sent = lock(*carried, f2_sent, acts_sent[0])
     f2_came = swap(f2_sent)
     acts_came = swap(acts_sent)
     low, a2_keep, a2_sent, m2_sums = mixer_step(1, carried)
@@ -1559,7 +1574,7 @@
     gx_one, _, mod_low_one, sums_one, gx_sent, mod_mine, mod_sent = input_step(
         0, low, mid_grad, f1_sums, m1_sums, (gx_two, mod_low_two)
     )
-    misc = pack_misc(mod_low_one, mod_low_two, sums_one, sums_two)
+    misc = pack_misc(conds, mod_low_one, mod_low_two, sums_one, sums_two)
     misc, a1_came, two_came, f1_came, gx_sent, mod_sent = lock(
         misc, a1_came, two_came, f1_came, gx_sent, mod_sent
     )
@@ -1589,7 +1604,7 @@
     grad_lifted = lifted_grads(mod_mine, mod_came, ada_all)
     lifted_came = swap(grad_lifted)
     mine, other, small_mine, small_other = finish(
-        keep, came, lifted, parts, (gx_mark, acts_mark, lifted_came)
+        keep, came, parts, (gx_mark, acts_mark, lifted_came)
     )
     came, small_came = swap(other), swap(small_other)
     (

time: 285 us -> 274 us (0.961)
  Pallas kernels: 135 us -> 126 us
  waiting for transfers between devices: 48.3 us -> 55.8 us
  starting transfers between devices: 57.1 us -> 53.2 us
    ppermute x40 -> x38, waiting for transfers between devices: 39.8 us -> 47.8 us  [across(): return lax.ppermute(values, 'row', [(i, i ^ flips) for i in range(size)])]
    ppermute x40 -> x38, starting transfers between devices: 54.5 us -> 50.5 us  [across(): return lax.ppermute(values, 'row', [(i, i ^ flips) for i in range(size)])]
    pallas_call x2, Pallas kernels: 3.21 us -> 0.05 us  [misc_step(): pl.pallas_call(misc_step_kernel, out_shape=jax.ShapeDtypeStruct((2 * held...]
    pallas_call x2, Pallas kernels: 5.45 us -> 2.59 us  [both_micros(): pl.pallas_call(both_kernel, out_shape=[jax.ShapeDtypeStruct((MICRO,) + on...]
    unnamed x84 -> x97, local copies, waits for them, and re-layouts: 21.4 us -> 19.3 us
  transfers between devices with their start and end apart: 57 -> 55, of which waited for: 19 -> 20; matrix products, arithmetic and copies ran while one was open for 2% -> 1% of each run, Pallas kernels for 33% -> 32%
where the time goes in v2:
time: 274 us; the launch traced here: 270 us
  Pallas kernels  126 us (46%)
  waiting for transfers between devices  55.8 us (20%)
  starting transfers between devices  53.2 us (19%)
  local copies, waits for them, and re-layouts  19.4 us (7%)
  between operations  15.1 us (6%)
    pallas_call x10, Pallas kernels, call(): pl.pallas_call(kernel, out_shape=[jax.ShapeDtypeStruct(shape, kind) for s...  102 us
    ppermute x38, starting transfers between devices, across(): return lax.ppermute(values, 'row', [(i, i ^ flips) for i in range(size)])  50.5 us
    ppermute x38, waiting for transfers between devices, across(): return lax.ppermute(values, 'row', [(i, i ^ flips) for i in range(size)])  47.8 us
    unnamed x97, local copies, waits for them, and re-layouts  19.3 us
    pallas_call x11, Pallas kernels, step(): pl.pallas_call(functools.partial(step_kernel, bit, widths, [count for _,...  14.5 us
    ppermute x16, waiting for transfers between devices, swap(): return lax.ppermute(values, 'section', [(0, 1), (1, 0)])  7.96 us
  transfers between devices with their start and end apart: 55, of which 20 were waited for; matrix products, arithmetic and copies ran while one was open for 1% of the time, Pallas kernels for 32%

profile of v2, /device:TPU:0, one launch (start us, length us, event | category | flops | bytes accessed | tf_op | source)
XLA Modules:
  0.0 269.9 jit_solution(15776866480253864041)
XLA Ops:
  15.1 4.0 %collective-permute-start = (bf16[1,4,384]{2,1,0:T(4,128)(2,1)S(1)}, bf16[1,4,384]{2,1,0:T(4,128)(2,1)S(1)}, u32[]{:S(2)}, u32[]{:S(2)}) collective-permute-start(bf16[1,4,384]{2,1,0:T(4,128)(2,1)S(1)} %get-tuple-element.193), channel_id=1, source_target_pairs={{0,8},{1,9},{2,10},{3,11},{4,12},{5,13},{6,14},{7,15},{8,0},{9,1},... | collective-permute-start | bytes 9224 | tf_op jit(solution)/shard_map/ppermute | solution.py:1391
  20.9 2.6 collective-permute-start.8
  26.6 2.7 collective-permute-start.10
  30.9 3.1 %collective-permute-done.10 = bf16[1,1,1,1,96,384]{5,4,3,2,1,0:T(8,128)(2,1)S(1)} collective-permute-done((bf16[1,1,1,1,96,384]{5,4,3,2,1,0:T(8,128)(2,1)S(1)}, bf16[1,1,1,1,96,384]{5,4,3,2,1,0:T(8,128)(2,1)S(1)}, u32[]{:S(2)}, u32[]{:S(2)}) %collective-permute-start.10) | collective-permute-done | bytes 73760 | tf_op jit(solution)/shard_map/ppermute | solution.py:1391
  34.2 2.0 collective-permute-start.14
  38.2 6.3 %collective-permute-done.1 = bf16[2,4,384]{2,1,0:T(4,128)(2,1)S(1)} collective-permute-done((bf16[2,4,384]{2,1,0:T(4,128)(2,1)S(1)}, bf16[2,4,384]{2,1,0:T(4,128)(2,1)S(1)}, u32[]{:S(2)}, u32[]{:S(2)}) %collective-permute-start.1) | collective-permute-done | bytes 6176 | tf_op jit(solution)/shard_map/ppermute | solution.py:1391
  45.4 3.6 %collective-permute-done.12 = bf16[2,1,1,1,24,896]{5,4,0,3,2,1:T(8,128)(2,1)S(1)} collective-permute-done((bf16[2,1,1,1,24,896]{5,4,0,3,2,1:T(8,128)(2,1)S(1)}, bf16[2,1,1,1,24,896]{5,4,0,3,2,1:T(8,128)(2,1)S(1)}, u32[]{:S(2)}, u32[]{:S(2)}) %collective-permute-start.12) | collective-permute-done | bytes 86048 | tf_op jit(solution)/shard_map/ppermute | solution.py:1391
  53.8 4.2 %collective-permute-done.4 = f32[2,4,2304]{2,1,0:T(4,128)S(1)} collective-permute-done((f32[2,4,2304]{2,1,0:T(4,128)S(1)}, f32[2,4,2304]{2,1,0:T(4,128)S(1)}, u32[]{:S(2)}, u32[]{:S(2)}) %collective-permute-start.4) | collective-permute-done | bytes 73760 | tf_op jit(solution)/shard_map/ppermute | solution.py:1391
  58.2 4.7 %collective-permute-done.5.refs_8_ = f32[1,4,2304]{2,1,0:T(4,128)S(1)} collective-permute-done((f32[1,4,2304]{2,1,0:T(4,128)S(1)}, f32[1,4,2304]{2,1,0:T(4,128)S(1)}, u32[]{:S(2)}, u32[]{:S(2)}) %collective-permute-start.5) | collective-permute-done | bytes 36896 | tf_op jit(solution)/shard_map/ppermute | solution.py:1391
  68.0 5.6 %collective-permute-done.19 = bf16[2,2,1,2,24,768]{5,4,3,1,0,2:T(8,128)(2,1)} collective-permute-done((bf16[2,2,1,2,24,768]{5,4,3,1,0,2:T(8,128)(2,1)}, bf16[2,2,1,2,24,768]{5,4,3,1,0,2:T(8,128)(2,1)}, u32[]{:S(2)}, u32[]{:S(2)}) %collective-permute-start.19) | collective-permute-done | bytes 294944 | tf_op jit(solution)/shard_map/ppermute | solution.py:1391
  73.7 2.2 shard_map.314
  80.3 9.2 %shard_map.315 = (bf16[512,384]{1,0:T(8,128)(2,1)}, f32[512,1536]{1,0:T(8,128)}, f32[512,128]{1,0:T(8,128)}, f32[512,384]{1,0:T(8,128)}, f32[512,128]{1,0:T(8,12...) custom-call(s32[2,1]{1,0:T(2,128)} %copy.37.refs_0_, bf16[2,512,384]{2,1,0:T(8,128)(2,1)} %refs_6_.3, ...), custom_call_target="tpu_custom_call" | custom-call | flops 4000000000 | bytes 4194304 | tf_op jit(solution)/shard_map/pallas_call | solution.py:735
  91.3 4.4 %collective-permute-done.27.refs_12_ = bf16[1536,384]{1,0:T(8,128)(2,1)S(1)} collective-permute-done((bf16[1536,384]{1,0:T(8,128)(2,1)S(1)}, bf16[1536,384]{1,0:T(8,128)(2,1)S(1)}, u32[]{:S(2)}, u32[]{:S(2)}) %collective-permute-start.27) | collective-permute-done | bytes 1179680 | tf_op jit(solution)/shard_map/ppermute | solution.py:1376
  97.9 6.6 %shard_map.317 = (bf16[512,384]{1,0:T(8,128)(2,1)}, f32[512,384]{1,0:T(8,128)}, f32[512,384]{1,0:T(8,128)}) custom-call(s32[2,1]{1,0:T(2,128)} %copy.37.refs_0_, bf16[512,384]{1,0:T(8,128)(2,1)} %get-tuple-element.215.refs_4_.refs_1_.refs_13_, bf16[2,512,384]{2,1,0:T(8,128)(2,1)} %refs_6_.3, bf16[384,1920]{1,0:T(8,128)(2,1)} %bitcast.238, ...), custom_call_target="tpu_custom_call" | custom-call | flops 3000000000 | bytes 4194304 | tf_op jit(solution)/shard_map/pallas_call | solution.py:735
  104.5 9.8 %shard_map.318 = (bf16[512,384]{1,0:T(8,128)(2,1)}, f32[512,1536]{1,0:T(8,128)}, f32[512,128]{1,0:T(8,128)}, f32[512,384]{1,0:T(8,128)}, f32[512,128]{1,0:T(8,12...) custom-call(s32[2,1]{1,0:T(2,128)} %copy.37.refs_0_, bf16[1,512,384]{2,1,0:T(8,128)(2,1)} %bitcast.170, ...), custom_call_target="tpu_custom_call" | custom-call | flops 4000000000 | bytes 4194304 | tf_op jit(solution)/shard_map/pallas_call | solution.py:735
  114.4 6.8 %shard_map.319 = (bf16[512,384]{1,0:T(8,128)(2,1)}, f32[512,384]{1,0:T(8,128)}, f32[512,384]{1,0:T(8,128)}, bf16[512,384]{1,0:T(8,128)(2,1)}) custom-call(s32[2,1]{1,0:T(2,128)} %copy.37.refs_0_, bf16[512,384]{1,0:T(8,128)(2,1)} %get-tuple-element.221.refs_1_.refs_13_, bf16[1,512,384]{2,1,0:T(8,128)(2,1)} %bitcast.171, bf16[384,1920]{1,0:T(8,128)(2,1)} %bitcast.240, ...), custom_call_target="tpu_custom_call" | custom-call | flops 3000000000 | bytes 4194304 | tf_op jit(solution)/shard_map/pallas_call | solution.py:735
  121.2 13.4 %shard_map.320 = (f32[512,384]{1,0:T(8,128)}, bf16[512,384]{1,0:T(8,128)(2,1)}, f32[384,384]{1,0:T(8,128)}, f32[8,1536]{1,0:T(8,128)}, f32[16,24,1536]{2,1,0:T(8,128)}, /*index=5*/bf16[16,24,1536]{2,1,0:T(8,128)(2,1)}) custom-call(s32[2,1]{1,0:T(2,128)} %copy.37.refs_0_, f32[4,2304]{1,0:T(4,128)} %copy-done.38, f32[4,2304]{1,0:T(4,128)} %copy-done.44, ...), custom_call_target="tpu_custom_call" | custom-call | flops 5000000000 | bytes 4194304 | tf_op jit(solution)/shard_map/pallas_call | solution.py:735
  135.2 15.5 %shard_map.321 = (bf16[512,1664]{1,0:T(8,128)(2,1)}, f32[384,1024]{1,0:T(8,128)}, bf16[384,1024]{1,0:T(8,128)(2,1)}, f32[8,384]{1,0:T(8,128)}) custom-call(s32[2,1]{1,0:T(2,128)} %copy.37.refs_0_, bf16[512,384]{1,0:T(8,128)(2,1)} %get-tuple-element.229.refs_1_, bf16[384,1920]{1,0:T(8,128)(2,1)} %bitcast.243, bf16[384,1920]{1,0:T(8,128)(2,1)} %copy-done.40, ...), custom_call_target="tpu_custom_call" | custom-call | flops 7000000000 | bytes 4194304 | tf_op jit(solution)/shard_map/pallas_call | solution.py:735
  152.0 6.8 %shard_map.323 = (f32[512,384]{1,0:T(8,128)}, bf16[512,384]{1,0:T(8,128)(2,1)}, bf16[8,2304]{1,0:T(8,128)(2,1)}, f32[8,768]{1,0:T(8,128)}) custom-call(s32[2,1]{1,0:T(2,128)} %copy.37.refs_0_, bf16[512,1664]{1,0:T(8,128)(2,1)} %get-tuple-element.244.refs_1_, bf16[384,768]{1,0:T(8,128)(2,1)} %bitcast.61.refs_4_.refs_2_, ...), custom_call_target="tpu_custom_call" | custom-call | flops 2000000000 | bytes 4194304 | tf_op jit(solution)/shard_map/pallas_call | solution.py:735
  160.9 2.5 collective-permute-start.32
  163.4 13.0 %shard_map.326 = (f32[512,384]{1,0:T(8,128)}, bf16[512,384]{1,0:T(8,128)(2,1)}, f32[384,384]{1,0:T(8,128)}, f32[8,1536]{1,0:T(8,128)}, f32[16,24,1536]{2,1,0:T(8,128)}, /*index=5*/bf16[16,24,1536]{2,1,0:T(8,128)(2,1)}) custom-call(s32[2,1]{1,0:T(2,128)} %copy.37.refs_0_, f32[4,2304]{1,0:T(4,128)} %copy-done.38, f32[4,2304]{1,0:T(4,128)} %copy-done.44, ...), custom_call_target="tpu_custom_call" | custom-call | flops 5000000000 | bytes 4194304 | tf_op jit(solution)/shard_map/pallas_call | solution.py:735
  186.5 15.2 %shard_map.330 = (bf16[512,1664]{1,0:T(8,128)(2,1)}, f32[384,1024]{1,0:T(8,128)}, bf16[384,1024]{1,0:T(8,128)(2,1)}, f32[8,384]{1,0:T(8,128)}) custom-call(s32[2,1]{1,0:T(2,128)} %copy.37.refs_0_, bf16[512,384]{1,0:T(8,128)(2,1)} %get-tuple-element.276.refs_1_, bf16[384,1920]{1,0:T(8,128)(2,1)} %bitcast.245, bf16[384,1920]{1,0:T(8,128)(2,1)} %copy-done.40, ...), custom_call_target="tpu_custom_call" | custom-call | flops 7000000000 | bytes 4194304 | tf_op jit(solution)/shard_map/pallas_call | solution.py:735
  202.5 3.0 %collective-permute-done.36 = bf16[8,24,1536]{2,1,0:T(8,128)(2,1)S(1)} collective-permute-done((bf16[8,24,1536]{2,1,0:T(8,128)(2,1)}, bf16[8,24,1536]{2,1,0:T(8,128)(2,1)S(1)}, u32[]{:S(2)}, u32[]{:S(2)}) %collective-permute-start.36) | collective-permute-done | bytes 589856 | tf_op jit(solution)/shard_map/ppermute | solution.py:1391
  206.5 2.2 shard_map.331
  214.6 5.8 %shard_map.334 = (f32[512,384]{1,0:T(8,128)}, bf16[512,384]{1,0:T(8,128)(2,1)}, bf16[8,2304]{1,0:T(8,128)(2,1)}, f32[8,768]{1,0:T(8,128)}, f32[512,384]{1,0:T(8,...) custom-call(s32[2,1]{1,0:T(2,128)} %copy.37.refs_0_, bf16[512,1664]{1,0:T(8,128)(2,1)} %get-tuple-element.303.refs_1_, ...), custom_call_target="tpu_custom_call" | custom-call | flops 2000000000 | bytes 4194304 | tf_op jit(solution)/shard_map/pallas_call | solution.py:735
  225.1 2.4 collective-permute-start.42
  227.5 4.5 %collective-permute-done.42.arrived = bf16[48,768]{1,0:T(8,128)(2,1)S(1)} collective-permute-done((bf16[48,768]{1,0:T(8,128)(2,1)S(1)}, bf16[48,768]{1,0:T(8,128)(2,1)S(1)}, u32[]{:S(2)}, u32[]{:S(2)}) %collective-permute-start.42) | collective-permute-done | bytes 73760 | tf_op jit(solution)/shard_map/ppermute | solution.py:1391
  235.8 6.7 %collective-permute-done.44.arrived = bf16[64,768]{1,0:T(8,128)(2,1)S(1)} collective-permute-done((bf16[64,768]{1,0:T(8,128)(2,1)S(1)}, bf16[64,768]{1,0:T(8,128)(2,1)S(1)}, u32[]{:S(2)}, u32[]{:S(2)}) %collective-permute-start.44) | collective-permute-done | bytes 98336 | tf_op jit(solution)/shard_map/ppermute | solution.py:1391
  242.6 2.4 shard_map.339
  245.0 3.4 %collective-permute-start.48 = (bf16[1,24,5120]{2,1,0:T(8,128)(2,1)S(1)}, bf16[1,24,5120]{2,1,0:T(8,128)(2,1)S(1)}, u32[]{:S(2)}, u32[]{:S(2)}) collective-permute-start(bf16[1,24,5120]{2,1,0:T(8,128)(2,1)S(1)} %bitcast.253), channel_id=1, source_target_pairs={{0,8},{1,9},{2,10},{3,11},{4,12},{5,13},{6,14},{7,15},{8,0},{9,1},... | collective-permute-start | bytes 737288 | tf_op jit(solution)/shard_map/ppermute | solution.py:1391
  249.3 2.6 collective-permute-start.51
  256.6 2.7 %collective-permute-done.48.refs_4_ = bf16[1,24,5120]{2,1,0:T(8,128)(2,1)S(1)} collective-permute-done((bf16[1,24,5120]{2,1,0:T(8,128)(2,1)S(1)}, bf16[1,24,5120]{2,1,0:T(8,128)(2,1)S(1)}, u32[]{:S(2)}, u32[]{:S(2)}) %collective-permute-start.48) | collective-permute-done | bytes 245792 | tf_op jit(solution)/shard_map/ppermute | solution.py:1391
  (226 shorter events, 74.7 us)
Async XLA Ops:
  7.2 194.5 %all-gather.2.cloned.1.call-start = ((), (), s32[]{:S(2)}) async-start(), calls=%async_computation | async-start | bytes 1880064 | tf_op jit(solution)/shard_map/all_gather | solution.py:1492
  15.1 14.2 %collective-permute-start = (bf16[1,4,384]{2,1,0:T(4,128)(2,1)S(1)}, bf16[1,4,384]{2,1,0:T(4,128)(2,1)S(1)}, u32[]{:S(2)}, u32[]{:S(2)}) collective-permute-start(bf16[1,4,384]{2,1,0:T(4,128)(2,1)S(1)} %get-tuple-element.193), channel_id=1, source_target_pairs={{0,8},{1,9},{2,10},{3,11},{4,12},{5,13},{6,14},{7,15},{8,0},{9,1},... | collective-permute-start | bytes 9224 | tf_op jit(solution)/shard_map/ppermute | solution.py:1391
  20.6 10.3 %collective-permute-start.7 = (bf16[1,1,1,1,24,768]{5,4,3,2,1,0:T(8,128)(2,1)S(1)}, bf16[1,1,1,1,24,768]{5,4,3,2,1,0:T(8,128)(2,1)S(1)}, u32[]{:S(2)}, u32[]{:S(2)}) collective-permute-start(bf16[1,1,1,1,24,768]{5,4,3,2,1,0:T(8,128)(2,1)S(1)} %bitcast.233), channel_id=1, source_target_pairs={{0,8},{1,9},{2,10},{3,11},{4,12},{5,13},{6,14},{7,15},{8,0},{9,1},... | collective-permute-start | bytes 110600 | tf_op jit(solution)/shard_map/ppermute | solution.py:1391
  20.9 10.0 %collective-permute-start.8 = (bf16[1,1,1,1,24,896]{5,4,3,2,1,0:T(8,128)(2,1)S(1)}, bf16[1,1,1,1,24,896]{5,4,3,2,1,0:T(8,128)(2,1)S(1)}, u32[]{:S(2)}, u32[]{:S(2)}) collective-permute-start(bf16[1,1,1,1,24,896]{5,4,3,2,1,0:T(8,128)(2,1)S(1)} %bitcast.230), channel_id=1, source_target_pairs={{0,8},{1,9},{2,10},{3,11},{4,12},{5,13},{6,14},{7,15},{8,0},{9,1},... | collective-permute-start | bytes 129032 | tf_op jit(solution)/shard_map/ppermute | solution.py:1391
  23.5 10.5 %collective-permute-start.9 = (bf16[1,1,1,1,24,1920]{5,4,3,2,1,0:T(8,128)(2,1)S(1)}, bf16[1,1,1,1,24,1920]{5,4,3,2,1,0:T(8,128)(2,1)S(1)}, u32[]{:S(2)}, u32[]{:S(2)}) collective-permute-start(bf16[1,1,1,1,24,1920]{5,4,3,2,1,0:T(8,128)(2,1)S(1)} %bitcast.216), channel_id=1, source_target_pairs={{0,8},{1,9},{2,10},{3,11},{4,12},{5,13},{6,14},{7,15},{8,0},{9,1},... | collective-permute-start | bytes 276488 | tf_op jit(solution)/shard_map/ppermute | solution.py:1391
  29.3 15.5 %collective-permute-start.3 = (bf16[1,1,1,2,24,2304]{5,4,3,2,1,0:T(8,128)(2,1)S(1)}, bf16[1,1,1,2,24,2304]{5,4,3,2,1,0:T(8,128)(2,1)S(1)}, u32[]{:S(2)}, u32[]{:S(2)}) collective-permute-start(bf16[1,1,1,2,24,2304]{5,4,3,2,1,0:T(8,128)(2,1)S(1)} %bitcast.146), channel_id=1, source_target_pairs={{0,2},{1,3},{2,0},{3,1},{4,6},{5,7},{6,4},{7,5},{8,10},{9,11},{10,... | collective-permute-start | bytes 663560 | tf_op jit(solution)/shard_map/ppermute | solution.py:1391
  34.1 14.9 %collective-permute-start.13 = (bf16[2,1,1,1,24,1920]{5,4,0,3,2,1:T(8,128)(2,1)S(1)}, bf16[2,1,1,1,24,1920]{5,4,0,3,2,1:T(8,128)(2,1)S(1)}, u32[]{:S(2)}, u32[]{:S(2)}) collective-permute-start(bf16[2,1,1,1,24,1920]{5,4,0,3,2,1:T(8,128)(2,1)S(1)} %bitcast.197), channel_id=1, source_target_pairs={{0,4},{1,5},{2,6},{3,7},{4,0},{5,1},{6,2},{7,3},{8,12},{9,13},{10,... | collective-permute-start | bytes 552968 | tf_op jit(solution)/shard_map/ppermute | solution.py:1391
  34.2 14.8 %collective-permute-start.14 = (bf16[2,1,1,1,96,384]{5,4,0,3,2,1:T(8,128)(2,1)S(1)}, bf16[2,1,1,1,96,384]{5,4,0,3,2,1:T(8,128)(2,1)S(1)}, u32[]{:S(2)}, u32[]{:S(2)}) collective-permute-start(bf16[2,1,1,1,96,384]{5,4,0,3,2,1:T(8,128)(2,1)S(1)} %bitcast.203), channel_id=1, source_target_pairs={{0,4},{1,5},{2,6},{3,7},{4,0},{5,1},{6,2},{7,3},{8,12},{9,13},{10,... | collective-permute-start | bytes 442376 | tf_op jit(solution)/shard_map/ppermute | solution.py:1391
  36.3 9.1 %collective-permute-start.11 = (bf16[2,1,1,1,24,768]{5,4,0,3,2,1:T(8,128)(2,1)S(1)}, bf16[2,1,1,1,24,768]{5,4,0,3,2,1:T(8,128)(2,1)S(1)}, u32[]{:S(2)}, u32[]{:S(2)}) collective-permute-start(bf16[2,1,1,1,24,768]{5,4,0,3,2,1:T(8,128)(2,1)S(1)} %bitcast.224), channel_id=1, source_target_pairs={{0,4},{1,5},{2,6},{3,7},{4,0},{5,1},{6,2},{7,3},{8,12},{9,13},{10,... | collective-permute-start | bytes 221192 | tf_op jit(solution)/shard_map/ppermute | solution.py:1391
  49.1 13.9 %collective-permute-start.17 = (bf16[2,2,1,1,24,1920]{5,4,1,0,3,2:T(8,128)(2,1)S(1)}, bf16[2,2,1,1,24,1920]{5,4,1,0,3,2:T(8,128)(2,1)S(1)}, u32[]{:S(2)}, u32[]{:S(2)}) collective-permute-start(bf16[2,2,1,1,24,1920]{5,4,1,0,3,2:T(8,128)(2,1)S(1)} %bitcast.178), channel_id=1, source_target_pairs={{0,1},{1,0},{2,3},{3,2},{4,5},{5,4},{6,7},{7,6},{8,9},{9,8},{10,11... | collective-permute-start | bytes 1105928 | tf_op jit(solution)/shard_map/ppermute | solution.py:1391
  49.7 13.3 %collective-permute-start.18 = (bf16[2,2,1,1,96,384]{5,4,1,0,3,2:T(8,128)(2,1)S(1)}, bf16[2,2,1,1,96,384]{5,4,1,0,3,2:T(8,128)(2,1)S(1)}, u32[]{:S(2)}, u32[]{:S(2)}) collective-permute-start(bf16[2,2,1,1,96,384]{5,4,1,0,3,2:T(8,128)(2,1)S(1)} %bitcast.185), channel_id=1, source_target_pairs={{0,2},{1,3},{2,0},{3,1},{4,6},{5,7},{6,4},{7,5},{8,10},{9,11},{10,... | collective-permute-start | bytes 884744 | tf_op jit(solution)/shard_map/ppermute | solution.py:1391
  51.3 11.7 %collective-permute-start.15 = (bf16[2,2,1,1,24,768]{5,4,1,0,3,2:T(8,128)(2,1)S(1)}, bf16[2,2,1,1,24,768]{5,4,1,0,3,2:T(8,128)(2,1)S(1)}, u32[]{:S(2)}, u32[]{:S(2)}) collective-permute-start(bf16[2,2,1,1,24,768]{5,4,1,0,3,2:T(8,128)(2,1)S(1)} %bitcast.208), channel_id=1, source_target_pairs={{0,1},{1,0},{2,3},{3,2},{4,5},{5,4},{6,7},{7,6},{8,9},{9,8},{10,11... | collective-permute-start | bytes 442376 | tf_op jit(solution)/shard_map/ppermute | solution.py:1391
  52.8 10.2 %collective-permute-start.16 = (bf16[2,2,1,1,24,896]{5,4,1,0,3,2:T(8,128)(2,1)S(1)}, bf16[2,2,1,1,24,896]{5,4,1,0,3,2:T(8,128)(2,1)S(1)}, u32[]{:S(2)}, u32[]{:S(2)}) collective-permute-start(bf16[2,2,1,1,24,896]{5,4,1,0,3,2:T(8,128)(2,1)S(1)} %bitcast.200), channel_id=1, source_target_pairs={{0,2},{1,3},{2,0},{3,1},{4,6},{5,7},{6,4},{7,5},{8,10},{9,11},{10,... | collective-permute-start | bytes 516104 | tf_op jit(solution)/shard_map/ppermute | solution.py:1391
  63.9 9.8 %collective-permute-start.20 = (bf16[2,2,2,1,24,896]{5,4,2,1,0,3:T(8,128)(2,1)S(1)}, bf16[2,2,2,1,24,896]{5,4,2,1,0,3:T(8,128)(2,1)S(1)}, u32[]{:S(2)}, u32[]{:S(2)}) collective-permute-start(bf16[2,2,2,1,24,896]{5,4,2,1,0,3:T(8,128)(2,1)S(1)} %bitcast.181), channel_id=1, source_target_pairs={{0,1},{1,0},{2,3},{3,2},{4,5},{5,4},{6,7},{7,6},{8,9},{9,8},{10,11... | collective-permute-start | bytes 1032200 | tf_op jit(solution)/shard_map/ppermute | solution.py:1391
  64.4 9.3 %collective-permute-start.19 = (bf16[2,2,1,2,24,768]{5,4,3,1,0,2:T(8,128)(2,1)}, bf16[2,2,1,2,24,768]{5,4,3,1,0,2:T(8,128)(2,1)}, u32[]{:S(2)}, u32[]{:S(2)}) collective-permute-start(bf16[2,2,1,2,24,768]{5,4,3,1,0,2:T(8,128)(2,1)} %bitcast.57), channel_id=1, source_target_pairs={{0,2},{1,3},{2,0},{3,1},{4,6},{5,7},{6,4},{7,5},{8,10},{9,11},{10,... | collective-permute-start | bytes 884744 | tf_op jit(solution)/shard_map/ppermute | solution.py:1391
  65.9 10.5 %collective-permute-start.23 = (f32[8,1536]{1,0:T(8,128)S(1)}, f32[8,1536]{1,0:T(8,128)}, u32[]{:S(2)}, u32[]{:S(2)}) collective-permute-start(f32[8,1536]{1,0:T(8,128)S(1)} %shard_map.310.refs_8_.refs_7_.refs_3_.refs_9_), channel_id=1, source_target_pairs={{0,16},{16,0},{1,17},{17,1},{2,18},{18,2},{3,19},{19,3},{4,20},{20... | collective-permute-start | bytes 147464 | tf_op jit(solution)/shard_map/ppermute | solution.py:1376
  66.0 23.5 %collective-permute-start.24 = (bf16[2,2,1,2,24,1920]{5,4,3,1,0,2:T(8,128)(2,1)S(1)}, bf16[2,2,1,2,24,1920]{5,4,3,1,0,2:T(8,128)(2,1)S(1)}, u32[]{:S(2)}, u32[]{:S(2)}) collective-permute-start(bf16[2,2,1,2,24,1920]{5,4,3,1,0,2:T(8,128)(2,1)S(1)} %bitcast.159), channel_id=1, source_target_pairs={{0,2},{1,3},{2,0},{3,1},{4,6},{5,7},{6,4},{7,5},{8,10},{9,11},{10,... | collective-permute-start | bytes 2211848 | tf_op jit(solution)/shard_map/ppermute | solution.py:1391
  66.5 23.0 %collective-permute-start.25 = (bf16[2,2,2,1,96,384]{5,4,2,1,0,3:T(8,128)(2,1)S(1)}, bf16[2,2,2,1,96,384]{5,4,2,1,0,3:T(8,128)(2,1)S(1)}, u32[]{:S(2)}, u32[]{:S(2)}) collective-permute-start(bf16[2,2,2,1,96,384]{5,4,2,1,0,3:T(8,128)(2,1)S(1)} %bitcast.165), channel_id=1, source_target_pairs={{0,1},{1,0},{2,3},{3,2},{4,5},{5,4},{6,7},{7,6},{8,9},{9,8},{10,11... | collective-permute-start | bytes 1769480 | tf_op jit(solution)/shard_map/ppermute | solution.py:1391
  134.6 16.1 %collective-permute-start.28 = (bf16[16,24,1536]{2,1,0:T(8,128)(2,1)}, bf16[16,24,1536]{2,1,0:T(8,128)(2,1)S(1)}, u32[]{:S(2)}, u32[]{:S(2)}) collective-permute-start(bf16[16,24,1536]{2,1,0:T(8,128)(2,1)} %get-tuple-element.240), channel_id=1, source_target_pairs={{0,16},{16,0},{1,17},{17,1},{2,18},{18,2},{3,19},{19,3},{4,20},{20... | collective-permute-start | bytes 3538952 | tf_op jit(solution)/shard_map/ppermute | solution.py:1376
  134.8 15.9 %collective-permute-start.29 = (bf16[512,384]{1,0:T(8,128)(2,1)S(1)}, bf16[512,384]{1,0:T(8,128)(2,1)S(1)}, u32[]{:S(2)}, u32[]{:S(2)}) collective-permute-start(bf16[512,384]{1,0:T(8,128)(2,1)S(1)} %copy-done.43), channel_id=1, source_target_pairs={{0,16},{16,0},{1,17},{17,1},{2,18},{18,2},{3,19},{19,3},{4,20},{20... | collective-permute-start | bytes 1179656 | tf_op jit(solution)/shard_map/ppermute | solution.py:1376
  159.4 18.8 %collective-permute-start.31 = (bf16[8,24,1536]{2,1,0:T(8,128)(2,1)S(1)}, bf16[8,24,1536]{2,1,0:T(8,128)(2,1)S(1)}, u32[]{:S(2)}, u32[]{:S(2)}) collective-permute-start(bf16[8,24,1536]{2,1,0:T(8,128)(2,1)S(1)} %bitcast.251), channel_id=1, source_target_pairs={{0,1},{1,0},{2,3},{3,2},{4,5},{5,4},{6,7},{7,6},{8,9},{9,8},{10,11... | collective-permute-start | bytes 1769480 | tf_op jit(solution)/shard_map/ppermute | solution.py:1391
  160.9 15.5 %collective-permute-start.32 = (bf16[8,24,1024]{2,1,0:T(8,128)(2,1)S(1)}, bf16[8,24,1024]{2,1,0:T(8,128)(2,1)S(1)}, u32[]{:S(2)}, u32[]{:S(2)}) collective-permute-start(bf16[8,24,1024]{2,1,0:T(8,128)(2,1)S(1)} %bitcast.252), channel_id=1, source_target_pairs={{0,2},{1,3},{2,0},{3,1},{4,6},{5,7},{6,4},{7,5},{8,10},{9,11},{10,... | collective-permute-start | bytes 1179656 | tf_op jit(solution)/shard_map/ppermute | solution.py:1391
  182.7 19.1 %collective-permute-start.34 = (bf16[4,24,1536]{2,1,0:T(8,128)(2,1)}, bf16[4,24,1536]{2,1,0:T(8,128)(2,1)S(1)}, u32[]{:S(2)}, u32[]{:S(2)}) collective-permute-start(bf16[4,24,1536]{2,1,0:T(8,128)(2,1)} %bitcast.83), channel_id=1, source_target_pairs={{0,2},{1,3},{2,0},{3,1},{4,6},{5,7},{6,4},{7,5},{8,10},{9,11},{10,... | collective-permute-start | bytes 884744 | tf_op jit(solution)/shard_map/ppermute | solution.py:1391
  184.5 17.3 %collective-permute-start.35 = (bf16[4,24,1024]{2,1,0:T(8,128)(2,1)}, bf16[4,24,1024]{2,1,0:T(8,128)(2,1)}, u32[]{:S(2)}, u32[]{:S(2)}) collective-permute-start(bf16[4,24,1024]{2,1,0:T(8,128)(2,1)} %bitcast.86), channel_id=1, source_target_pairs={{0,1},{1,0},{2,3},{3,2},{4,5},{5,4},{6,7},{7,6},{8,9},{9,8},{10,11... | collective-permute-start | bytes 589832 | tf_op jit(solution)/shard_map/ppermute | solution.py:1391
  185.0 20.5 %collective-permute-start.36 = (bf16[8,24,1536]{2,1,0:T(8,128)(2,1)}, bf16[8,24,1536]{2,1,0:T(8,128)(2,1)S(1)}, u32[]{:S(2)}, u32[]{:S(2)}) collective-permute-start(bf16[8,24,1536]{2,1,0:T(8,128)(2,1)} %bitcast.89), channel_id=1, source_target_pairs={{0,1},{1,0},{2,3},{3,2},{4,5},{5,4},{6,7},{7,6},{8,9},{9,8},{10,11... | collective-permute-start | bytes 1769480 | tf_op jit(solution)/shard_map/ppermute | solution.py:1391
  211.0 11.8 %collective-permute-start.38 = (bf16[8,24,1024]{2,1,0:T(8,128)(2,1)}, bf16[8,24,1024]{2,1,0:T(8,128)(2,1)S(1)}, u32[]{:S(2)}, u32[]{:S(2)}) collective-permute-start(bf16[8,24,1024]{2,1,0:T(8,128)(2,1)} %bitcast.102), channel_id=1, source_target_pairs={{0,1},{1,0},{2,3},{3,2},{4,5},{5,4},{6,7},{7,6},{8,9},{9,8},{10,11... | collective-permute-start | bytes 1179656 | tf_op jit(solution)/shard_map/ppermute | solution.py:1391
  211.3 11.4 %collective-permute-start.40 = (bf16[4,24,1536]{2,1,0:T(8,128)(2,1)}, bf16[4,24,1536]{2,1,0:T(8,128)(2,1)S(1)}, u32[]{:S(2)}, u32[]{:S(2)}) collective-permute-start(bf16[4,24,1536]{2,1,0:T(8,128)(2,1)} %bitcast.99), channel_id=1, source_target_pairs={{0,2},{1,3},{2,0},{3,1},{4,6},{5,7},{6,4},{7,5},{8,10},{9,11},{10,... | collective-permute-start | bytes 884744 | tf_op jit(solution)/shard_map/ppermute | solution.py:1391
  213.0 9.0 %collective-permute-start.39 = (bf16[2,24,2560]{2,1,0:T(8,128)(2,1)}, bf16[2,24,2560]{2,1,0:T(8,128)(2,1)S(1)}, u32[]{:S(2)}, u32[]{:S(2)}) collective-permute-start(bf16[2,24,2560]{2,1,0:T(8,128)(2,1)} %bitcast.96), channel_id=1, source_target_pairs={{0,4},{1,5},{2,6},{3,7},{4,0},{5,1},{6,2},{7,3},{8,12},{9,13},{10,... | collective-permute-start | bytes 737288 | tf_op jit(solution)/shard_map/ppermute | solution.py:1391
  222.8 22.3 %collective-permute-start.45 = (f32[512,384]{1,0:T(8,128)}, f32[512,384]{1,0:T(8,128)S(1)}, u32[]{:S(2)}, u32[]{:S(2)}) collective-permute-start(f32[512,384]{1,0:T(8,128)} %get-tuple-element.336), channel_id=1, source_target_pairs={{0,16},{16,0},{1,17},{17,1},{2,18},{18,2},{3,19},{19,3},{4,20},{20... | collective-permute-start | bytes 2359304 | tf_op jit(solution)/shard_map/ppermute | solution.py:1376
  233.7 8.8 %collective-permute-start.43 = (bf16[2,24,2560]{2,1,0:T(8,128)(2,1)S(1)}, bf16[2,24,2560]{2,1,0:T(8,128)(2,1)S(1)}, u32[]{:S(2)}, u32[]{:S(2)}) collective-permute-start(bf16[2,24,2560]{2,1,0:T(8,128)(2,1)S(1)} %bitcast.254), channel_id=1, source_target_pairs={{0,4},{1,5},{2,6},{3,7},{4,0},{5,1},{6,2},{7,3},{8,12},{9,13},{10,... | collective-permute-start | bytes 737288 | tf_op jit(solution)/shard_map/ppermute | solution.py:1391
  235.8 9.2 %collective-permute-start.46 = (bf16[8,2304]{1,0:T(8,128)(2,1)S(1)}, bf16[8,2304]{1,0:T(8,128)(2,1)S(1)}, u32[]{:S(2)}, u32[]{:S(2)}) collective-permute-start(bf16[8,2304]{1,0:T(8,128)(2,1)S(1)} %copy-done.45), channel_id=1, source_target_pairs={{0,16},{16,0},{1,17},{17,1},{2,18},{18,2},{3,19},{19,3},{4,20},{20... | collective-permute-start | bytes 110600 | tf_op jit(solution)/shard_map/ppermute | solution.py:1376
  245.0 14.3 %collective-permute-start.48 = (bf16[1,24,5120]{2,1,0:T(8,128)(2,1)S(1)}, bf16[1,24,5120]{2,1,0:T(8,128)(2,1)S(1)}, u32[]{:S(2)}, u32[]{:S(2)}) collective-permute-start(bf16[1,24,5120]{2,1,0:T(8,128)(2,1)S(1)} %bitcast.253), channel_id=1, source_target_pairs={{0,8},{1,9},{2,10},{3,11},{4,12},{5,13},{6,14},{7,15},{8,0},{9,1},... | collective-permute-start | bytes 737288 | tf_op jit(solution)/shard_map/ppermute | solution.py:1391
  (70 other events, 387.8 us)
Sparse Core Ops, SparseCore 0:
  135.3 64.5 all-gather.1

commit v3 on v2

--- a/solution.py
+++ b/solution.py
@@ -339,8 +339,6 @@
 
     for i in range(2):
         tile(i, 0)
-    if k.layer == 1:
-        k.sent[...] = jnp.where(k.section == 0, k.out[...].astype(f32), x[...].astype(f32)).astype(bf16)
 
 
 def ffn_backward_body(k):
@@ -348,8 +346,13 @@
     gmod[...] = jnp.zeros(gmod.shape, f32)
     gbu[...] = jnp.zeros(gbu.shape, f32)
     gbn[...] = jnp.zeros(gbn.shape, f32)
+    both_ways = k.layer == 1
     k.mods(), k.small()
-    x, grad, branch, down = k.x(), k.grad(), k.branch(), k.down()
+    x, grad = k.x(), k.grad()
+    if both_ways:
+        gated, wo = k.gated(), k.wo()
+    else:
+        branch, down = k.branch(), k.down()
 
     def tile(i, carry):
         start = i * HALF
@@ -360,22 +363,27 @@
             where = (pl.ds(slot, 1), slice((part - 2) * D, (part - 1) * D))
             gmod[where] = gmod[where] + jnp.sum(values, axis=0, keepdims=True)
 
-        grown = branch[rows, :]
+        grown = mm(gated[rows, :], wo[...]) if both_ways else branch[rows, :]
         middle = x[rows, :].astype(f32) + k.share(slot, 2) * grown
         normal, rate = normalise(middle)
         inner = (normal * (1.0 + k.share(slot, 4)) + k.share(slot, 3)).astype(bf16)
         k.inner_s[rows, :] = inner
+        up = mm(inner, k.wu()[...]) + k.bu()
+        square, tanh = gelu_parts(up)
+        half = 0.5 * (1.0 + tanh)
+        hidden = (up * half).astype(bf16)
+        k.hidden_s[rows, :] = hidden
+        lower = (mm(hidden, k.wn()[...]) if both_ways else down[rows, :]) + k.bn()
         live = (row_iota(HALF, 1) + start) < k.live_rows
+        if both_ways:
+            result = middle + k.share(slot, 5) * lower
+            k.out[rows, :] = jnp.where(live, result, 0.0).astype(bf16)
         above = jnp.where(live, grad[rows, :].astype(f32), 0.0)
-        add(5, above * (down[rows, :] + k.bn()))
+        add(5, above * lower)
         grad_down = above * k.share(slot, 5)
         gbn[...] = gbn[...] + jnp.sum(grad_down, axis=0, keepdims=True)
         down_low = grad_down.astype(bf16)
         k.down_s[rows, :] = down_low
-        up = mm(inner, k.wu()[...]) + k.bu()
-        square, tanh = gelu_parts(up)
-        half = 0.5 * (1.0 + tanh)
-        k.hidden_s[rows, :] = (up * half).astype(bf16)
         slope = half + 0.5 * up * (1.0 - tanh * tanh) * (
             GELU_A * (1.0 + 3.0 * GELU_B * square)
         )
@@ -398,6 +406,11 @@
         tile(i, 0)
     k.push("mid_grad")
     k.push("branch_low")
+    if both_ways:
+        own = k.section == 0
+        k.sent[...] = jnp.where(own, k.out[...].astype(f32), x[...].astype(f32)).astype(bf16)
+        k.push("out")
+        k.push("sent")
 
     def weights(j, carry):
         part = pl.ds(pl.multiple_of(j * HALF, HALF), HALF)
@@ -411,7 +424,7 @@
         devices, shard, _ = k.keep.shape
 
         def halves(j, carry):
-            for kept, own in ((k.keep, c_section), (k.sent, 1 - c_section)):
+            for kept, own in ((k.keep, c_section), (k.gone, 1 - c_section)):
                 columns = pl.ds(pl.multiple_of(j * HALF + own * (FF // 2), HALF), HALF)
                 here = pl.ds(pl.multiple_of(j * HALF, HALF), HALF)
                 part = mm(inner_t, k.up_s[:, columns]).reshape(devices, shard, HALF)
@@ -422,7 +435,7 @@
         lax.fori_loop(0, FF // 2 // HALF, halves, 0)
 
         def owner(r, carry):
-            for kept, own in ((k.keep, c_section), (k.sent, 1 - c_section)):
+            for kept, own in ((k.keep, c_section), (k.gone, 1 - c_section)):
                 for piece in range(2):
                     start = pl.multiple_of((4 * r + 2 * own + piece) * shard, 8)
                     rows = k.gwn[pl.ds(start, shard), :]
@@ -432,7 +445,7 @@
 
         lax.fori_loop(0, devices, owner, 0)
         k.push("keep")
-        k.push("sent")
+        k.push("gone")
     else:
         k.gwu[...] = mm(inner_t, k.up_s[...])
     gated = k.gated()
@@ -811,7 +824,6 @@
             out=((ROWS, D), bf16, True),
             branch=((ROWS, D), f32, True),
             down=((ROWS, D), f32, True),
-            **({"sent": ((ROWS, D), bf16, False)} if layer == 1 else {}),
         ),
         {},
         3 * 10**9,
@@ -826,7 +838,7 @@
     if in_kernel:
         sums = dict(
             keep=((devices, shard, FF), f32, True),
-            sent=((devices, shard, FF), bf16, False),
+            gone=((devices, shard, FF), bf16, False),
         )
     else:
         sums = dict(gwu=((D, FF), f32, False), gwn=((FF, D), f32, False))
@@ -838,14 +850,22 @@
             mods=own(mods),
             small=own(small),
             x=micro(x),
+            **(
+                dict(gated=plain(gated), wo=own(upo, AT_OUT))
+                if layer == 1
+                else dict(branch=plain(branch), down=plain(down_raw))
+            ),
             grad=micro(grad),
-            branch=plain(branch),
-            down=plain(down_raw),
             wu=own(upo, AT_UP),
             wn=own(down),
-            gated=plain(gated),
+            **(dict(gated=plain(gated)) if layer == 0 else {}),
         ),
         dict(
+            **(
+                dict(out=((ROWS, D), bf16, True), sent=((ROWS, D), bf16, False))
+                if layer == 1
+                else {}
+            ),
             mid_grad=((ROWS, D), f32, True),
             branch_low=((ROWS, D), bf16, True),
             gwo=((D, D), f32, True),
@@ -969,10 +989,10 @@
 
 def pack_kernel(
     w_query, w_key, w_value, w_gate, w_out, w_decay, w_up, w_down, w_ada, conditions,
-    qk, vgd, upo, down, ada, lifted,
+    qkuo, vgd, down, ada, lifted,
 ):
-    qk[:, :D] = w_query[0]
-    qk[:, D:] = w_key[0]
+    qkuo[:, :D] = w_query[0]
+    qkuo[:, D : 2 * D] = w_key[0]
     vgd[:, :D] = w_value[0]
     vgd[:, D : 2 * D] = w_gate[0]
     place = jnp.where(row_iota(HEADS, LANES) == lane_iota(HEADS, LANES), 1.0, 0.0).astype(bf16)
@@ -980,8 +1000,8 @@
         w_decay[0], place, (((0,), (0,)), ((), ())), preferred_element_type=f32
     )
     vgd[:, 2 * D :] = turned.astype(bf16)
-    upo[:, :FF] = w_up[0]
-    upo[:, FF:] = w_out[0]
+    qkuo[:, 2 * D : 2 * D + FF] = w_up[0]
+    qkuo[:, 2 * D + FF :] = w_out[0]
     down[...] = w_down[0]
     ada[...] = w_ada[0]
     values = jnp.concatenate([conditions[m].astype(f32) for m in range(MICRO)], axis=0)
@@ -990,14 +1010,13 @@
 
 def pack(*weights):
     shard = weights[0].shape[1]
-    shapes = [(shard, width) for width in (2 * D, 2 * D + LANES, FF + D)]
+    shapes = [(shard, width) for width in (3 * D + FF, 2 * D + LANES)]
     shapes += [weights[7].shape[1:], weights[8].shape[1:], (1, MICRO * SLOTS, D)]
     return pl.pallas_call(
         pack_kernel,
         out_shape=[jax.ShapeDtypeStruct(shape, bf16) for shape in shapes],
         in_specs=[VMEM] * len(weights),
         out_specs=[VMEM] * len(shapes),
-        compiler_params=pltpu.CompilerParams(vmem_limit_bytes=8 * 1024 * 1024),
     )(*weights)
 
 
@@ -1433,7 +1452,7 @@
     def both(values):
         return values, swap(values)
 
-    qk, vgd, upo, down, ada, lifted = pack(
+    qkuo, vgd, down, ada, lifted = pack(
         w_query, w_key, w_value, w_gate, w_out, w_decay.transpose(0, 2, 1), w_up, w_down, w_ada,
         conditions,
     )
@@ -1443,10 +1462,13 @@
     lag = len(along_z)
     plane = along_x + along_y
     bounds = [len(plane) * i // lag for i in range(lag + 1)]
-    held = [single(array) for array in (qk, vgd, upo, down)]
+    held = [single(array) for array in (qkuo, vgd, down)]
     ada = single(ada)
     for place, pair in enumerate(steps):
-        bits = pair + pair
+        bits = pair + pair[1:]
+        if place == len(steps) - 1:
+            bits = pair + pair
+            held = [held[0][..., : 2 * D], held[1], held[0][..., 2 * D :], held[2]]
         came = [partner(array, bit) for array, bit in zip(held, bits)]
         after = ()
         if place < lag:
@@ -1476,26 +1498,21 @@
             *saved, gated = attn_forward(0, layouts, x, mods, smalls, qk, vgd)
             held = join(held[2:], came[2:], bits[2:], (gated,))
     upo, down = [both(flat(array)) for array in held]
-    kept = []
-    acts = []
-    for l in range(2):
-        if l:
-            *saved, gated = attn_forward(l, layouts, x, mods, smalls, qk, vgd)
-        out, branch, down_raw, *acts_sent = ffn_forward(
-            l, layouts, x, mods, smalls, gated, upo, down
-        )
-        kept.append((x, saved, gated, branch, down_raw))
-        acts.append(out)
-        x = out[None]
-
-    late, _ = lock(w_ada[0], acts[0])
+    out_one, branch, down_raw = ffn_forward(0, layouts, x, mods, smalls, gated, upo, down)
+    kept = [(x, saved, gated, branch, down_raw)]
+    x = out_one[None]
+    *saved, gated = attn_forward(1, layouts, x, mods, smalls, qk, vgd)
+    kept.append((x, saved, gated, None, None))
+
+    late, _ = lock(w_ada[0], out_one)
     ada_all = lax.all_gather(late, "row", axis=0, tiled=True)
 
     def ffn_step(l, grad, after=()):
         x, saved, gated, branch, down_raw = kept[l]
-        mid_grad, branch_low, gwo, sums, *terms = ffn_backward(
+        results = ffn_backward(
             l, layouts, x, mods, smalls, gated, branch, down_raw, grad, upo, down, devices, after
         )
+        acts, (mid_grad, branch_low, gwo, sums, *terms) = results[: 2 * l], results[2 * l :]
         if terms[0].ndim == 2:
             up_sum = terms[0].reshape(devices, shard, 2, FF // 2)
             down_sum = terms[1].reshape(devices, 2, 2, shard, D)
@@ -1507,7 +1524,7 @@
                     jnp.concatenate([up_half, down_half[:, 0], down_half[:, 1]], axis=2)
                 )
             terms[1] = terms[1].astype(bf16)
-        return [branch_low, gwo], mid_grad, terms[0], terms[1], sums
+        return [branch_low, gwo], mid_grad, terms[0], terms[1], sums, *acts
 
     def mixer_step(l, carried, after=()):
         low, keep, sent, sums = mixer_backward(
@@ -1534,8 +1551,8 @@
         return mod
 
     x_bits, y_bits, z_bits = along_x, along_y, along_z
-    carried, mid_grad, f2_keep, f2_sent, f2_sums = ffn_step(1, output_grad)
-    *carried, f2_sent, acts_sent = lock(*carried, f2_sent, acts_sent[0])
+    carried, mid_grad, f2_keep, f2_sent, f2_sums, out_two, acts_sent = ffn_step(1, output_grad)
+    *carried, f2_sent, acts_sent = lock(*carried, f2_sent, acts_sent)
     f2_came = swap(f2_sent)
     acts_came = swap(acts_sent)
     low, a2_keep, a2_sent, m2_sums = mixer_step(1, carried)
@@ -1600,7 +1617,7 @@
     last = (1 << x_bits[-1], 1 << y_bits[-1])
     parts = [misc] + [across(misc, flips) for flips in (last[0], last[1], last[0] + last[1])]
     gx_out, gx_mark = both_micros(gx_one, gx_two, gx_came)
-    acts_out, acts_mark = both_micros(acts[0], acts[1], acts_came)
+    acts_out, acts_mark = both_micros(out_one, out_two, acts_came)
     grad_lifted = lifted_grads(mod_mine, mod_came, ada_all)
     lifted_came = swap(grad_lifted)
     mine, other, small_mine, small_other = finish(

time: 274 us -> 261 us (0.953)
  Pallas kernels: 126 us -> 121 us
  starting transfers between devices: 53.2 us -> 49.1 us
  local copies, waits for them, and re-layouts: 19.4 us -> 15.8 us
    pallas_call x10 -> x9, Pallas kernels: 102 us -> 95.4 us  [call(): pl.pallas_call(kernel, out_shape=[jax.ShapeDtypeStruct(shape, kind) for s...]
    ppermute x38 -> x35, starting transfers between devices: 50.5 us -> 46.4 us  [across(): return lax.ppermute(values, 'row', [(i, i ^ flips) for i in range(size)])]
    unnamed x97 -> x87, local copies, waits for them, and re-layouts: 19.3 us -> 15.6 us
    ppermute x38 -> x35, waiting for transfers between devices: 47.8 us -> 47.7 us  [across(): return lax.ppermute(values, 'row', [(i, i ^ flips) for i in range(size)])]
  transfers between devices with their start and end apart: 55 -> 52, of which waited for: 20 -> 17; matrix products, arithmetic and copies ran while one was open for 1% -> 1% of each run, Pallas kernels for 32% -> 33%
where the time goes in v3:
time: 261 us; the launch traced here: 258 us
  Pallas kernels  121 us (46%)
  waiting for transfers between devices  55.8 us (21%)
  starting transfers between devices  49.1 us (19%)
  local copies, waits for them, and re-layouts  15.8 us (6%)
  between operations  15.1 us (6%)
    pallas_call x9, Pallas kernels, call(): pl.pallas_call(kernel, out_shape=[jax.ShapeDtypeStruct(shape, kind) for s...  95.4 us
    ppermute x35, waiting for transfers between devices, across(): return lax.ppermute(values, 'row', [(i, i ^ flips) for i in range(size)])  47.7 us
    ppermute x35, starting transfers between devices, across(): return lax.ppermute(values, 'row', [(i, i ^ flips) for i in range(size)])  46.4 us
    unnamed x87, local copies, waits for them, and re-layouts  15.6 us
    pallas_call x11, Pallas kernels, step(): pl.pallas_call(functools.partial(step_kernel, bit, widths, [count for _,...  14.9 us
    ppermute x16, waiting for transfers between devices, swap(): return lax.ppermute(values, 'section', [(0, 1), (1, 0)])  8.07 us
  transfers between devices with their start and end apart: 52, of which 17 were waited for; matrix products, arithmetic and copies ran while one was open for 1% of the time, Pallas kernels for 33%

profile of v3, /device:TPU:0, one launch (start us, length us, event | category | flops | bytes accessed | tf_op | source)
XLA Modules:
  0.0 257.5 jit_solution(3332173137703655283)
XLA Ops:
  7.2 1.9 shard_map.305
  9.1 4.0 %collective-permute-start = (bf16[1,4,384]{2,1,0:T(4,128)(2,1)}, bf16[1,4,384]{2,1,0:T(4,128)(2,1)S(1)}, u32[]{:S(2)}, u32[]{:S(2)}) collective-permute-start(bf16[1,4,384]{2,1,0:T(4,128)(2,1)} %get-tuple-element.187), channel_id=1, source_target_pairs={{0,8},{1,9},{2,10},{3,11},{4,12},{5,13},{6,14},{7,15},{8,0},{9,1},... | collective-permute-start | bytes 9224 | tf_op jit(solution)/shard_map/ppermute | solution.py:1410
  15.0 2.6 %collective-permute-start.9 = (bf16[1,1,1,1,96,384]{5,4,3,2,1,0:T(8,128)(2,1)}, bf16[1,1,1,1,96,384]{5,4,3,2,1,0:T(8,128)(2,1)S(1)}, u32[]{:S(2)}, u32[]{:S(2)}) collective-permute-start(bf16[1,1,1,1,96,384]{5,4,3,2,1,0:T(8,128)(2,1)} %bitcast.206), channel_id=1, source_target_pairs={{0,8},{1,9},{2,10},{3,11},{4,12},{5,13},{6,14},{7,15},{8,0},{9,1},... | collective-permute-start | bytes 221192 | tf_op jit(solution)/shard_map/ppermute | solution.py:1410
  22.3 5.9 %collective-permute-done.8 = bf16[1,1,1,1,24,896]{5,4,3,2,1,0:T(8,128)(2,1)S(1)} collective-permute-done((bf16[1,1,1,1,24,896]{5,4,3,2,1,0:T(8,128)(2,1)}, bf16[1,1,1,1,24,896]{5,4,3,2,1,0:T(8,128)(2,1)S(1)}, u32[]{:S(2)}, u32[]{:S(2)}) %collective-permute-start.8) | collective-permute-done | bytes 43040 | tf_op jit(solution)/shard_map/ppermute | solution.py:1410
  32.5 1.9 collective-permute-start.12
  34.5 1.9 collective-permute-start.11
  36.4 5.7 %collective-permute-done.1 = bf16[2,4,384]{2,1,0:T(4,128)(2,1)S(1)} collective-permute-done((bf16[2,4,384]{2,1,0:T(4,128)(2,1)S(1)}, bf16[2,4,384]{2,1,0:T(4,128)(2,1)S(1)}, u32[]{:S(2)}, u32[]{:S(2)}) %collective-permute-start.1) | collective-permute-done | bytes 6176 | tf_op jit(solution)/shard_map/ppermute | solution.py:1410
  46.4 4.1 %collective-permute-done.4 = f32[2,4,2304]{2,1,0:T(4,128)S(1)} collective-permute-done((f32[2,4,2304]{2,1,0:T(4,128)S(1)}, f32[2,4,2304]{2,1,0:T(4,128)S(1)}, u32[]{:S(2)}, u32[]{:S(2)}) %collective-permute-start.4) | collective-permute-done | bytes 73760 | tf_op jit(solution)/shard_map/ppermute | solution.py:1410
  51.8 3.8 %collective-permute-done.5.refs_6_ = f32[1,4,2304]{2,1,0:T(4,128)S(1)} collective-permute-done((f32[1,4,2304]{2,1,0:T(4,128)S(1)}, f32[1,4,2304]{2,1,0:T(4,128)S(1)}, u32[]{:S(2)}, u32[]{:S(2)}) %collective-permute-start.5) | collective-permute-done | bytes 36896 | tf_op jit(solution)/shard_map/ppermute | solution.py:1410
  61.8 6.3 %collective-permute-done.16 = bf16[2,2,1,2,24,768]{5,4,3,1,0,2:T(8,128)(2,1)} collective-permute-done((bf16[2,2,1,2,24,768]{5,4,3,1,0,2:T(8,128)(2,1)S(1)}, bf16[2,2,1,2,24,768]{5,4,3,1,0,2:T(8,128)(2,1)}, u32[]{:S(2)}, u32[]{:S(2)}) %collective-permute-start.16) | collective-permute-done | bytes 294944 | tf_op jit(solution)/shard_map/ppermute | solution.py:1410
  68.0 2.3 shard_map.314
  73.7 9.2 %shard_map.315 = (bf16[512,384]{1,0:T(8,128)(2,1)}, f32[512,1536]{1,0:T(8,128)}, f32[512,128]{1,0:T(8,128)}, f32[512,384]{1,0:T(8,128)}, f32[512,128]{1,0:T(8,12...) custom-call(s32[2,1]{1,0:T(2,128)} %copy.37.refs_0_, bf16[2,512,384]{2,1,0:T(8,128)(2,1)} %refs_6_.1, ...), custom_call_target="tpu_custom_call" | custom-call | flops 4000000000 | bytes 4194304 | tf_op jit(solution)/shard_map/pallas_call | solution.py:748
  84.8 4.4 %collective-permute-done.24.refs_12_.refs_13_ = bf16[1536,384]{1,0:T(8,128)(2,1)S(1)} collective-permute-done((bf16[1536,384]{1,0:T(8,128)(2,1)S(1)}, bf16[1536,384]{1,0:T(8,128)(2,1)S(1)}, u32[]{:S(2)}, u32[]{:S(2)}) %collective-permute-start.24) | collective-permute-done | bytes 1179680 | tf_op jit(solution)/shard_map/ppermute | solution.py:1395
  91.3 6.5 %shard_map.317 = (bf16[512,384]{1,0:T(8,128)(2,1)}, f32[512,384]{1,0:T(8,128)}, f32[512,384]{1,0:T(8,128)}) custom-call(s32[2,1]{1,0:T(2,128)} %copy.37.refs_0_, bf16[512,384]{1,0:T(8,128)(2,1)} %get-tuple-element.206.refs_4_.refs_1_.refs_13_, bf16[2,512,384]{2,1,0:T(8,128)(2,1)} %refs_6_.1, bf16[384,1920]{1,0:T(8,128)(2,1)} %bitcast.215, ...), custom_call_target="tpu_custom_call" | custom-call | flops 3000000000 | bytes 4194304 | tf_op jit(solution)/shard_map/pallas_call | solution.py:748
  97.9 9.8 %shard_map.318 = (bf16[512,384]{1,0:T(8,128)(2,1)}, f32[512,1536]{1,0:T(8,128)}, f32[512,128]{1,0:T(8,128)}, f32[512,384]{1,0:T(8,128)}, f32[512,128]{1,0:T(8,12...) custom-call(s32[2,1]{1,0:T(2,128)} %copy.37.refs_0_, bf16[1,512,384]{2,1,0:T(8,128)(2,1)} %bitcast.164, ...), custom_call_target="tpu_custom_call" | custom-call | flops 4000000000 | bytes 4194304 | tf_op jit(solution)/shard_map/pallas_call | solution.py:748
  107.7 13.9 %shard_map.319 = (bf16[512,384]{1,0:T(8,128)(2,1)}, bf16[512,384]{1,0:T(8,128)(2,1)}, f32[512,384]{1,0:T(8,128)}, bf16[512,384]{1,0:T(8,128)(2,1)}, f32[384,384]...) custom-call(s32[2,1]{1,0:T(2,128)} %copy.37.refs_0_, ...), custom_call_target="tpu_custom_call" | custom-call | flops 5000000000 | bytes 4194304 | tf_op jit(solution)/shard_map/pallas_call | solution.py:748
  122.2 15.4 %shard_map.320 = (bf16[512,1664]{1,0:T(8,128)(2,1)}, f32[384,1024]{1,0:T(8,128)}, bf16[384,1024]{1,0:T(8,128)(2,1)}, f32[8,384]{1,0:T(8,128)}) custom-call(s32[2,1]{1,0:T(2,128)} %copy.37.refs_0_, bf16[512,384]{1,0:T(8,128)(2,1)} %get-tuple-element.217.refs_1_, bf16[384,1920]{1,0:T(8,128)(2,1)} %bitcast.219, bf16[384,1920]{1,0:T(8,128)(2,1)} %copy-done.36, ...), custom_call_target="tpu_custom_call" | custom-call | flops 7000000000 | bytes 4194304 | tf_op jit(solution)/shard_map/pallas_call | solution.py:748
  138.9 6.4 %shard_map.322 = (f32[512,384]{1,0:T(8,128)}, bf16[512,384]{1,0:T(8,128)(2,1)}, bf16[8,2304]{1,0:T(8,128)(2,1)}, f32[8,768]{1,0:T(8,128)}) custom-call(s32[2,1]{1,0:T(2,128)} %copy.37.refs_0_, bf16[512,1664]{1,0:T(8,128)(2,1)} %get-tuple-element.234.refs_1_, bf16[384,768]{1,0:T(8,128)(2,1)} %bitcast.52.refs_4_.refs_2_, ...), custom_call_target="tpu_custom_call" | custom-call | flops 2000000000 | bytes 4194304 | tf_op jit(solution)/shard_map/pallas_call | solution.py:748
  147.1 2.6 %collective-permute-start.29 = (bf16[8,24,1024]{2,1,0:T(8,128)(2,1)S(1)}, bf16[8,24,1024]{2,1,0:T(8,128)(2,1)S(1)}, u32[]{:S(2)}, u32[]{:S(2)}) collective-permute-start(bf16[8,24,1024]{2,1,0:T(8,128)(2,1)S(1)} %bitcast.227), channel_id=1, source_target_pairs={{0,2},{1,3},{2,0},{3,1},{4,6},{5,7},{6,4},{7,5},{8,10},{9,11},{10,... | collective-permute-start | bytes 1179656 | tf_op jit(solution)/shard_map/ppermute | solution.py:1410
  149.7 13.0 %shard_map.325 = (f32[512,384]{1,0:T(8,128)}, bf16[512,384]{1,0:T(8,128)(2,1)}, f32[384,384]{1,0:T(8,128)}, f32[8,1536]{1,0:T(8,128)}, f32[16,24,1536]{2,1,0:T(8,128)}, /*index=5*/bf16[16,24,1536]{2,1,0:T(8,128)(2,1)}) custom-call(s32[2,1]{1,0:T(2,128)} %copy.37.refs_0_, f32[4,2304]{1,0:T(4,128)} %copy-done.33, f32[4,2304]{1,0:T(4,128)} %copy-done.39, ...), custom_call_target="tpu_custom_call" | custom-call | flops 5000000000 | bytes 4194304 | tf_op jit(solution)/shard_map/pallas_call | solution.py:748
  162.8 2.4 collective-permute-done.28
  173.4 15.2 %shard_map.329 = (bf16[512,1664]{1,0:T(8,128)(2,1)}, f32[384,1024]{1,0:T(8,128)}, bf16[384,1024]{1,0:T(8,128)(2,1)}, f32[8,384]{1,0:T(8,128)}) custom-call(s32[2,1]{1,0:T(2,128)} %copy.37.refs_0_, bf16[512,384]{1,0:T(8,128)(2,1)} %get-tuple-element.264.refs_1_, bf16[384,1920]{1,0:T(8,128)(2,1)} %bitcast.221, bf16[384,1920]{1,0:T(8,128)(2,1)} %copy-done.36, ...), custom_call_target="tpu_custom_call" | custom-call | flops 7000000000 | bytes 4194304 | tf_op jit(solution)/shard_map/pallas_call | solution.py:748
  188.6 3.8 %collective-permute-done.32 = bf16[4,24,1024]{2,1,0:T(8,128)(2,1)} collective-permute-done((bf16[4,24,1024]{2,1,0:T(8,128)(2,1)}, bf16[4,24,1024]{2,1,0:T(8,128)(2,1)}, u32[]{:S(2)}, u32[]{:S(2)}) %collective-permute-start.32) | collective-permute-done | bytes 196640 | tf_op jit(solution)/shard_map/ppermute | solution.py:1410
  194.2 2.2 shard_map.330
  202.2 5.8 %shard_map.333 = (f32[512,384]{1,0:T(8,128)}, bf16[512,384]{1,0:T(8,128)(2,1)}, bf16[8,2304]{1,0:T(8,128)(2,1)}, f32[8,768]{1,0:T(8,128)}, f32[512,384]{1,0:T(8,...) custom-call(s32[2,1]{1,0:T(2,128)} %copy.37.refs_0_, bf16[512,1664]{1,0:T(8,128)(2,1)} %get-tuple-element.291.refs_1_, ...), custom_call_target="tpu_custom_call" | custom-call | flops 2000000000 | bytes 4194304 | tf_op jit(solution)/shard_map/pallas_call | solution.py:748
  212.7 2.4 collective-permute-start.39
  215.1 4.5 %collective-permute-done.39.arrived = bf16[48,768]{1,0:T(8,128)(2,1)S(1)} collective-permute-done((bf16[48,768]{1,0:T(8,128)(2,1)S(1)}, bf16[48,768]{1,0:T(8,128)(2,1)S(1)}, u32[]{:S(2)}, u32[]{:S(2)}) %collective-permute-start.39) | collective-permute-done | bytes 73760 | tf_op jit(solution)/shard_map/ppermute | solution.py:1410
  223.4 6.7 %collective-permute-done.41.arrived = bf16[64,768]{1,0:T(8,128)(2,1)S(1)} collective-permute-done((bf16[64,768]{1,0:T(8,128)(2,1)S(1)}, bf16[64,768]{1,0:T(8,128)(2,1)S(1)}, u32[]{:S(2)}, u32[]{:S(2)}) %collective-permute-start.41) | collective-permute-done | bytes 98336 | tf_op jit(solution)/shard_map/ppermute | solution.py:1410
  230.2 2.4 shard_map.338
  232.7 3.4 %collective-permute-start.45 = (bf16[1,24,5120]{2,1,0:T(8,128)(2,1)S(1)}, bf16[1,24,5120]{2,1,0:T(8,128)(2,1)S(1)}, u32[]{:S(2)}, u32[]{:S(2)}) collective-permute-start(bf16[1,24,5120]{2,1,0:T(8,128)(2,1)S(1)} %bitcast.228), channel_id=1, source_target_pairs={{0,8},{1,9},{2,10},{3,11},{4,12},{5,13},{6,14},{7,15},{8,0},{9,1},... | collective-permute-start | bytes 737288 | tf_op jit(solution)/shard_map/ppermute | solution.py:1410
  237.0 2.6 %collective-permute-start.48 = (bf16[96,768]{1,0:T(8,128)(2,1)S(1)}, bf16[96,768]{1,0:T(8,128)(2,1)S(1)}, u32[]{:S(2)}, u32[]{:S(2)}) collective-permute-start(bf16[96,768]{1,0:T(8,128)(2,1)S(1)} %shard_map.339.refs_5_), channel_id=1, source_target_pairs={{0,3},{1,2},{2,1},{3,0},{4,7},{5,6},{6,5},{7,4},{8,11},{9,10},{10,... | collective-permute-start | bytes 442376 | tf_op jit(solution)/shard_map/ppermute | solution.py:1410
  244.3 2.7 %collective-permute-done.45.refs_4_ = bf16[1,24,5120]{2,1,0:T(8,128)(2,1)S(1)} collective-permute-done((bf16[1,24,5120]{2,1,0:T(8,128)(2,1)S(1)}, bf16[1,24,5120]{2,1,0:T(8,128)(2,1)S(1)}, u32[]{:S(2)}, u32[]{:S(2)}) %collective-permute-start.45) | collective-permute-done | bytes 245792 | tf_op jit(solution)/shard_map/ppermute | solution.py:1410
  (211 shorter events, 66.4 us)
Async XLA Ops:
  7.2 181.4 %all-gather.2.cloned.1.call-start = ((), (), s32[]{:S(2)}) async-start(), calls=%async_computation | async-start | bytes 1880064 | tf_op jit(solution)/shard_map/all_gather | solution.py:1508
  9.1 12.2 %collective-permute-start = (bf16[1,4,384]{2,1,0:T(4,128)(2,1)}, bf16[1,4,384]{2,1,0:T(4,128)(2,1)S(1)}, u32[]{:S(2)}, u32[]{:S(2)}) collective-permute-start(bf16[1,4,384]{2,1,0:T(4,128)(2,1)} %get-tuple-element.187), channel_id=1, source_target_pairs={{0,8},{1,9},{2,10},{3,11},{4,12},{5,13},{6,14},{7,15},{8,0},{9,1},... | collective-permute-start | bytes 9224 | tf_op jit(solution)/shard_map/ppermute | solution.py:1410
  14.7 13.5 %collective-permute-start.7 = (bf16[1,1,1,1,24,2688]{5,4,3,2,1,0:T(8,128)(2,1)}, bf16[1,1,1,1,24,2688]{5,4,3,2,1,0:T(8,128)(2,1)S(1)}, u32[]{:S(2)}, u32[]{:S(2)}) collective-permute-start(bf16[1,1,1,1,24,2688]{5,4,3,2,1,0:T(8,128)(2,1)} %bitcast.195), channel_id=1, source_target_pairs={{0,8},{1,9},{2,10},{3,11},{4,12},{5,13},{6,14},{7,15},{8,0},{9,1},... | collective-permute-start | bytes 387080 | tf_op jit(solution)/shard_map/ppermute | solution.py:1410
  15.0 13.2 %collective-permute-start.9 = (bf16[1,1,1,1,96,384]{5,4,3,2,1,0:T(8,128)(2,1)}, bf16[1,1,1,1,96,384]{5,4,3,2,1,0:T(8,128)(2,1)S(1)}, u32[]{:S(2)}, u32[]{:S(2)}) collective-permute-start(bf16[1,1,1,1,96,384]{5,4,3,2,1,0:T(8,128)(2,1)} %bitcast.206), channel_id=1, source_target_pairs={{0,8},{1,9},{2,10},{3,11},{4,12},{5,13},{6,14},{7,15},{8,0},{9,1},... | collective-permute-start | bytes 221192 | tf_op jit(solution)/shard_map/ppermute | solution.py:1410
  17.6 10.6 %collective-permute-start.8 = (bf16[1,1,1,1,24,896]{5,4,3,2,1,0:T(8,128)(2,1)}, bf16[1,1,1,1,24,896]{5,4,3,2,1,0:T(8,128)(2,1)S(1)}, u32[]{:S(2)}, u32[]{:S(2)}) collective-permute-start(bf16[1,1,1,1,24,896]{5,4,3,2,1,0:T(8,128)(2,1)} %bitcast.211), channel_id=1, source_target_pairs={{0,8},{1,9},{2,10},{3,11},{4,12},{5,13},{6,14},{7,15},{8,0},{9,1},... | collective-permute-start | bytes 129032 | tf_op jit(solution)/shard_map/ppermute | solution.py:1410
  30.8 12.3 %collective-permute-start.10 = (bf16[2,1,1,1,24,2688]{5,4,0,3,2,1:T(8,128)(2,1)S(1)}, bf16[2,1,1,1,24,2688]{5,4,0,3,2,1:T(8,128)(2,1)S(1)}, u32[]{:S(2)}, u32[]{:S(2)}) collective-permute-start(bf16[2,1,1,1,24,2688]{5,4,0,3,2,1:T(8,128)(2,1)S(1)} %bitcast.178), channel_id=1, source_target_pairs={{0,4},{1,5},{2,6},{3,7},{4,0},{5,1},{6,2},{7,3},{8,12},{9,13},{10,... | collective-permute-start | bytes 774152 | tf_op jit(solution)/shard_map/ppermute | solution.py:1410
  30.9 11.3 %collective-permute-start.3 = (bf16[1,1,1,2,24,2304]{5,4,3,2,1,0:T(8,128)(2,1)S(1)}, bf16[1,1,1,2,24,2304]{5,4,3,2,1,0:T(8,128)(2,1)S(1)}, u32[]{:S(2)}, u32[]{:S(2)}) collective-permute-start(bf16[1,1,1,2,24,2304]{5,4,3,2,1,0:T(8,128)(2,1)S(1)} %bitcast.138), channel_id=1, source_target_pairs={{0,2},{1,3},{2,0},{3,1},{4,6},{5,7},{6,4},{7,5},{8,10},{9,11},{10,... | collective-permute-start | bytes 663560 | tf_op jit(solution)/shard_map/ppermute | solution.py:1410
  32.5 10.6 %collective-permute-start.12 = (bf16[2,1,1,1,96,384]{5,4,0,3,2,1:T(8,128)(2,1)S(1)}, bf16[2,1,1,1,96,384]{5,4,0,3,2,1:T(8,128)(2,1)S(1)}, u32[]{:S(2)}, u32[]{:S(2)}) collective-permute-start(bf16[2,1,1,1,96,384]{5,4,0,3,2,1:T(8,128)(2,1)S(1)} %bitcast.190), channel_id=1, source_target_pairs={{0,4},{1,5},{2,6},{3,7},{4,0},{5,1},{6,2},{7,3},{8,12},{9,13},{10,... | collective-permute-start | bytes 442376 | tf_op jit(solution)/shard_map/ppermute | solution.py:1410
  34.5 8.6 %collective-permute-start.11 = (bf16[2,1,1,1,24,896]{5,4,0,3,2,1:T(8,128)(2,1)S(1)}, bf16[2,1,1,1,24,896]{5,4,0,3,2,1:T(8,128)(2,1)S(1)}, u32[]{:S(2)}, u32[]{:S(2)}) collective-permute-start(bf16[2,1,1,1,24,896]{5,4,0,3,2,1:T(8,128)(2,1)S(1)} %bitcast.203), channel_id=1, source_target_pairs={{0,4},{1,5},{2,6},{3,7},{4,0},{5,1},{6,2},{7,3},{8,12},{9,13},{10,... | collective-permute-start | bytes 258056 | tf_op jit(solution)/shard_map/ppermute | solution.py:1410
  43.2 12.4 %collective-permute-start.13 = (bf16[2,2,1,1,24,2688]{5,4,1,0,3,2:T(8,128)(2,1)S(1)}, bf16[2,2,1,1,24,2688]{5,4,1,0,3,2:T(8,128)(2,1)S(1)}, u32[]{:S(2)}, u32[]{:S(2)}) collective-permute-start(bf16[2,2,1,1,24,2688]{5,4,1,0,3,2:T(8,128)(2,1)S(1)} %bitcast.161), channel_id=1, source_target_pairs={{0,1},{1,0},{2,3},{3,2},{4,5},{5,4},{6,7},{7,6},{8,9},{9,8},{10,11... | collective-permute-start | bytes 1548296 | tf_op jit(solution)/shard_map/ppermute | solution.py:1410
  43.8 11.8 %collective-permute-start.15 = (bf16[2,2,1,1,96,384]{5,4,1,0,3,2:T(8,128)(2,1)S(1)}, bf16[2,2,1,1,96,384]{5,4,1,0,3,2:T(8,128)(2,1)S(1)}, u32[]{:S(2)}, u32[]{:S(2)}) collective-permute-start(bf16[2,2,1,1,96,384]{5,4,1,0,3,2:T(8,128)(2,1)S(1)} %bitcast.172), channel_id=1, source_target_pairs={{0,2},{1,3},{2,0},{3,1},{4,6},{5,7},{6,4},{7,5},{8,10},{9,11},{10,... | collective-permute-start | bytes 884744 | tf_op jit(solution)/shard_map/ppermute | solution.py:1410
  45.4 10.2 %collective-permute-start.14 = (bf16[2,2,1,1,24,896]{5,4,1,0,3,2:T(8,128)(2,1)S(1)}, bf16[2,2,1,1,24,896]{5,4,1,0,3,2:T(8,128)(2,1)S(1)}, u32[]{:S(2)}, u32[]{:S(2)}) collective-permute-start(bf16[2,2,1,1,24,896]{5,4,1,0,3,2:T(8,128)(2,1)S(1)} %bitcast.187), channel_id=1, source_target_pairs={{0,2},{1,3},{2,0},{3,1},{4,6},{5,7},{6,4},{7,5},{8,10},{9,11},{10,... | collective-permute-start | bytes 516104 | tf_op jit(solution)/shard_map/ppermute | solution.py:1410
  57.4 10.6 %collective-permute-start.17 = (bf16[2,2,2,1,24,896]{5,4,2,1,0,3:T(8,128)(2,1)}, bf16[2,2,2,1,24,896]{5,4,2,1,0,3:T(8,128)(2,1)}, u32[]{:S(2)}, u32[]{:S(2)}) collective-permute-start(bf16[2,2,2,1,24,896]{5,4,2,1,0,3:T(8,128)(2,1)} %bitcast.50), channel_id=1, source_target_pairs={{0,1},{1,0},{2,3},{3,2},{4,5},{5,4},{6,7},{7,6},{8,9},{9,8},{10,11... | collective-permute-start | bytes 1032200 | tf_op jit(solution)/shard_map/ppermute | solution.py:1410
  59.2 8.8 %collective-permute-start.16 = (bf16[2,2,1,2,24,768]{5,4,3,1,0,2:T(8,128)(2,1)S(1)}, bf16[2,2,1,2,24,768]{5,4,3,1,0,2:T(8,128)(2,1)}, u32[]{:S(2)}, u32[]{:S(2)}) collective-permute-start(bf16[2,2,1,2,24,768]{5,4,3,1,0,2:T(8,128)(2,1)S(1)} %slice.8), channel_id=1, source_target_pairs={{0,2},{1,3},{2,0},{3,1},{4,6},{5,7},{6,4},{7,5},{8,10},{9,11},{10,... | collective-permute-start | bytes 884744 | tf_op jit(solution)/shard_map/ppermute | solution.py:1410
  60.8 10.0 %collective-permute-start.20 = (f32[8,1536]{1,0:T(8,128)S(1)}, f32[8,1536]{1,0:T(8,128)S(1)}, u32[]{:S(2)}, u32[]{:S(2)}) collective-permute-start(f32[8,1536]{1,0:T(8,128)S(1)} %shard_map.310.refs_6_.refs_8_.refs_7_.refs_3_.refs_9_), channel_id=1, source_target_pairs={{0,16},{16,0},{1,17},{17,1},{2,18},{18,2},{3,19},{19,3},{4,20},{20... | collective-permute-start | bytes 147464 | tf_op jit(solution)/shard_map/ppermute | solution.py:1395
  60.9 22.0 %collective-permute-start.21 = (bf16[2,2,1,2,24,1920]{5,4,3,1,0,2:T(8,128)(2,1)S(1)}, bf16[2,2,1,2,24,1920]{5,4,3,1,0,2:T(8,128)(2,1)S(1)}, u32[]{:S(2)}, u32[]{:S(2)}) collective-permute-start(bf16[2,2,1,2,24,1920]{5,4,3,1,0,2:T(8,128)(2,1)S(1)} %slice.9), channel_id=1, source_target_pairs={{0,2},{1,3},{2,0},{3,1},{4,6},{5,7},{6,4},{7,5},{8,10},{9,11},{10,... | collective-permute-start | bytes 2211848 | tf_op jit(solution)/shard_map/ppermute | solution.py:1410
  61.5 21.4 %collective-permute-start.22 = (bf16[2,2,2,1,96,384]{5,4,2,1,0,3:T(8,128)(2,1)S(1)}, bf16[2,2,2,1,96,384]{5,4,2,1,0,3:T(8,128)(2,1)S(1)}, u32[]{:S(2)}, u32[]{:S(2)}) collective-permute-start(bf16[2,2,2,1,96,384]{5,4,2,1,0,3:T(8,128)(2,1)S(1)} %bitcast.157), channel_id=1, source_target_pairs={{0,1},{1,0},{2,3},{3,2},{4,5},{5,4},{6,7},{7,6},{8,9},{9,8},{10,11... | collective-permute-start | bytes 1769480 | tf_op jit(solution)/shard_map/ppermute | solution.py:1410
  121.6 16.0 %collective-permute-start.25 = (bf16[16,24,1536]{2,1,0:T(8,128)(2,1)}, bf16[16,24,1536]{2,1,0:T(8,128)(2,1)S(1)}, u32[]{:S(2)}, u32[]{:S(2)}) collective-permute-start(bf16[16,24,1536]{2,1,0:T(8,128)(2,1)} %get-tuple-element.228), channel_id=1, source_target_pairs={{0,16},{16,0},{1,17},{17,1},{2,18},{18,2},{3,19},{19,3},{4,20},{20... | collective-permute-start | bytes 3538952 | tf_op jit(solution)/shard_map/ppermute | solution.py:1395
  121.9 15.7 %collective-permute-start.26 = (bf16[512,384]{1,0:T(8,128)(2,1)}, bf16[512,384]{1,0:T(8,128)(2,1)S(1)}, u32[]{:S(2)}, u32[]{:S(2)}) collective-permute-start(bf16[512,384]{1,0:T(8,128)(2,1)} %get-tuple-element.229), channel_id=1, source_target_pairs={{0,16},{16,0},{1,17},{17,1},{2,18},{18,2},{3,19},{19,3},{4,20},{20... | collective-permute-start | bytes 1179656 | tf_op jit(solution)/shard_map/ppermute | solution.py:1395
  146.4 18.8 %collective-permute-start.28 = (bf16[8,24,1536]{2,1,0:T(8,128)(2,1)S(1)}, bf16[8,24,1536]{2,1,0:T(8,128)(2,1)S(1)}, u32[]{:S(2)}, u32[]{:S(2)}) collective-permute-start(bf16[8,24,1536]{2,1,0:T(8,128)(2,1)S(1)} %bitcast.226), channel_id=1, source_target_pairs={{0,1},{1,0},{2,3},{3,2},{4,5},{5,4},{6,7},{7,6},{8,9},{9,8},{10,11... | collective-permute-start | bytes 1769480 | tf_op jit(solution)/shard_map/ppermute | solution.py:1410
  147.1 15.7 %collective-permute-start.29 = (bf16[8,24,1024]{2,1,0:T(8,128)(2,1)S(1)}, bf16[8,24,1024]{2,1,0:T(8,128)(2,1)S(1)}, u32[]{:S(2)}, u32[]{:S(2)}) collective-permute-start(bf16[8,24,1024]{2,1,0:T(8,128)(2,1)S(1)} %bitcast.227), channel_id=1, source_target_pairs={{0,2},{1,3},{2,0},{3,1},{4,6},{5,7},{6,4},{7,5},{8,10},{9,11},{10,... | collective-permute-start | bytes 1179656 | tf_op jit(solution)/shard_map/ppermute | solution.py:1410
  169.6 23.6 %collective-permute-start.33 = (bf16[8,24,1536]{2,1,0:T(8,128)(2,1)}, bf16[8,24,1536]{2,1,0:T(8,128)(2,1)S(1)}, u32[]{:S(2)}, u32[]{:S(2)}) collective-permute-start(bf16[8,24,1536]{2,1,0:T(8,128)(2,1)} %bitcast.79), channel_id=1, source_target_pairs={{0,1},{1,0},{2,3},{3,2},{4,5},{5,4},{6,7},{7,6},{8,9},{9,8},{10,11... | collective-permute-start | bytes 1769480 | tf_op jit(solution)/shard_map/ppermute | solution.py:1410
  170.1 22.3 %collective-permute-start.31 = (bf16[4,24,1536]{2,1,0:T(8,128)(2,1)}, bf16[4,24,1536]{2,1,0:T(8,128)(2,1)S(1)}, u32[]{:S(2)}, u32[]{:S(2)}) collective-permute-start(bf16[4,24,1536]{2,1,0:T(8,128)(2,1)} %bitcast.73), channel_id=1, source_target_pairs={{0,2},{1,3},{2,0},{3,1},{4,6},{5,7},{6,4},{7,5},{8,10},{9,11},{10,... | collective-permute-start | bytes 884744 | tf_op jit(solution)/shard_map/ppermute | solution.py:1410
  171.8 20.6 %collective-permute-start.32 = (bf16[4,24,1024]{2,1,0:T(8,128)(2,1)}, bf16[4,24,1024]{2,1,0:T(8,128)(2,1)}, u32[]{:S(2)}, u32[]{:S(2)}) collective-permute-start(bf16[4,24,1024]{2,1,0:T(8,128)(2,1)} %bitcast.76), channel_id=1, source_target_pairs={{0,1},{1,0},{2,3},{3,2},{4,5},{5,4},{6,7},{7,6},{8,9},{9,8},{10,11... | collective-permute-start | bytes 589832 | tf_op jit(solution)/shard_map/ppermute | solution.py:1410
  198.6 11.8 %collective-permute-start.35 = (bf16[8,24,1024]{2,1,0:T(8,128)(2,1)}, bf16[8,24,1024]{2,1,0:T(8,128)(2,1)S(1)}, u32[]{:S(2)}, u32[]{:S(2)}) collective-permute-start(bf16[8,24,1024]{2,1,0:T(8,128)(2,1)} %bitcast.92), channel_id=1, source_target_pairs={{0,1},{1,0},{2,3},{3,2},{4,5},{5,4},{6,7},{7,6},{8,9},{9,8},{10,11... | collective-permute-start | bytes 1179656 | tf_op jit(solution)/shard_map/ppermute | solution.py:1410
  199.0 11.4 %collective-permute-start.37 = (bf16[4,24,1536]{2,1,0:T(8,128)(2,1)}, bf16[4,24,1536]{2,1,0:T(8,128)(2,1)S(1)}, u32[]{:S(2)}, u32[]{:S(2)}) collective-permute-start(bf16[4,24,1536]{2,1,0:T(8,128)(2,1)} %bitcast.89), channel_id=1, source_target_pairs={{0,2},{1,3},{2,0},{3,1},{4,6},{5,7},{6,4},{7,5},{8,10},{9,11},{10,... | collective-permute-start | bytes 884744 | tf_op jit(solution)/shard_map/ppermute | solution.py:1410
  200.7 9.0 %collective-permute-start.36 = (bf16[2,24,2560]{2,1,0:T(8,128)(2,1)}, bf16[2,24,2560]{2,1,0:T(8,128)(2,1)S(1)}, u32[]{:S(2)}, u32[]{:S(2)}) collective-permute-start(bf16[2,24,2560]{2,1,0:T(8,128)(2,1)} %bitcast.86), channel_id=1, source_target_pairs={{0,4},{1,5},{2,6},{3,7},{4,0},{5,1},{6,2},{7,3},{8,12},{9,13},{10,... | collective-permute-start | bytes 737288 | tf_op jit(solution)/shard_map/ppermute | solution.py:1410
  210.4 22.3 %collective-permute-start.42 = (f32[512,384]{1,0:T(8,128)}, f32[512,384]{1,0:T(8,128)S(1)}, u32[]{:S(2)}, u32[]{:S(2)}) collective-permute-start(f32[512,384]{1,0:T(8,128)} %get-tuple-element.324), channel_id=1, source_target_pairs={{0,16},{16,0},{1,17},{17,1},{2,18},{18,2},{3,19},{19,3},{4,20},{20... | collective-permute-start | bytes 2359304 | tf_op jit(solution)/shard_map/ppermute | solution.py:1395
  211.2 8.4 %collective-permute-start.38 = (bf16[4,24,1024]{2,1,0:T(8,128)(2,1)S(1)}, bf16[4,24,1024]{2,1,0:T(8,128)(2,1)S(1)}, u32[]{:S(2)}, u32[]{:S(2)}) collective-permute-start(bf16[4,24,1024]{2,1,0:T(8,128)(2,1)S(1)} %bitcast.230), channel_id=1, source_target_pairs={{0,2},{1,3},{2,0},{3,1},{4,6},{5,7},{6,4},{7,5},{8,10},{9,11},{10,... | collective-permute-start | bytes 589832 | tf_op jit(solution)/shard_map/ppermute | solution.py:1410
  221.3 8.9 %collective-permute-start.40 = (bf16[2,24,2560]{2,1,0:T(8,128)(2,1)S(1)}, bf16[2,24,2560]{2,1,0:T(8,128)(2,1)S(1)}, u32[]{:S(2)}, u32[]{:S(2)}) collective-permute-start(bf16[2,24,2560]{2,1,0:T(8,128)(2,1)S(1)} %bitcast.229), channel_id=1, source_target_pairs={{0,4},{1,5},{2,6},{3,7},{4,0},{5,1},{6,2},{7,3},{8,12},{9,13},{10,... | collective-permute-start | bytes 737288 | tf_op jit(solution)/shard_map/ppermute | solution.py:1410
  223.4 9.2 %collective-permute-start.43 = (bf16[8,2304]{1,0:T(8,128)(2,1)S(1)}, bf16[8,2304]{1,0:T(8,128)(2,1)S(1)}, u32[]{:S(2)}, u32[]{:S(2)}) collective-permute-start(bf16[8,2304]{1,0:T(8,128)(2,1)S(1)} %copy-done.40), channel_id=1, source_target_pairs={{0,16},{16,0},{1,17},{17,1},{2,18},{18,2},{3,19},{19,3},{4,20},{20... | collective-permute-start | bytes 110600 | tf_op jit(solution)/shard_map/ppermute | solution.py:1395
  232.7 14.3 %collective-permute-start.45 = (bf16[1,24,5120]{2,1,0:T(8,128)(2,1)S(1)}, bf16[1,24,5120]{2,1,0:T(8,128)(2,1)S(1)}, u32[]{:S(2)}, u32[]{:S(2)}) collective-permute-start(bf16[1,24,5120]{2,1,0:T(8,128)(2,1)S(1)} %bitcast.228), channel_id=1, source_target_pairs={{0,8},{1,9},{2,10},{3,11},{4,12},{5,13},{6,14},{7,15},{8,0},{9,1},... | collective-permute-start | bytes 737288 | tf_op jit(solution)/shard_map/ppermute | solution.py:1410
  (62 other events, 361.4 us)
Sparse Core Ops, SparseCore 0:
  122.3 63.7 all-gather.1

commit v4 on v3

--- a/solution.py
+++ b/solution.py
@@ -139,6 +139,8 @@
         return In(copy, kept)
 
     def push(self, name):
+        if name not in self.results:
+            return
         kept, target, sem = self.results[name]
         copy = pltpu.make_async_copy(kept, target, sem)
         copy.start()
@@ -626,6 +628,17 @@
         return carry
 
     lax.fori_loop(0, GROUP // HALF, halves, 0)
+
+
+def second_layer_body(k):
+    attn_forward_body(k)
+    for name in ("ordered", "qkvg", "dp", "vc", "cum", "cumt", "o", "gated"):
+        setattr(k, name, In(None, getattr(k, name)))
+    ffn_backward_body(k)
+    for name in ("branch_low", "gwo"):
+        setattr(k, name, In(None, getattr(k, name)))
+    k.sums = k.mixer_sums
+    mixer_backward_body(k)
 
 
 def input_backward_body(k):
@@ -888,6 +901,75 @@
     )
 
 
+def second_layer(layouts, x, mods, small, grad, qk, vgd, upo, down, devices):
+    shard = D // devices
+    in_kernel = shard % 8 == 0
+    if in_kernel:
+        sums = dict(
+            keep=((devices, shard, FF), f32, True),
+            gone=((devices, shard, FF), bf16, False),
+        )
+    else:
+        sums = dict(gwu=((D, FF), f32, False), gwn=((FF, D), f32, False))
+    return call(
+        second_layer_body,
+        1,
+        layouts,
+        dict(
+            x=micro(x),
+            mods=own(mods),
+            w_qk=own(qk),
+            w_vgd=own(vgd),
+            small=own(small),
+            wo=own(upo, AT_OUT),
+            grad=micro(grad),
+            wu=own(upo, AT_UP),
+            wn=own(down),
+        ),
+        dict(
+            out=((ROWS, D), bf16, True),
+            sent=((ROWS, D), bf16, False),
+            mid_grad=((ROWS, D), f32, True),
+            sums=((8, FF), f32, True),
+            low=((ROWS, QKVG + LANES), bf16, True),
+            gw_keep=((D, GROUP), f32, True),
+            gw_send=((D, GROUP), bf16, False),
+            mixer_sums=((8, D), f32, True),
+            **sums,
+        ),
+        dict(
+            ordered=((ROWS, D), bf16),
+            qkvg=((ROWS, QKVG), f32),
+            dp=((ROWS, LANES), f32),
+            vc=((ROWS, D), f32),
+            cum=((ROWS, LANES), f32),
+            cumt=((LANES, ROWS), f32),
+            o=((ROWS, D), f32),
+            gated=((ROWS, D), bf16),
+            inner=((ROWS, D), bf16),
+            vpad=((ROWS + 8, D), f32),
+            bias=((HALF, ROWS), f32),
+            branch_low=((ROWS, D), bf16),
+            gwo=((D, D), f32),
+            **({"gwn": ((FF, D), f32)} if in_kernel else {}),
+            hidden_s=((ROWS, FF), bf16),
+            inner_s=((ROWS, D), bf16),
+            up_s=((ROWS, FF), bf16),
+            down_s=((ROWS, D), bf16),
+            gmod=((8, FF), f32),
+            gbu=((1, FF), f32),
+            gbn=((1, D), f32),
+            mixed_s=((ROWS, D), f32),
+            dv_s=((ROWS + 8, D), f32),
+            rows_s=((ROWS, LANES), f32),
+            cols_s=((LANES, ROWS), f32),
+            gw=((D, 2 * GROUP), f32),
+        ),
+        14 * 10**9,
+        packed=in_kernel,
+    )
+
+
 def mixer_backward(layer, layouts, small, saved, branch_low, gwo, upo, after=()):
     ordered, qkvg, dp, vc, cum, cumt, o = saved
     return call(
@@ -1501,18 +1583,12 @@
     out_one, branch, down_raw = ffn_forward(0, layouts, x, mods, smalls, gated, upo, down)
     kept = [(x, saved, gated, branch, down_raw)]
     x = out_one[None]
-    *saved, gated = attn_forward(1, layouts, x, mods, smalls, qk, vgd)
-    kept.append((x, saved, gated, None, None))
+    kept.append((x,))
 
     late, _ = lock(w_ada[0], out_one)
     ada_all = lax.all_gather(late, "row", axis=0, tiled=True)
 
-    def ffn_step(l, grad, after=()):
-        x, saved, gated, branch, down_raw = kept[l]
-        results = ffn_backward(
-            l, layouts, x, mods, smalls, gated, branch, down_raw, grad, upo, down, devices, after
-        )
-        acts, (mid_grad, branch_low, gwo, sums, *terms) = results[: 2 * l], results[2 * l :]
+    def halved(terms):
         if terms[0].ndim == 2:
             up_sum = terms[0].reshape(devices, shard, 2, FF // 2)
             down_sum = terms[1].reshape(devices, 2, 2, shard, D)
@@ -1524,14 +1600,10 @@
                     jnp.concatenate([up_half, down_half[:, 0], down_half[:, 1]], axis=2)
                 )
             terms[1] = terms[1].astype(bf16)
-        return [branch_low, gwo], mid_grad, terms[0], terms[1], sums, *acts
-
-    def mixer_step(l, carried, after=()):
-        low, keep, sent, sums = mixer_backward(
-            l, layouts, smalls, kept[l][1], *carried, upo, after
-        )
-        by_row = lambda array: array.reshape(devices, shard, GROUP)
-        return low, by_row(keep), by_row(sent), sums
+        return terms
+
+    def by_row(array):
+        return array.reshape(devices, shard, GROUP)
 
     def input_step(l, low, mid_grad, ffn_sums, mixer_sums, two=None, after=()):
         x = kept[l][0]
@@ -1551,22 +1623,31 @@
         return mod
 
     x_bits, y_bits, z_bits = along_x, along_y, along_z
-    carried, mid_grad, f2_keep, f2_sent, f2_sums, out_two, acts_sent = ffn_step(1, output_grad)
-    *carried, f2_sent, acts_sent = lock(*carried, f2_sent, acts_sent)
+    (
+        out_two, acts_sent, mid_grad, f2_sums, low, a2_keep, a2_sent, m2_sums, *terms
+    ) = second_layer(
+        layouts, x, mods, smalls, output_grad, qk, vgd, upo, down, devices
+    )
+    f2_keep, f2_sent = halved(terms)
+    a2_keep, a2_sent = by_row(a2_keep), by_row(a2_sent)
+    low, f2_sent, a2_sent, acts_sent = lock(low, f2_sent, a2_sent, acts_sent)
     f2_came = swap(f2_sent)
+    a2_came = swap(a2_sent)
     acts_came = swap(acts_sent)
-    low, a2_keep, a2_sent, m2_sums = mixer_step(1, carried)
-    low, a2_sent, f2_came, acts_came = lock(low, a2_sent, f2_came, acts_came)
-    a2_came = swap(a2_sent)
     gx_two, grad, mod_low_two, sums_two = input_step(1, low, mid_grad, f2_sums, m2_sums)
-    grad, a2_came = lock(grad, a2_came)
+    grad, f2_came, a2_came, acts_came = lock(grad, f2_came, a2_came, acts_came)
     f2_keep, f2_sent = run([f2_keep], [(f2_came, 1)], x_bits)
     a2_keep, a2_sent = run([a2_keep], [(a2_came, 1)], y_bits, 1 << len(x_bits))
     grad, f2_sent, a2_sent = lock(grad, f2_sent, a2_sent)
     f2_came = partner(f2_sent, x_bits[-1])
     a2_came = partner(a2_sent, y_bits[-1])
 
-    carried, mid_grad, f1_keep, f1_sent, f1_sums = ffn_step(0, grad[None])
+    x, saved, gated, branch, down_raw = kept[0]
+    mid_grad, branch_low, gwo, f1_sums, *terms = ffn_backward(
+        0, layouts, x, mods, smalls, gated, branch, down_raw, grad[None], upo, down, devices
+    )
+    f1_keep, f1_sent = halved(terms)
+    carried = (branch_low, gwo)
     *carried, f1_sent, f2_came, a2_came = lock(*carried, f1_sent, f2_came, a2_came)
     f1_came = swap(f1_sent)
     f2_keep, f2_sent = run(f2_keep, [(f2_came, 1)], y_bits)
@@ -1576,7 +1657,8 @@
     f1_came = partner(f1_sent, x_bits[-1])
     a2_came = partner(a2_sent, x_bits[-1])
     f2_came = partner(f2_sent, y_bits[-1])
-    low, a1_keep, a1_sent, m1_sums = mixer_step(0, carried)
+    low, a1_keep, a1_sent, m1_sums = mixer_backward(0, layouts, smalls, saved, *carried, upo)
+    a1_keep, a1_sent = by_row(a1_keep), by_row(a1_sent)
     low, a1_sent, f2_came, a2_came, f1_came, ada_all = lock(
         low, a1_sent, f2_came, a2_came, f1_came, ada_all
     )

time: 261 us -> 260 us (level)
  Pallas kernels: 121 us -> 112 us
  waiting for transfers between devices: 55.8 us -> 62.1 us
  local copies, waits for them, and re-layouts: 15.8 us -> 18.5 us
    pallas_call x9 -> x7, Pallas kernels: 95.4 us -> 88.2 us  [call(): pl.pallas_call(kernel, out_shape=[jax.ShapeDtypeStruct(shape, kind) for s...]
    all_gather x1, waiting for transfers between devices: 0.02 us -> 4.93 us  [on_device(): ada_all = lax.all_gather(late, 'row', axis=0, tiled=True)]
    unnamed x87 -> x91, local copies, waits for them, and re-layouts: 15.6 us -> 18.3 us
  transfers between devices with their start and end apart: 52 -> 52, of which waited for: 17 -> 17; matrix products, arithmetic and copies ran while one was open for 1% -> 1% of each run, Pallas kernels for 33% -> 27%
where the time goes in v4:
time: 260 us; the launch traced here: 256 us
  Pallas kernels  112 us (43%)
  waiting for transfers between devices  62.1 us (24%)
  starting transfers between devices  46.9 us (18%)
  local copies, waits for them, and re-layouts  18.5 us (7%)
  between operations  15.1 us (6%)
    pallas_call x7, Pallas kernels, call(): pl.pallas_call(kernel, out_shape=[jax.ShapeDtypeStruct(shape, kind) for s...  88.2 us
    ppermute x35, waiting for transfers between devices, across(): return lax.ppermute(values, 'row', [(i, i ^ flips) for i in range(size)])  48.4 us
    ppermute x35, starting transfers between devices, across(): return lax.ppermute(values, 'row', [(i, i ^ flips) for i in range(size)])  44.2 us
    unnamed x91, local copies, waits for them, and re-layouts  18.3 us
    pallas_call x11, Pallas kernels, step(): pl.pallas_call(functools.partial(step_kernel, bit, widths, [count for _,...  13.5 us
    ppermute x16, waiting for transfers between devices, swap(): return lax.ppermute(values, 'section', [(0, 1), (1, 0)])  8.71 us
  transfers between devices with their start and end apart: 52, of which 17 were waited for; matrix products, arithmetic and copies ran while one was open for 1% of the time, Pallas kernels for 27%

profile of v4, /device:TPU:0, one launch (start us, length us, event | category | flops | bytes accessed | tf_op | source)
XLA Modules:
  0.0 255.9 jit_solution(9831197107752617301)
XLA Ops:
  7.2 1.9 shard_map.305
  9.1 4.0 %collective-permute-start = (bf16[1,4,384]{2,1,0:T(4,128)(2,1)}, bf16[1,4,384]{2,1,0:T(4,128)(2,1)S(1)}, u32[]{:S(2)}, u32[]{:S(2)}) collective-permute-start(bf16[1,4,384]{2,1,0:T(4,128)(2,1)} %get-tuple-element.175), channel_id=1, source_target_pairs={{0,8},{1,9},{2,10},{3,11},{4,12},{5,13},{6,14},{7,15},{8,0},{9,1},... | collective-permute-start | bytes 9224 | tf_op jit(solution)/shard_map/ppermute | solution.py:1492
  15.0 2.6 %collective-permute-start.9 = (bf16[1,1,1,1,96,384]{5,4,3,2,1,0:T(8,128)(2,1)}, bf16[1,1,1,1,96,384]{5,4,3,2,1,0:T(8,128)(2,1)S(1)}, u32[]{:S(2)}, u32[]{:S(2)}) collective-permute-start(bf16[1,1,1,1,96,384]{5,4,3,2,1,0:T(8,128)(2,1)} %bitcast.206), channel_id=1, source_target_pairs={{0,8},{1,9},{2,10},{3,11},{4,12},{5,13},{6,14},{7,15},{8,0},{9,1},... | collective-permute-start | bytes 221192 | tf_op jit(solution)/shard_map/ppermute | solution.py:1492
  22.3 5.9 %collective-permute-done.8 = bf16[1,1,1,1,24,896]{5,4,3,2,1,0:T(8,128)(2,1)S(1)} collective-permute-done((bf16[1,1,1,1,24,896]{5,4,3,2,1,0:T(8,128)(2,1)}, bf16[1,1,1,1,24,896]{5,4,3,2,1,0:T(8,128)(2,1)S(1)}, u32[]{:S(2)}, u32[]{:S(2)}) %collective-permute-start.8) | collective-permute-done | bytes 43040 | tf_op jit(solution)/shard_map/ppermute | solution.py:1492
  32.5 1.9 collective-permute-start.12
  34.5 1.9 collective-permute-start.11
  36.4 5.7 %collective-permute-done.1 = bf16[2,4,384]{2,1,0:T(4,128)(2,1)S(1)} collective-permute-done((bf16[2,4,384]{2,1,0:T(4,128)(2,1)S(1)}, bf16[2,4,384]{2,1,0:T(4,128)(2,1)S(1)}, u32[]{:S(2)}, u32[]{:S(2)}) %collective-permute-start.1) | collective-permute-done | bytes 6176 | tf_op jit(solution)/shard_map/ppermute | solution.py:1492
  46.4 4.1 %collective-permute-done.4 = f32[2,4,2304]{2,1,0:T(4,128)S(1)} collective-permute-done((f32[2,4,2304]{2,1,0:T(4,128)S(1)}, f32[2,4,2304]{2,1,0:T(4,128)S(1)}, u32[]{:S(2)}, u32[]{:S(2)}) %collective-permute-start.4) | collective-permute-done | bytes 73760 | tf_op jit(solution)/shard_map/ppermute | solution.py:1492
  51.8 3.8 %collective-permute-done.5.refs_6_ = f32[1,4,2304]{2,1,0:T(4,128)S(1)} collective-permute-done((f32[1,4,2304]{2,1,0:T(4,128)S(1)}, f32[1,4,2304]{2,1,0:T(4,128)S(1)}, u32[]{:S(2)}, u32[]{:S(2)}) %collective-permute-start.5) | collective-permute-done | bytes 36896 | tf_op jit(solution)/shard_map/ppermute | solution.py:1492
  57.4 1.8 collective-permute-start.17
  61.8 6.3 %collective-permute-done.16 = bf16[2,2,1,2,24,768]{5,4,3,1,0,2:T(8,128)(2,1)} collective-permute-done((bf16[2,2,1,2,24,768]{5,4,3,1,0,2:T(8,128)(2,1)S(1)}, bf16[2,2,1,2,24,768]{5,4,3,1,0,2:T(8,128)(2,1)}, u32[]{:S(2)}, u32[]{:S(2)}) %collective-permute-start.16) | collective-permute-done | bytes 294944 | tf_op jit(solution)/shard_map/ppermute | solution.py:1492
  68.0 2.3 shard_map.314
  73.8 9.2 %shard_map.315 = (bf16[512,384]{1,0:T(8,128)(2,1)}, f32[512,1536]{1,0:T(8,128)}, f32[512,128]{1,0:T(8,128)}, f32[512,384]{1,0:T(8,128)}, f32[512,128]{1,0:T(8,12...) custom-call(s32[2,1]{1,0:T(2,128)} %copy.37.refs_0_, bf16[2,512,384]{2,1,0:T(8,128)(2,1)} %refs_6_.1, ...), custom_call_target="tpu_custom_call" | custom-call | flops 4000000000 | bytes 4194304 | tf_op jit(solution)/shard_map/pallas_call | solution.py:761
  84.8 4.4 %collective-permute-done.24.refs_12_.refs_16_ = bf16[1536,384]{1,0:T(8,128)(2,1)S(1)} collective-permute-done((bf16[1536,384]{1,0:T(8,128)(2,1)S(1)}, bf16[1536,384]{1,0:T(8,128)(2,1)S(1)}, u32[]{:S(2)}, u32[]{:S(2)}) %collective-permute-start.24) | collective-permute-done | bytes 1179680 | tf_op jit(solution)/shard_map/ppermute | solution.py:1477
  91.5 6.6 %shard_map.317 = (bf16[512,384]{1,0:T(8,128)(2,1)}, f32[512,384]{1,0:T(8,128)}, f32[512,384]{1,0:T(8,128)}) custom-call(s32[2,1]{1,0:T(2,128)} %copy.37.refs_0_, bf16[512,384]{1,0:T(8,128)(2,1)} %get-tuple-element.194.refs_4_.refs_1_.refs_13_, bf16[2,512,384]{2,1,0:T(8,128)(2,1)} %refs_6_.1, bf16[384,1920]{1,0:T(8,128)(2,1)} %bitcast.215, ...), custom_call_target="tpu_custom_call" | custom-call | flops 3000000000 | bytes 4194304 | tf_op jit(solution)/shard_map/pallas_call | solution.py:761
  98.1 31.9 %shard_map.318 = (bf16[512,384]{1,0:T(8,128)(2,1)}, bf16[512,384]{1,0:T(8,128)(2,1)}, f32[512,384]{1,0:T(8,128)}, f32[8,1536]{1,0:T(8,128)}, bf16[512,1664]{1,0:...) custom-call(s32[2,1]{1,0:T(2,128)} %copy.37.refs_0_, ...), custom_call_target="tpu_custom_call" | custom-call | flops 14000000000 | bytes 4194304 | tf_op jit(solution)/shard_map/pallas_call | solution.py:761
  130.8 6.4 %shard_map.319 = (f32[512,384]{1,0:T(8,128)}, bf16[512,384]{1,0:T(8,128)(2,1)}, bf16[8,2304]{1,0:T(8,128)(2,1)}, f32[8,768]{1,0:T(8,128)}) custom-call(s32[2,1]{1,0:T(2,128)} %copy.37.refs_0_, bf16[512,1664]{1,0:T(8,128)(2,1)} %get-tuple-element.204.refs_1_, bf16[384,768]{1,0:T(8,128)(2,1)} %bitcast.52.refs_4_.refs_2_, ...), custom_call_target="tpu_custom_call" | custom-call | flops 2000000000 | bytes 4194304 | tf_op jit(solution)/shard_map/pallas_call | solution.py:761
  141.1 2.6 %collective-permute-start.29 = (bf16[8,24,1024]{2,1,0:T(8,128)(2,1)S(1)}, bf16[8,24,1024]{2,1,0:T(8,128)(2,1)S(1)}, u32[]{:S(2)}, u32[]{:S(2)}) collective-permute-start(bf16[8,24,1024]{2,1,0:T(8,128)(2,1)S(1)} %bitcast.226), channel_id=1, source_target_pairs={{0,2},{1,3},{2,0},{3,1},{4,6},{5,7},{6,4},{7,5},{8,10},{9,11},{10,... | collective-permute-start | bytes 1179656 | tf_op jit(solution)/shard_map/ppermute | solution.py:1492
  143.7 13.0 %shard_map.323 = (f32[512,384]{1,0:T(8,128)}, bf16[512,384]{1,0:T(8,128)(2,1)}, f32[384,384]{1,0:T(8,128)}, f32[8,1536]{1,0:T(8,128)}, f32[16,24,1536]{2,1,0:T(8,128)}, /*index=5*/bf16[16,24,1536]{2,1,0:T(8,128)(2,1)}) custom-call(s32[2,1]{1,0:T(2,128)} %copy.37.refs_0_, f32[4,2304]{1,0:T(4,128)} %copy-done.35, f32[4,2304]{1,0:T(4,128)} %copy-done.41, ...), custom_call_target="tpu_custom_call" | custom-call | flops 5000000000 | bytes 4194304 | tf_op jit(solution)/shard_map/pallas_call | solution.py:761
  165.2 15.2 %shard_map.327 = (bf16[512,1664]{1,0:T(8,128)(2,1)}, f32[384,1024]{1,0:T(8,128)}, bf16[384,1024]{1,0:T(8,128)(2,1)}, f32[8,384]{1,0:T(8,128)}) custom-call(s32[2,1]{1,0:T(2,128)} %copy.37.refs_0_, bf16[512,384]{1,0:T(8,128)(2,1)} %get-tuple-element.240.refs_1_, bf16[384,1920]{1,0:T(8,128)(2,1)} %bitcast.220, bf16[384,1920]{1,0:T(8,128)(2,1)} %copy-done.38, ...), custom_call_target="tpu_custom_call" | custom-call | flops 7000000000 | bytes 4194304 | tf_op jit(solution)/shard_map/pallas_call | solution.py:761
  180.4 7.1 %collective-permute-done.32 = bf16[4,24,1024]{2,1,0:T(8,128)(2,1)S(1)} collective-permute-done((bf16[4,24,1024]{2,1,0:T(8,128)(2,1)S(1)}, bf16[4,24,1024]{2,1,0:T(8,128)(2,1)S(1)}, u32[]{:S(2)}, u32[]{:S(2)}) %collective-permute-start.32) | collective-permute-done | bytes 196640 | tf_op jit(solution)/shard_map/ppermute | solution.py:1492
  188.9 4.9 %all-gather.2.cloned.1.call-done.ada = bf16[384,2304]{1,0:T(8,128)(2,1)} async-done(((bf16[24,2304]{1,0:T(8,128)(2,1)}), bf16[384,2304]{1,0:T(8,128)(2,1)}) %all-gather.2.cloned.1.call-update) | async-done | bytes 1769488 | tf_op jit(solution)/shard_map/all_gather | solution.py:1589
  200.2 1.7 collective-permute-start.37
  203.1 5.8 %shard_map.331 = (f32[512,384]{1,0:T(8,128)}, bf16[512,384]{1,0:T(8,128)(2,1)}, bf16[8,2304]{1,0:T(8,128)(2,1)}, f32[8,768]{1,0:T(8,128)}, f32[512,384]{1,0:T(8,...) custom-call(s32[2,1]{1,0:T(2,128)} %copy.37.refs_0_, bf16[512,1664]{1,0:T(8,128)(2,1)} %get-tuple-element.267.refs_1_, ...), custom_call_target="tpu_custom_call" | custom-call | flops 2000000000 | bytes 4194304 | tf_op jit(solution)/shard_map/pallas_call | solution.py:761
  213.4 1.9 collective-permute-start.39
  215.3 4.9 %collective-permute-done.39.arrived = bf16[48,768]{1,0:T(8,128)(2,1)S(1)} collective-permute-done((bf16[48,768]{1,0:T(8,128)(2,1)S(1)}, bf16[48,768]{1,0:T(8,128)(2,1)S(1)}, u32[]{:S(2)}, u32[]{:S(2)}) %collective-permute-start.39) | collective-permute-done | bytes 73760 | tf_op jit(solution)/shard_map/ppermute | solution.py:1492
  220.3 1.6 shard_map.334
  222.4 1.7 collective-permute-start.41
  224.1 6.8 %collective-permute-done.41.arrived = bf16[64,768]{1,0:T(8,128)(2,1)S(1)} collective-permute-done((bf16[64,768]{1,0:T(8,128)(2,1)S(1)}, bf16[64,768]{1,0:T(8,128)(2,1)S(1)}, u32[]{:S(2)}, u32[]{:S(2)}) %collective-permute-start.41) | collective-permute-done | bytes 98336 | tf_op jit(solution)/shard_map/ppermute | solution.py:1492
  230.9 2.4 shard_map.336
  233.4 1.7 collective-permute-start.45
  243.5 1.9 collective-permute-done.45.refs_4_
  (213 shorter events, 66.6 us)
Async XLA Ops:
  7.2 186.6 %all-gather.2.cloned.1.call-start = ((), (), s32[]{:S(2)}) async-start(), calls=%async_computation | async-start | bytes 1880064 | tf_op jit(solution)/shard_map/all_gather | solution.py:1589
  9.1 12.2 %collective-permute-start = (bf16[1,4,384]{2,1,0:T(4,128)(2,1)}, bf16[1,4,384]{2,1,0:T(4,128)(2,1)S(1)}, u32[]{:S(2)}, u32[]{:S(2)}) collective-permute-start(bf16[1,4,384]{2,1,0:T(4,128)(2,1)} %get-tuple-element.175), channel_id=1, source_target_pairs={{0,8},{1,9},{2,10},{3,11},{4,12},{5,13},{6,14},{7,15},{8,0},{9,1},... | collective-permute-start | bytes 9224 | tf_op jit(solution)/shard_map/ppermute | solution.py:1492
  13.2 8.2 %collective-permute-start.2 = (bf16[1,1,1,1,24,2304]{5,4,3,2,1,0:T(8,128)(2,1)}, bf16[1,1,1,1,24,2304]{5,4,3,2,1,0:T(8,128)(2,1)S(1)}, u32[]{:S(2)}, u32[]{:S(2)}) collective-permute-start(bf16[1,1,1,1,24,2304]{5,4,3,2,1,0:T(8,128)(2,1)} %bitcast.198), channel_id=1, source_target_pairs={{0,1},{1,0},{2,3},{3,2},{4,5},{5,4},{6,7},{7,6},{8,9},{9,8},{10,11... | collective-permute-start | bytes 331784 | tf_op jit(solution)/shard_map/ppermute | solution.py:1492
  14.7 13.5 %collective-permute-start.7 = (bf16[1,1,1,1,24,2688]{5,4,3,2,1,0:T(8,128)(2,1)}, bf16[1,1,1,1,24,2688]{5,4,3,2,1,0:T(8,128)(2,1)S(1)}, u32[]{:S(2)}, u32[]{:S(2)}) collective-permute-start(bf16[1,1,1,1,24,2688]{5,4,3,2,1,0:T(8,128)(2,1)} %bitcast.195), channel_id=1, source_target_pairs={{0,8},{1,9},{2,10},{3,11},{4,12},{5,13},{6,14},{7,15},{8,0},{9,1},... | collective-permute-start | bytes 387080 | tf_op jit(solution)/shard_map/ppermute | solution.py:1492
  15.0 13.2 %collective-permute-start.9 = (bf16[1,1,1,1,96,384]{5,4,3,2,1,0:T(8,128)(2,1)}, bf16[1,1,1,1,96,384]{5,4,3,2,1,0:T(8,128)(2,1)S(1)}, u32[]{:S(2)}, u32[]{:S(2)}) collective-permute-start(bf16[1,1,1,1,96,384]{5,4,3,2,1,0:T(8,128)(2,1)} %bitcast.206), channel_id=1, source_target_pairs={{0,8},{1,9},{2,10},{3,11},{4,12},{5,13},{6,14},{7,15},{8,0},{9,1},... | collective-permute-start | bytes 221192 | tf_op jit(solution)/shard_map/ppermute | solution.py:1492
  17.6 10.6 %collective-permute-start.8 = (bf16[1,1,1,1,24,896]{5,4,3,2,1,0:T(8,128)(2,1)}, bf16[1,1,1,1,24,896]{5,4,3,2,1,0:T(8,128)(2,1)S(1)}, u32[]{:S(2)}, u32[]{:S(2)}) collective-permute-start(bf16[1,1,1,1,24,896]{5,4,3,2,1,0:T(8,128)(2,1)} %bitcast.211), channel_id=1, source_target_pairs={{0,8},{1,9},{2,10},{3,11},{4,12},{5,13},{6,14},{7,15},{8,0},{9,1},... | collective-permute-start | bytes 129032 | tf_op jit(solution)/shard_map/ppermute | solution.py:1492
  30.8 12.3 %collective-permute-start.10 = (bf16[2,1,1,1,24,2688]{5,4,0,3,2,1:T(8,128)(2,1)S(1)}, bf16[2,1,1,1,24,2688]{5,4,0,3,2,1:T(8,128)(2,1)S(1)}, u32[]{:S(2)}, u32[]{:S(2)}) collective-permute-start(bf16[2,1,1,1,24,2688]{5,4,0,3,2,1:T(8,128)(2,1)S(1)} %bitcast.177), channel_id=1, source_target_pairs={{0,4},{1,5},{2,6},{3,7},{4,0},{5,1},{6,2},{7,3},{8,12},{9,13},{10,... | collective-permute-start | bytes 774152 | tf_op jit(solution)/shard_map/ppermute | solution.py:1492
  30.9 11.3 %collective-permute-start.3 = (bf16[1,1,1,2,24,2304]{5,4,3,2,1,0:T(8,128)(2,1)S(1)}, bf16[1,1,1,2,24,2304]{5,4,3,2,1,0:T(8,128)(2,1)S(1)}, u32[]{:S(2)}, u32[]{:S(2)}) collective-permute-start(bf16[1,1,1,2,24,2304]{5,4,3,2,1,0:T(8,128)(2,1)S(1)} %bitcast.138), channel_id=1, source_target_pairs={{0,2},{1,3},{2,0},{3,1},{4,6},{5,7},{6,4},{7,5},{8,10},{9,11},{10,... | collective-permute-start | bytes 663560 | tf_op jit(solution)/shard_map/ppermute | solution.py:1492
  32.5 10.6 %collective-permute-start.12 = (bf16[2,1,1,1,96,384]{5,4,0,3,2,1:T(8,128)(2,1)S(1)}, bf16[2,1,1,1,96,384]{5,4,0,3,2,1:T(8,128)(2,1)S(1)}, u32[]{:S(2)}, u32[]{:S(2)}) collective-permute-start(bf16[2,1,1,1,96,384]{5,4,0,3,2,1:T(8,128)(2,1)S(1)} %bitcast.190), channel_id=1, source_target_pairs={{0,4},{1,5},{2,6},{3,7},{4,0},{5,1},{6,2},{7,3},{8,12},{9,13},{10,... | collective-permute-start | bytes 442376 | tf_op jit(solution)/shard_map/ppermute | solution.py:1492
  34.5 8.6 %collective-permute-start.11 = (bf16[2,1,1,1,24,896]{5,4,0,3,2,1:T(8,128)(2,1)S(1)}, bf16[2,1,1,1,24,896]{5,4,0,3,2,1:T(8,128)(2,1)S(1)}, u32[]{:S(2)}, u32[]{:S(2)}) collective-permute-start(bf16[2,1,1,1,24,896]{5,4,0,3,2,1:T(8,128)(2,1)S(1)} %bitcast.203), channel_id=1, source_target_pairs={{0,4},{1,5},{2,6},{3,7},{4,0},{5,1},{6,2},{7,3},{8,12},{9,13},{10,... | collective-permute-start | bytes 258056 | tf_op jit(solution)/shard_map/ppermute | solution.py:1492
  43.2 12.4 %collective-permute-start.13 = (bf16[2,2,1,1,24,2688]{5,4,1,0,3,2:T(8,128)(2,1)S(1)}, bf16[2,2,1,1,24,2688]{5,4,1,0,3,2:T(8,128)(2,1)S(1)}, u32[]{:S(2)}, u32[]{:S(2)}) collective-permute-start(bf16[2,2,1,1,24,2688]{5,4,1,0,3,2:T(8,128)(2,1)S(1)} %bitcast.161), channel_id=1, source_target_pairs={{0,1},{1,0},{2,3},{3,2},{4,5},{5,4},{6,7},{7,6},{8,9},{9,8},{10,11... | collective-permute-start | bytes 1548296 | tf_op jit(solution)/shard_map/ppermute | solution.py:1492
  43.8 11.8 %collective-permute-start.15 = (bf16[2,2,1,1,96,384]{5,4,1,0,3,2:T(8,128)(2,1)S(1)}, bf16[2,2,1,1,96,384]{5,4,1,0,3,2:T(8,128)(2,1)S(1)}, u32[]{:S(2)}, u32[]{:S(2)}) collective-permute-start(bf16[2,2,1,1,96,384]{5,4,1,0,3,2:T(8,128)(2,1)S(1)} %bitcast.171), channel_id=1, source_target_pairs={{0,2},{1,3},{2,0},{3,1},{4,6},{5,7},{6,4},{7,5},{8,10},{9,11},{10,... | collective-permute-start | bytes 884744 | tf_op jit(solution)/shard_map/ppermute | solution.py:1492
  45.4 10.2 %collective-permute-start.14 = (bf16[2,2,1,1,24,896]{5,4,1,0,3,2:T(8,128)(2,1)S(1)}, bf16[2,2,1,1,24,896]{5,4,1,0,3,2:T(8,128)(2,1)S(1)}, u32[]{:S(2)}, u32[]{:S(2)}) collective-permute-start(bf16[2,2,1,1,24,896]{5,4,1,0,3,2:T(8,128)(2,1)S(1)} %bitcast.187), channel_id=1, source_target_pairs={{0,2},{1,3},{2,0},{3,1},{4,6},{5,7},{6,4},{7,5},{8,10},{9,11},{10,... | collective-permute-start | bytes 516104 | tf_op jit(solution)/shard_map/ppermute | solution.py:1492
  57.4 10.6 %collective-permute-start.17 = (bf16[2,2,2,1,24,896]{5,4,2,1,0,3:T(8,128)(2,1)}, bf16[2,2,2,1,24,896]{5,4,2,1,0,3:T(8,128)(2,1)}, u32[]{:S(2)}, u32[]{:S(2)}) collective-permute-start(bf16[2,2,2,1,24,896]{5,4,2,1,0,3:T(8,128)(2,1)} %bitcast.50), channel_id=1, source_target_pairs={{0,1},{1,0},{2,3},{3,2},{4,5},{5,4},{6,7},{7,6},{8,9},{9,8},{10,11... | collective-permute-start | bytes 1032200 | tf_op jit(solution)/shard_map/ppermute | solution.py:1492
  59.2 8.8 %collective-permute-start.16 = (bf16[2,2,1,2,24,768]{5,4,3,1,0,2:T(8,128)(2,1)S(1)}, bf16[2,2,1,2,24,768]{5,4,3,1,0,2:T(8,128)(2,1)}, u32[]{:S(2)}, u32[]{:S(2)}) collective-permute-start(bf16[2,2,1,2,24,768]{5,4,3,1,0,2:T(8,128)(2,1)S(1)} %slice.8), channel_id=1, source_target_pairs={{0,2},{1,3},{2,0},{3,1},{4,6},{5,7},{6,4},{7,5},{8,10},{9,11},{10,... | collective-permute-start | bytes 884744 | tf_op jit(solution)/shard_map/ppermute | solution.py:1492
  60.8 10.1 %collective-permute-start.20 = (f32[8,1536]{1,0:T(8,128)S(1)}, f32[8,1536]{1,0:T(8,128)S(1)}, u32[]{:S(2)}, u32[]{:S(2)}) collective-permute-start(f32[8,1536]{1,0:T(8,128)S(1)} %shard_map.310.refs_6_.refs_8_.refs_7_.refs_3_.refs_9_), channel_id=1, source_target_pairs={{0,16},{16,0},{1,17},{17,1},{2,18},{18,2},{3,19},{19,3},{4,20},{20... | collective-permute-start | bytes 147464 | tf_op jit(solution)/shard_map/ppermute | solution.py:1477
  60.9 22.1 %collective-permute-start.21 = (bf16[2,2,1,2,24,1920]{5,4,3,1,0,2:T(8,128)(2,1)S(1)}, bf16[2,2,1,2,24,1920]{5,4,3,1,0,2:T(8,128)(2,1)S(1)}, u32[]{:S(2)}, u32[]{:S(2)}) collective-permute-start(bf16[2,2,1,2,24,1920]{5,4,3,1,0,2:T(8,128)(2,1)S(1)} %slice.9), channel_id=1, source_target_pairs={{0,2},{1,3},{2,0},{3,1},{4,6},{5,7},{6,4},{7,5},{8,10},{9,11},{10,... | collective-permute-start | bytes 2211848 | tf_op jit(solution)/shard_map/ppermute | solution.py:1492
  61.5 21.5 %collective-permute-start.22 = (bf16[2,2,2,1,96,384]{5,4,2,1,0,3:T(8,128)(2,1)S(1)}, bf16[2,2,2,1,96,384]{5,4,2,1,0,3:T(8,128)(2,1)S(1)}, u32[]{:S(2)}, u32[]{:S(2)}) collective-permute-start(bf16[2,2,2,1,96,384]{5,4,2,1,0,3:T(8,128)(2,1)S(1)} %bitcast.157), channel_id=1, source_target_pairs={{0,1},{1,0},{2,3},{3,2},{4,5},{5,4},{6,7},{7,6},{8,9},{9,8},{10,11... | collective-permute-start | bytes 1769480 | tf_op jit(solution)/shard_map/ppermute | solution.py:1492
  140.4 16.4 %collective-permute-start.28 = (bf16[8,24,1536]{2,1,0:T(8,128)(2,1)S(1)}, bf16[8,24,1536]{2,1,0:T(8,128)(2,1)S(1)}, u32[]{:S(2)}, u32[]{:S(2)}) collective-permute-start(bf16[8,24,1536]{2,1,0:T(8,128)(2,1)S(1)} %bitcast.225), channel_id=1, source_target_pairs={{0,1},{1,0},{2,3},{3,2},{4,5},{5,4},{6,7},{7,6},{8,9},{9,8},{10,11... | collective-permute-start | bytes 1769480 | tf_op jit(solution)/shard_map/ppermute | solution.py:1492
  141.1 15.7 %collective-permute-start.29 = (bf16[8,24,1024]{2,1,0:T(8,128)(2,1)S(1)}, bf16[8,24,1024]{2,1,0:T(8,128)(2,1)S(1)}, u32[]{:S(2)}, u32[]{:S(2)}) collective-permute-start(bf16[8,24,1024]{2,1,0:T(8,128)(2,1)S(1)} %bitcast.226), channel_id=1, source_target_pairs={{0,2},{1,3},{2,0},{3,1},{4,6},{5,7},{6,4},{7,5},{8,10},{9,11},{10,... | collective-permute-start | bytes 1179656 | tf_op jit(solution)/shard_map/ppermute | solution.py:1492
  161.3 32.5 %collective-permute-start.33 = (bf16[8,24,1536]{2,1,0:T(8,128)(2,1)}, bf16[8,24,1536]{2,1,0:T(8,128)(2,1)S(1)}, u32[]{:S(2)}, u32[]{:S(2)}) collective-permute-start(bf16[8,24,1536]{2,1,0:T(8,128)(2,1)} %bitcast.79), channel_id=1, source_target_pairs={{0,1},{1,0},{2,3},{3,2},{4,5},{5,4},{6,7},{7,6},{8,9},{9,8},{10,11... | collective-permute-start | bytes 1769480 | tf_op jit(solution)/shard_map/ppermute | solution.py:1492
  162.7 25.5 %collective-permute-start.31 = (bf16[4,24,1536]{2,1,0:T(8,128)(2,1)S(1)}, bf16[4,24,1536]{2,1,0:T(8,128)(2,1)S(1)}, u32[]{:S(2)}, u32[]{:S(2)}) collective-permute-start(bf16[4,24,1536]{2,1,0:T(8,128)(2,1)S(1)} %bitcast.227), channel_id=1, source_target_pairs={{0,2},{1,3},{2,0},{3,1},{4,6},{5,7},{6,4},{7,5},{8,10},{9,11},{10,... | collective-permute-start | bytes 884744 | tf_op jit(solution)/shard_map/ppermute | solution.py:1492
  163.8 23.7 %collective-permute-start.32 = (bf16[4,24,1024]{2,1,0:T(8,128)(2,1)S(1)}, bf16[4,24,1024]{2,1,0:T(8,128)(2,1)S(1)}, u32[]{:S(2)}, u32[]{:S(2)}) collective-permute-start(bf16[4,24,1024]{2,1,0:T(8,128)(2,1)S(1)} %bitcast.230), channel_id=1, source_target_pairs={{0,1},{1,0},{2,3},{3,2},{4,5},{5,4},{6,7},{7,6},{8,9},{9,8},{10,11... | collective-permute-start | bytes 589832 | tf_op jit(solution)/shard_map/ppermute | solution.py:1492
  199.5 11.8 %collective-permute-start.35 = (bf16[8,24,1024]{2,1,0:T(8,128)(2,1)}, bf16[8,24,1024]{2,1,0:T(8,128)(2,1)S(1)}, u32[]{:S(2)}, u32[]{:S(2)}) collective-permute-start(bf16[8,24,1024]{2,1,0:T(8,128)(2,1)} %bitcast.92), channel_id=1, source_target_pairs={{0,1},{1,0},{2,3},{3,2},{4,5},{5,4},{6,7},{7,6},{8,9},{9,8},{10,11... | collective-permute-start | bytes 1179656 | tf_op jit(solution)/shard_map/ppermute | solution.py:1492
  200.2 11.0 %collective-permute-start.37 = (bf16[4,24,1536]{2,1,0:T(8,128)(2,1)}, bf16[4,24,1536]{2,1,0:T(8,128)(2,1)S(1)}, u32[]{:S(2)}, u32[]{:S(2)}) collective-permute-start(bf16[4,24,1536]{2,1,0:T(8,128)(2,1)} %bitcast.89), channel_id=1, source_target_pairs={{0,2},{1,3},{2,0},{3,1},{4,6},{5,7},{6,4},{7,5},{8,10},{9,11},{10,... | collective-permute-start | bytes 884744 | tf_op jit(solution)/shard_map/ppermute | solution.py:1492
  202.0 8.6 %collective-permute-start.36 = (bf16[2,24,2560]{2,1,0:T(8,128)(2,1)}, bf16[2,24,2560]{2,1,0:T(8,128)(2,1)S(1)}, u32[]{:S(2)}, u32[]{:S(2)}) collective-permute-start(bf16[2,24,2560]{2,1,0:T(8,128)(2,1)} %bitcast.86), channel_id=1, source_target_pairs={{0,4},{1,5},{2,6},{3,7},{4,0},{5,1},{6,2},{7,3},{8,12},{9,13},{10,... | collective-permute-start | bytes 737288 | tf_op jit(solution)/shard_map/ppermute | solution.py:1492
  211.3 22.1 %collective-permute-start.42 = (f32[512,384]{1,0:T(8,128)}, f32[512,384]{1,0:T(8,128)S(1)}, u32[]{:S(2)}, u32[]{:S(2)}) collective-permute-start(f32[512,384]{1,0:T(8,128)} %get-tuple-element.300), channel_id=1, source_target_pairs={{0,16},{16,0},{1,17},{17,1},{2,18},{18,2},{3,19},{19,3},{4,20},{20... | collective-permute-start | bytes 2359304 | tf_op jit(solution)/shard_map/ppermute | solution.py:1477
  212.1 8.2 %collective-permute-start.38 = (bf16[4,24,1024]{2,1,0:T(8,128)(2,1)S(1)}, bf16[4,24,1024]{2,1,0:T(8,128)(2,1)S(1)}, u32[]{:S(2)}, u32[]{:S(2)}) collective-permute-start(bf16[4,24,1024]{2,1,0:T(8,128)(2,1)S(1)} %bitcast.231), channel_id=1, source_target_pairs={{0,2},{1,3},{2,0},{3,1},{4,6},{5,7},{6,4},{7,5},{8,10},{9,11},{10,... | collective-permute-start | bytes 589832 | tf_op jit(solution)/shard_map/ppermute | solution.py:1492
  222.0 8.9 %collective-permute-start.40 = (bf16[2,24,2560]{2,1,0:T(8,128)(2,1)S(1)}, bf16[2,24,2560]{2,1,0:T(8,128)(2,1)S(1)}, u32[]{:S(2)}, u32[]{:S(2)}) collective-permute-start(bf16[2,24,2560]{2,1,0:T(8,128)(2,1)S(1)} %bitcast.229), channel_id=1, source_target_pairs={{0,4},{1,5},{2,6},{3,7},{4,0},{5,1},{6,2},{7,3},{8,12},{9,13},{10,... | collective-permute-start | bytes 737288 | tf_op jit(solution)/shard_map/ppermute | solution.py:1492
  222.4 8.4 %collective-permute-start.41 = (bf16[64,768]{1,0:T(8,128)(2,1)S(1)}, bf16[64,768]{1,0:T(8,128)(2,1)S(1)}, u32[]{:S(2)}, u32[]{:S(2)}) collective-permute-start(bf16[64,768]{1,0:T(8,128)(2,1)S(1)} %shard_map.335.held), channel_id=1, source_target_pairs={{0,4},{1,5},{2,6},{3,7},{4,0},{5,1},{6,2},{7,3},{8,12},{9,13},{10,... | collective-permute-start | bytes 294920 | tf_op jit(solution)/shard_map/ppermute | solution.py:1492
  224.1 9.3 %collective-permute-start.43 = (bf16[8,2304]{1,0:T(8,128)(2,1)S(1)}, bf16[8,2304]{1,0:T(8,128)(2,1)S(1)}, u32[]{:S(2)}, u32[]{:S(2)}) collective-permute-start(bf16[8,2304]{1,0:T(8,128)(2,1)S(1)} %copy-done.42), channel_id=1, source_target_pairs={{0,16},{16,0},{1,17},{17,1},{2,18},{18,2},{3,19},{19,3},{4,20},{20... | collective-permute-start | bytes 110600 | tf_op jit(solution)/shard_map/ppermute | solution.py:1477
  233.4 12.0 %collective-permute-start.45 = (bf16[1,24,5120]{2,1,0:T(8,128)(2,1)S(1)}, bf16[1,24,5120]{2,1,0:T(8,128)(2,1)S(1)}, u32[]{:S(2)}, u32[]{:S(2)}) collective-permute-start(bf16[1,24,5120]{2,1,0:T(8,128)(2,1)S(1)} %bitcast.228), channel_id=1, source_target_pairs={{0,8},{1,9},{2,10},{3,11},{4,12},{5,13},{6,14},{7,15},{8,0},{9,1},... | collective-permute-start | bytes 737288 | tf_op jit(solution)/shard_map/ppermute | solution.py:1492
  (64 other events, 335.8 us)
Sparse Core Ops, SparseCore 0:
  130.4 63.4 all-gather.1

commit v5 on v4

--- a/solution.py
+++ b/solution.py
@@ -895,7 +895,7 @@
             gbu=((1, FF), f32),
             gbn=((1, D), f32),
         ),
-        5 * 10**9,
+        2 * 10**9,
         packed=in_kernel,
         after=after,
     )
@@ -1003,7 +1003,7 @@
             bias=((HALF, ROWS), f32),
             gw=((D, 2 * GROUP), f32),
         ),
-        7 * 10**9,
+        3 * 10**9,
         after=after,
     )
 
@@ -1046,7 +1046,7 @@
             perm_s=((ROWS, 3 * D), bf16),
             gmod=((8, 2 * D), f32),
         ),
-        2 * 10**9,
+        1 * 10**9,
         after=after,
     )
 
@@ -1236,7 +1236,6 @@
     above = blocks // below
     paired = lambda array: array.reshape((above, 2, below) + array.shape[1:])
     widths = [array.shape[2] for array in kept]
-    size = sum(array.size for array in kept)
     arrays = [paired(array) for array in kept] + [paired(array) for array, _ in came]
     shapes = [((above, below, rows, width), f32) for width in widths]
     shapes.append(((above, below, rows, sum(widths)), bf16))
@@ -1249,7 +1248,7 @@
         + [pltpu.VMEM(shape, kind) for shape, kind in shapes]
         + [pltpu.SemaphoreType.DMA((len(arrays),)), pltpu.SemaphoreType.DMA((len(shapes),))],
         compiler_params=pltpu.CompilerParams(vmem_limit_bytes=10 * 1024 * 1024),
-        cost_estimate=pl.CostEstimate(flops=size, bytes_accessed=8 * size, transcendentals=0),
+        cost_estimate=pl.CostEstimate(flops=10**5, bytes_accessed=10**5, transcendentals=0),
     )(*arrays, *after)
     count = len(kept)
     flat_blocks = [array.reshape((blocks,) + array.shape[2:]) for array in out]

time: 260 us -> 263 us (1.012)
    unnamed x91 -> x99, local copies, waits for them, and re-layouts: 18.3 us -> 20.6 us
  transfers between devices with their start and end apart: 52 -> 52, of which waited for: 17 -> 19; matrix products, arithmetic and copies ran while one was open for 1% -> 1% of each run, Pallas kernels for 27% -> 26%
where the time goes in v5:
time: 263 us; the launch traced here: 259 us
  Pallas kernels  112 us (43%)
  waiting for transfers between devices  63.4 us (24%)
  starting transfers between devices  45.5 us (17%)
  local copies, waits for them, and re-layouts  20.8 us (8%)
  between operations  15.1 us (6%)
    pallas_call x7, Pallas kernels, call(): pl.pallas_call(kernel, out_shape=[jax.ShapeDtypeStruct(shape, kind) for s...  88.2 us
    ppermute x35, waiting for transfers between devices, across(): return lax.ppermute(values, 'row', [(i, i ^ flips) for i in range(size)])  49.8 us
    ppermute x35, starting transfers between devices, across(): return lax.ppermute(values, 'row', [(i, i ^ flips) for i in range(size)])  42.7 us
    unnamed x99, local copies, waits for them, and re-layouts  20.6 us
    pallas_call x11, Pallas kernels, step(): pl.pallas_call(functools.partial(step_kernel, bit, widths, [count for _,...  13.2 us
    ppermute x16, waiting for transfers between devices, swap(): return lax.ppermute(values, 'section', [(0, 1), (1, 0)])  8.44 us
  transfers between devices with their start and end apart: 52, of which 19 were waited for; matrix products, arithmetic and copies ran while one was open for 1% of the time, Pallas kernels for 26%

profile of v5, /device:TPU:0, one launch (start us, length us, event | category | flops | bytes accessed | tf_op | source)
XLA Modules:
  0.0 258.6 jit_solution(8521972231692843113)
XLA Ops:
  7.2 1.9 shard_map.305
  9.1 4.0 %collective-permute-start = (bf16[1,4,384]{2,1,0:T(4,128)(2,1)}, bf16[1,4,384]{2,1,0:T(4,128)(2,1)S(1)}, u32[]{:S(2)}, u32[]{:S(2)}) collective-permute-start(bf16[1,4,384]{2,1,0:T(4,128)(2,1)} %get-tuple-element.175), channel_id=1, source_target_pairs={{0,8},{1,9},{2,10},{3,11},{4,12},{5,13},{6,14},{7,15},{8,0},{9,1},... | collective-permute-start | bytes 9224 | tf_op jit(solution)/shard_map/ppermute | solution.py:1491
  15.0 2.6 %collective-permute-start.9 = (bf16[1,1,1,1,96,384]{5,4,3,2,1,0:T(8,128)(2,1)}, bf16[1,1,1,1,96,384]{5,4,3,2,1,0:T(8,128)(2,1)S(1)}, u32[]{:S(2)}, u32[]{:S(2)}) collective-permute-start(bf16[1,1,1,1,96,384]{5,4,3,2,1,0:T(8,128)(2,1)} %bitcast.226), channel_id=1, source_target_pairs={{0,8},{1,9},{2,10},{3,11},{4,12},{5,13},{6,14},{7,15},{8,0},{9,1},... | collective-permute-start | bytes 221192 | tf_op jit(solution)/shard_map/ppermute | solution.py:1491
  22.3 5.9 %collective-permute-done.8 = bf16[1,1,1,1,24,896]{5,4,3,2,1,0:T(8,128)(2,1)S(1)} collective-permute-done((bf16[1,1,1,1,24,896]{5,4,3,2,1,0:T(8,128)(2,1)}, bf16[1,1,1,1,24,896]{5,4,3,2,1,0:T(8,128)(2,1)S(1)}, u32[]{:S(2)}, u32[]{:S(2)}) %collective-permute-start.8) | collective-permute-done | bytes 43040 | tf_op jit(solution)/shard_map/ppermute | solution.py:1491
  30.9 1.6 collective-permute-start.3
  32.5 1.9 collective-permute-start.12
  34.5 1.9 collective-permute-start.11
  36.4 5.7 %collective-permute-done.1 = bf16[2,4,384]{2,1,0:T(4,128)(2,1)S(1)} collective-permute-done((bf16[2,4,384]{2,1,0:T(4,128)(2,1)S(1)}, bf16[2,4,384]{2,1,0:T(4,128)(2,1)S(1)}, u32[]{:S(2)}, u32[]{:S(2)}) %collective-permute-start.1) | collective-permute-done | bytes 6176 | tf_op jit(solution)/shard_map/ppermute | solution.py:1491
  43.8 1.5 collective-permute-start.15
  46.4 4.1 %collective-permute-done.4 = f32[2,4,2304]{2,1,0:T(4,128)S(1)} collective-permute-done((f32[2,4,2304]{2,1,0:T(4,128)S(1)}, f32[2,4,2304]{2,1,0:T(4,128)S(1)}, u32[]{:S(2)}, u32[]{:S(2)}) %collective-permute-start.4) | collective-permute-done | bytes 73760 | tf_op jit(solution)/shard_map/ppermute | solution.py:1491
  51.8 3.8 %collective-permute-done.5.refs_6_ = f32[1,4,2304]{2,1,0:T(4,128)S(1)} collective-permute-done((f32[1,4,2304]{2,1,0:T(4,128)S(1)}, f32[1,4,2304]{2,1,0:T(4,128)S(1)}, u32[]{:S(2)}, u32[]{:S(2)}) %collective-permute-start.5) | collective-permute-done | bytes 36896 | tf_op jit(solution)/shard_map/ppermute | solution.py:1491
  58.4 1.8 collective-permute-start.17
  60.2 1.6 collective-permute-start.16
  63.4 5.1 %collective-permute-done.16 = bf16[2,2,1,2,24,768]{5,4,3,1,0,2:T(8,128)(2,1)} collective-permute-done((bf16[2,2,1,2,24,768]{5,4,3,1,0,2:T(8,128)(2,1)S(1)}, bf16[2,2,1,2,24,768]{5,4,3,1,0,2:T(8,128)(2,1)}, u32[]{:S(2)}, u32[]{:S(2)}) %collective-permute-start.16) | collective-permute-done | bytes 294944 | tf_op jit(solution)/shard_map/ppermute | solution.py:1491
  72.9 9.2 %shard_map.315 = (bf16[512,384]{1,0:T(8,128)(2,1)}, f32[512,1536]{1,0:T(8,128)}, f32[512,128]{1,0:T(8,128)}, f32[512,384]{1,0:T(8,128)}, f32[512,128]{1,0:T(8,12...) custom-call(s32[2,1]{1,0:T(2,128)} %copy.37.refs_0_, bf16[2,512,384]{2,1,0:T(8,128)(2,1)} %refs_6_.1, ...), custom_call_target="tpu_custom_call" | custom-call | flops 4000000000 | bytes 4194304 | tf_op jit(solution)/shard_map/pallas_call | solution.py:761
  87.9 4.4 %collective-permute-done.24.refs_12_.refs_16_ = bf16[1536,384]{1,0:T(8,128)(2,1)S(1)} collective-permute-done((bf16[1536,384]{1,0:T(8,128)(2,1)S(1)}, bf16[1536,384]{1,0:T(8,128)(2,1)S(1)}, u32[]{:S(2)}, u32[]{:S(2)}) %collective-permute-start.24) | collective-permute-done | bytes 1179680 | tf_op jit(solution)/shard_map/ppermute | solution.py:1476
  94.5 6.6 %shard_map.317 = (bf16[512,384]{1,0:T(8,128)(2,1)}, f32[512,384]{1,0:T(8,128)}, f32[512,384]{1,0:T(8,128)}) custom-call(s32[2,1]{1,0:T(2,128)} %copy.37.refs_0_, bf16[512,384]{1,0:T(8,128)(2,1)} %get-tuple-element.194.refs_4_.refs_1_.refs_13_, bf16[2,512,384]{2,1,0:T(8,128)(2,1)} %refs_6_.1, bf16[384,1920]{1,0:T(8,128)(2,1)} %bitcast.155, ...), custom_call_target="tpu_custom_call" | custom-call | flops 3000000000 | bytes 4194304 | tf_op jit(solution)/shard_map/pallas_call | solution.py:761
  101.1 31.9 %shard_map.318 = (bf16[512,384]{1,0:T(8,128)(2,1)}, bf16[512,384]{1,0:T(8,128)(2,1)}, f32[512,384]{1,0:T(8,128)}, f32[8,1536]{1,0:T(8,128)}, bf16[512,1664]{1,0:...) custom-call(s32[2,1]{1,0:T(2,128)} %copy.37.refs_0_, ...), custom_call_target="tpu_custom_call" | custom-call | flops 14000000000 | bytes 4194304 | tf_op jit(solution)/shard_map/pallas_call | solution.py:761
  133.9 6.4 %shard_map.319 = (f32[512,384]{1,0:T(8,128)}, bf16[512,384]{1,0:T(8,128)(2,1)}, bf16[8,2304]{1,0:T(8,128)(2,1)}, f32[8,768]{1,0:T(8,128)}) custom-call(s32[2,1]{1,0:T(2,128)} %copy.37.refs_0_, bf16[512,1664]{1,0:T(8,128)(2,1)} %get-tuple-element.204.refs_1_, bf16[384,768]{1,0:T(8,128)(2,1)} %bitcast.145, ...), custom_call_target="tpu_custom_call" | custom-call | flops 1000000000 | bytes 4194304 | tf_op jit(solution)/shard_map/pallas_call | solution.py:761
  143.7 2.4 collective-permute-start.29
  146.2 13.0 %shard_map.323 = (f32[512,384]{1,0:T(8,128)}, bf16[512,384]{1,0:T(8,128)(2,1)}, f32[384,384]{1,0:T(8,128)}, f32[8,1536]{1,0:T(8,128)}, f32[16,24,1536]{2,1,0:T(8,128)}, /*index=5*/bf16[16,24,1536]{2,1,0:T(8,128)(2,1)}) custom-call(s32[2,1]{1,0:T(2,128)} %copy.37.refs_0_, f32[4,2304]{1,0:T(4,128)} %copy-done.41, f32[4,2304]{1,0:T(4,128)} %copy-done.42, ...), custom_call_target="tpu_custom_call" | custom-call | flops 2000000000 | bytes 4194304 | tf_op jit(solution)/shard_map/pallas_call | solution.py:761
  167.5 15.2 %shard_map.327 = (bf16[512,1664]{1,0:T(8,128)(2,1)}, f32[384,1024]{1,0:T(8,128)}, bf16[384,1024]{1,0:T(8,128)(2,1)}, f32[8,384]{1,0:T(8,128)}) custom-call(s32[2,1]{1,0:T(2,128)} %copy.37.refs_0_, bf16[512,384]{1,0:T(8,128)(2,1)} %get-tuple-element.240.refs_1_, bf16[384,1920]{1,0:T(8,128)(2,1)} %bitcast.160, bf16[384,1920]{1,0:T(8,128)(2,1)} %copy-done.39, ...), custom_call_target="tpu_custom_call" | custom-call | flops 3000000000 | bytes 4194304 | tf_op jit(solution)/shard_map/pallas_call | solution.py:761
  182.8 7.2 %collective-permute-done.32 = bf16[4,24,1024]{2,1,0:T(8,128)(2,1)S(1)} collective-permute-done((bf16[4,24,1024]{2,1,0:T(8,128)(2,1)S(1)}, bf16[4,24,1024]{2,1,0:T(8,128)(2,1)S(1)}, u32[]{:S(2)}, u32[]{:S(2)}) %collective-permute-start.32) | collective-permute-done | bytes 196640 | tf_op jit(solution)/shard_map/ppermute | solution.py:1491
  191.3 5.1 %all-gather.2.cloned.1.call-done.ada = bf16[384,2304]{1,0:T(8,128)(2,1)} async-done(((bf16[24,2304]{1,0:T(8,128)(2,1)}), bf16[384,2304]{1,0:T(8,128)(2,1)}) %all-gather.2.cloned.1.call-update) | async-done | bytes 1769488 | tf_op jit(solution)/shard_map/all_gather | solution.py:1588
  202.6 2.0 collective-permute-start.37
  205.5 5.8 %shard_map.331 = (f32[512,384]{1,0:T(8,128)}, bf16[512,384]{1,0:T(8,128)(2,1)}, bf16[8,2304]{1,0:T(8,128)(2,1)}, f32[8,768]{1,0:T(8,128)}, f32[512,384]{1,0:T(8,...) custom-call(s32[2,1]{1,0:T(2,128)} %copy.37.refs_0_, bf16[512,1664]{1,0:T(8,128)(2,1)} %get-tuple-element.267.refs_1_, ...), custom_call_target="tpu_custom_call" | custom-call | flops 1000000000 | bytes 4194304 | tf_op jit(solution)/shard_map/pallas_call | solution.py:761
  215.8 1.9 collective-permute-start.39
  217.7 4.9 %collective-permute-done.39.arrived = bf16[48,768]{1,0:T(8,128)(2,1)S(1)} collective-permute-done((bf16[48,768]{1,0:T(8,128)(2,1)S(1)}, bf16[48,768]{1,0:T(8,128)(2,1)S(1)}, u32[]{:S(2)}, u32[]{:S(2)}) %collective-permute-start.39) | collective-permute-done | bytes 73760 | tf_op jit(solution)/shard_map/ppermute | solution.py:1491
  224.6 1.7 collective-permute-start.41
  226.2 7.1 %collective-permute-done.41.arrived = bf16[64,768]{1,0:T(8,128)(2,1)S(1)} collective-permute-done((bf16[64,768]{1,0:T(8,128)(2,1)S(1)}, bf16[64,768]{1,0:T(8,128)(2,1)S(1)}, u32[]{:S(2)}, u32[]{:S(2)}) %collective-permute-start.41) | collective-permute-done | bytes 98336 | tf_op jit(solution)/shard_map/ppermute | solution.py:1491
  233.3 2.4 shard_map.336
  245.7 2.4 collective-permute-done.45.refs_4_
  (221 shorter events, 70.4 us)
Async XLA Ops:
  7.2 189.3 %all-gather.2.cloned.1.call-start = ((), (), s32[]{:S(2)}) async-start(), calls=%async_computation | async-start | bytes 1880064 | tf_op jit(solution)/shard_map/all_gather | solution.py:1588
  9.1 12.2 %collective-permute-start = (bf16[1,4,384]{2,1,0:T(4,128)(2,1)}, bf16[1,4,384]{2,1,0:T(4,128)(2,1)S(1)}, u32[]{:S(2)}, u32[]{:S(2)}) collective-permute-start(bf16[1,4,384]{2,1,0:T(4,128)(2,1)} %get-tuple-element.175), channel_id=1, source_target_pairs={{0,8},{1,9},{2,10},{3,11},{4,12},{5,13},{6,14},{7,15},{8,0},{9,1},... | collective-permute-start | bytes 9224 | tf_op jit(solution)/shard_map/ppermute | solution.py:1491
  13.2 8.2 %collective-permute-start.2 = (bf16[1,1,1,1,24,2304]{5,4,3,2,1,0:T(8,128)(2,1)}, bf16[1,1,1,1,24,2304]{5,4,3,2,1,0:T(8,128)(2,1)S(1)}, u32[]{:S(2)}, u32[]{:S(2)}) collective-permute-start(bf16[1,1,1,1,24,2304]{5,4,3,2,1,0:T(8,128)(2,1)} %bitcast.218), channel_id=1, source_target_pairs={{0,1},{1,0},{2,3},{3,2},{4,5},{5,4},{6,7},{7,6},{8,9},{9,8},{10,11... | collective-permute-start | bytes 331784 | tf_op jit(solution)/shard_map/ppermute | solution.py:1491
  14.7 13.5 %collective-permute-start.7 = (bf16[1,1,1,1,24,2688]{5,4,3,2,1,0:T(8,128)(2,1)}, bf16[1,1,1,1,24,2688]{5,4,3,2,1,0:T(8,128)(2,1)S(1)}, u32[]{:S(2)}, u32[]{:S(2)}) collective-permute-start(bf16[1,1,1,1,24,2688]{5,4,3,2,1,0:T(8,128)(2,1)} %bitcast.215), channel_id=1, source_target_pairs={{0,8},{1,9},{2,10},{3,11},{4,12},{5,13},{6,14},{7,15},{8,0},{9,1},... | collective-permute-start | bytes 387080 | tf_op jit(solution)/shard_map/ppermute | solution.py:1491
  15.0 13.2 %collective-permute-start.9 = (bf16[1,1,1,1,96,384]{5,4,3,2,1,0:T(8,128)(2,1)}, bf16[1,1,1,1,96,384]{5,4,3,2,1,0:T(8,128)(2,1)S(1)}, u32[]{:S(2)}, u32[]{:S(2)}) collective-permute-start(bf16[1,1,1,1,96,384]{5,4,3,2,1,0:T(8,128)(2,1)} %bitcast.226), channel_id=1, source_target_pairs={{0,8},{1,9},{2,10},{3,11},{4,12},{5,13},{6,14},{7,15},{8,0},{9,1},... | collective-permute-start | bytes 221192 | tf_op jit(solution)/shard_map/ppermute | solution.py:1491
  17.6 10.6 %collective-permute-start.8 = (bf16[1,1,1,1,24,896]{5,4,3,2,1,0:T(8,128)(2,1)}, bf16[1,1,1,1,24,896]{5,4,3,2,1,0:T(8,128)(2,1)S(1)}, u32[]{:S(2)}, u32[]{:S(2)}) collective-permute-start(bf16[1,1,1,1,24,896]{5,4,3,2,1,0:T(8,128)(2,1)} %bitcast.231), channel_id=1, source_target_pairs={{0,8},{1,9},{2,10},{3,11},{4,12},{5,13},{6,14},{7,15},{8,0},{9,1},... | collective-permute-start | bytes 129032 | tf_op jit(solution)/shard_map/ppermute | solution.py:1491
  30.8 12.3 %collective-permute-start.10 = (bf16[2,1,1,1,24,2688]{5,4,0,3,2,1:T(8,128)(2,1)S(1)}, bf16[2,1,1,1,24,2688]{5,4,0,3,2,1:T(8,128)(2,1)S(1)}, u32[]{:S(2)}, u32[]{:S(2)}) collective-permute-start(bf16[2,1,1,1,24,2688]{5,4,0,3,2,1:T(8,128)(2,1)S(1)} %bitcast.197), channel_id=1, source_target_pairs={{0,4},{1,5},{2,6},{3,7},{4,0},{5,1},{6,2},{7,3},{8,12},{9,13},{10,... | collective-permute-start | bytes 774152 | tf_op jit(solution)/shard_map/ppermute | solution.py:1491
  30.9 11.3 %collective-permute-start.3 = (bf16[1,1,1,2,24,2304]{5,4,3,2,1,0:T(8,128)(2,1)S(1)}, bf16[1,1,1,2,24,2304]{5,4,3,2,1,0:T(8,128)(2,1)S(1)}, u32[]{:S(2)}, u32[]{:S(2)}) collective-permute-start(bf16[1,1,1,2,24,2304]{5,4,3,2,1,0:T(8,128)(2,1)S(1)} %bitcast.148), channel_id=1, source_target_pairs={{0,2},{1,3},{2,0},{3,1},{4,6},{5,7},{6,4},{7,5},{8,10},{9,11},{10,... | collective-permute-start | bytes 663560 | tf_op jit(solution)/shard_map/ppermute | solution.py:1491
  32.5 10.6 %collective-permute-start.12 = (bf16[2,1,1,1,96,384]{5,4,0,3,2,1:T(8,128)(2,1)S(1)}, bf16[2,1,1,1,96,384]{5,4,0,3,2,1:T(8,128)(2,1)S(1)}, u32[]{:S(2)}, u32[]{:S(2)}) collective-permute-start(bf16[2,1,1,1,96,384]{5,4,0,3,2,1:T(8,128)(2,1)S(1)} %bitcast.210), channel_id=1, source_target_pairs={{0,4},{1,5},{2,6},{3,7},{4,0},{5,1},{6,2},{7,3},{8,12},{9,13},{10,... | collective-permute-start | bytes 442376 | tf_op jit(solution)/shard_map/ppermute | solution.py:1491
  34.5 8.6 %collective-permute-start.11 = (bf16[2,1,1,1,24,896]{5,4,0,3,2,1:T(8,128)(2,1)S(1)}, bf16[2,1,1,1,24,896]{5,4,0,3,2,1:T(8,128)(2,1)S(1)}, u32[]{:S(2)}, u32[]{:S(2)}) collective-permute-start(bf16[2,1,1,1,24,896]{5,4,0,3,2,1:T(8,128)(2,1)S(1)} %bitcast.223), channel_id=1, source_target_pairs={{0,4},{1,5},{2,6},{3,7},{4,0},{5,1},{6,2},{7,3},{8,12},{9,13},{10,... | collective-permute-start | bytes 258056 | tf_op jit(solution)/shard_map/ppermute | solution.py:1491
  43.2 12.4 %collective-permute-start.13 = (bf16[2,2,1,1,24,2688]{5,4,1,0,3,2:T(8,128)(2,1)S(1)}, bf16[2,2,1,1,24,2688]{5,4,1,0,3,2:T(8,128)(2,1)S(1)}, u32[]{:S(2)}, u32[]{:S(2)}) collective-permute-start(bf16[2,2,1,1,24,2688]{5,4,1,0,3,2:T(8,128)(2,1)S(1)} %bitcast.181), channel_id=1, source_target_pairs={{0,1},{1,0},{2,3},{3,2},{4,5},{5,4},{6,7},{7,6},{8,9},{9,8},{10,11... | collective-permute-start | bytes 1548296 | tf_op jit(solution)/shard_map/ppermute | solution.py:1491
  43.8 11.8 %collective-permute-start.15 = (bf16[2,2,1,1,96,384]{5,4,1,0,3,2:T(8,128)(2,1)S(1)}, bf16[2,2,1,1,96,384]{5,4,1,0,3,2:T(8,128)(2,1)S(1)}, u32[]{:S(2)}, u32[]{:S(2)}) collective-permute-start(bf16[2,2,1,1,96,384]{5,4,1,0,3,2:T(8,128)(2,1)S(1)} %bitcast.191), channel_id=1, source_target_pairs={{0,2},{1,3},{2,0},{3,1},{4,6},{5,7},{6,4},{7,5},{8,10},{9,11},{10,... | collective-permute-start | bytes 884744 | tf_op jit(solution)/shard_map/ppermute | solution.py:1491
  45.4 10.2 %collective-permute-start.14 = (bf16[2,2,1,1,24,896]{5,4,1,0,3,2:T(8,128)(2,1)S(1)}, bf16[2,2,1,1,24,896]{5,4,1,0,3,2:T(8,128)(2,1)S(1)}, u32[]{:S(2)}, u32[]{:S(2)}) collective-permute-start(bf16[2,2,1,1,24,896]{5,4,1,0,3,2:T(8,128)(2,1)S(1)} %bitcast.207), channel_id=1, source_target_pairs={{0,2},{1,3},{2,0},{3,1},{4,6},{5,7},{6,4},{7,5},{8,10},{9,11},{10,... | collective-permute-start | bytes 516104 | tf_op jit(solution)/shard_map/ppermute | solution.py:1491
  58.4 10.0 %collective-permute-start.17 = (bf16[2,2,2,1,24,896]{5,4,2,1,0,3:T(8,128)(2,1)S(1)}, bf16[2,2,2,1,24,896]{5,4,2,1,0,3:T(8,128)(2,1)}, u32[]{:S(2)}, u32[]{:S(2)}) collective-permute-start(bf16[2,2,2,1,24,896]{5,4,2,1,0,3:T(8,128)(2,1)S(1)} %bitcast.188), channel_id=1, source_target_pairs={{0,1},{1,0},{2,3},{3,2},{4,5},{5,4},{6,7},{7,6},{8,9},{9,8},{10,11... | collective-permute-start | bytes 1032200 | tf_op jit(solution)/shard_map/ppermute | solution.py:1491
  60.2 8.2 %collective-permute-start.16 = (bf16[2,2,1,2,24,768]{5,4,3,1,0,2:T(8,128)(2,1)S(1)}, bf16[2,2,1,2,24,768]{5,4,3,1,0,2:T(8,128)(2,1)}, u32[]{:S(2)}, u32[]{:S(2)}) collective-permute-start(bf16[2,2,1,2,24,768]{5,4,3,1,0,2:T(8,128)(2,1)S(1)} %slice.8), channel_id=1, source_target_pairs={{0,2},{1,3},{2,0},{3,1},{4,6},{5,7},{6,4},{7,5},{8,10},{9,11},{10,... | collective-permute-start | bytes 884744 | tf_op jit(solution)/shard_map/ppermute | solution.py:1491
  61.8 8.4 %collective-permute-start.20 = (f32[8,1536]{1,0:T(8,128)S(1)}, f32[8,1536]{1,0:T(8,128)}, u32[]{:S(2)}, u32[]{:S(2)}) collective-permute-start(f32[8,1536]{1,0:T(8,128)S(1)} %shard_map.310.refs_6_.refs_8_.refs_7_.refs_3_.refs_9_), channel_id=1, source_target_pairs={{0,16},{16,0},{1,17},{17,1},{2,18},{18,2},{3,19},{19,3},{4,20},{20... | collective-permute-start | bytes 147464 | tf_op jit(solution)/shard_map/ppermute | solution.py:1476
  62.5 20.3 %collective-permute-start.21 = (bf16[2,2,1,2,24,1920]{5,4,3,1,0,2:T(8,128)(2,1)S(1)}, bf16[2,2,1,2,24,1920]{5,4,3,1,0,2:T(8,128)(2,1)S(1)}, u32[]{:S(2)}, u32[]{:S(2)}) collective-permute-start(bf16[2,2,1,2,24,1920]{5,4,3,1,0,2:T(8,128)(2,1)S(1)} %slice.9), channel_id=1, source_target_pairs={{0,2},{1,3},{2,0},{3,1},{4,6},{5,7},{6,4},{7,5},{8,10},{9,11},{10,... | collective-permute-start | bytes 2211848 | tf_op jit(solution)/shard_map/ppermute | solution.py:1491
  63.1 19.0 %collective-permute-start.22 = (bf16[2,2,2,1,96,384]{5,4,2,1,0,3:T(8,128)(2,1)}, bf16[2,2,2,1,96,384]{5,4,2,1,0,3:T(8,128)(2,1)}, u32[]{:S(2)}, u32[]{:S(2)}) collective-permute-start(bf16[2,2,2,1,96,384]{5,4,2,1,0,3:T(8,128)(2,1)} %bitcast.57), channel_id=1, source_target_pairs={{0,1},{1,0},{2,3},{3,2},{4,5},{5,4},{6,7},{7,6},{8,9},{9,8},{10,11... | collective-permute-start | bytes 1769480 | tf_op jit(solution)/shard_map/ppermute | solution.py:1491
  143.4 15.8 %collective-permute-start.28 = (bf16[8,24,1536]{2,1,0:T(8,128)(2,1)S(1)}, bf16[8,24,1536]{2,1,0:T(8,128)(2,1)S(1)}, u32[]{:S(2)}, u32[]{:S(2)}) collective-permute-start(bf16[8,24,1536]{2,1,0:T(8,128)(2,1)S(1)} %bitcast.234), channel_id=1, source_target_pairs={{0,1},{1,0},{2,3},{3,2},{4,5},{5,4},{6,7},{7,6},{8,9},{9,8},{10,11... | collective-permute-start | bytes 1769480 | tf_op jit(solution)/shard_map/ppermute | solution.py:1491
  143.7 15.5 %collective-permute-start.29 = (bf16[8,24,1024]{2,1,0:T(8,128)(2,1)S(1)}, bf16[8,24,1024]{2,1,0:T(8,128)(2,1)S(1)}, u32[]{:S(2)}, u32[]{:S(2)}) collective-permute-start(bf16[8,24,1024]{2,1,0:T(8,128)(2,1)S(1)} %bitcast.235), channel_id=1, source_target_pairs={{0,2},{1,3},{2,0},{3,1},{4,6},{5,7},{6,4},{7,5},{8,10},{9,11},{10,... | collective-permute-start | bytes 1179656 | tf_op jit(solution)/shard_map/ppermute | solution.py:1491
  163.8 32.7 %collective-permute-start.33 = (bf16[8,24,1536]{2,1,0:T(8,128)(2,1)}, bf16[8,24,1536]{2,1,0:T(8,128)(2,1)S(1)}, u32[]{:S(2)}, u32[]{:S(2)}) collective-permute-start(bf16[8,24,1536]{2,1,0:T(8,128)(2,1)} %bitcast.79), channel_id=1, source_target_pairs={{0,1},{1,0},{2,3},{3,2},{4,5},{5,4},{6,7},{7,6},{8,9},{9,8},{10,11... | collective-permute-start | bytes 1769480 | tf_op jit(solution)/shard_map/ppermute | solution.py:1491
  165.1 25.6 %collective-permute-start.31 = (bf16[4,24,1536]{2,1,0:T(8,128)(2,1)S(1)}, bf16[4,24,1536]{2,1,0:T(8,128)(2,1)S(1)}, u32[]{:S(2)}, u32[]{:S(2)}) collective-permute-start(bf16[4,24,1536]{2,1,0:T(8,128)(2,1)S(1)} %bitcast.236), channel_id=1, source_target_pairs={{0,2},{1,3},{2,0},{3,1},{4,6},{5,7},{6,4},{7,5},{8,10},{9,11},{10,... | collective-permute-start | bytes 884744 | tf_op jit(solution)/shard_map/ppermute | solution.py:1491
  166.2 23.7 %collective-permute-start.32 = (bf16[4,24,1024]{2,1,0:T(8,128)(2,1)S(1)}, bf16[4,24,1024]{2,1,0:T(8,128)(2,1)S(1)}, u32[]{:S(2)}, u32[]{:S(2)}) collective-permute-start(bf16[4,24,1024]{2,1,0:T(8,128)(2,1)S(1)} %bitcast.239), channel_id=1, source_target_pairs={{0,1},{1,0},{2,3},{3,2},{4,5},{5,4},{6,7},{7,6},{8,9},{9,8},{10,11... | collective-permute-start | bytes 589832 | tf_op jit(solution)/shard_map/ppermute | solution.py:1491
  202.1 11.8 %collective-permute-start.35 = (bf16[8,24,1024]{2,1,0:T(8,128)(2,1)}, bf16[8,24,1024]{2,1,0:T(8,128)(2,1)S(1)}, u32[]{:S(2)}, u32[]{:S(2)}) collective-permute-start(bf16[8,24,1024]{2,1,0:T(8,128)(2,1)} %bitcast.92), channel_id=1, source_target_pairs={{0,1},{1,0},{2,3},{3,2},{4,5},{5,4},{6,7},{7,6},{8,9},{9,8},{10,11... | collective-permute-start | bytes 1179656 | tf_op jit(solution)/shard_map/ppermute | solution.py:1491
  202.6 10.3 %collective-permute-start.37 = (bf16[4,24,1536]{2,1,0:T(8,128)(2,1)}, bf16[4,24,1536]{2,1,0:T(8,128)(2,1)S(1)}, u32[]{:S(2)}, u32[]{:S(2)}) collective-permute-start(bf16[4,24,1536]{2,1,0:T(8,128)(2,1)} %bitcast.89), channel_id=1, source_target_pairs={{0,2},{1,3},{2,0},{3,1},{4,6},{5,7},{6,4},{7,5},{8,10},{9,11},{10,... | collective-permute-start | bytes 884744 | tf_op jit(solution)/shard_map/ppermute | solution.py:1491
  204.6 8.3 %collective-permute-start.36 = (bf16[2,24,2560]{2,1,0:T(8,128)(2,1)}, bf16[2,24,2560]{2,1,0:T(8,128)(2,1)S(1)}, u32[]{:S(2)}, u32[]{:S(2)}) collective-permute-start(bf16[2,24,2560]{2,1,0:T(8,128)(2,1)} %bitcast.86), channel_id=1, source_target_pairs={{0,4},{1,5},{2,6},{3,7},{4,0},{5,1},{6,2},{7,3},{8,12},{9,13},{10,... | collective-permute-start | bytes 737288 | tf_op jit(solution)/shard_map/ppermute | solution.py:1491
  213.9 21.9 %collective-permute-start.42 = (f32[512,384]{1,0:T(8,128)}, f32[512,384]{1,0:T(8,128)S(1)}, u32[]{:S(2)}, u32[]{:S(2)}) collective-permute-start(f32[512,384]{1,0:T(8,128)} %get-tuple-element.300), channel_id=1, source_target_pairs={{0,16},{16,0},{1,17},{17,1},{2,18},{18,2},{3,19},{19,3},{4,20},{20... | collective-permute-start | bytes 2359304 | tf_op jit(solution)/shard_map/ppermute | solution.py:1476
  214.7 7.9 %collective-permute-start.38 = (bf16[4,24,1024]{2,1,0:T(8,128)(2,1)S(1)}, bf16[4,24,1024]{2,1,0:T(8,128)(2,1)S(1)}, u32[]{:S(2)}, u32[]{:S(2)}) collective-permute-start(bf16[4,24,1024]{2,1,0:T(8,128)(2,1)S(1)} %bitcast.240), channel_id=1, source_target_pairs={{0,2},{1,3},{2,0},{3,1},{4,6},{5,7},{6,4},{7,5},{8,10},{9,11},{10,... | collective-permute-start | bytes 589832 | tf_op jit(solution)/shard_map/ppermute | solution.py:1491
  224.1 9.2 %collective-permute-start.40 = (bf16[2,24,2560]{2,1,0:T(8,128)(2,1)S(1)}, bf16[2,24,2560]{2,1,0:T(8,128)(2,1)S(1)}, u32[]{:S(2)}, u32[]{:S(2)}) collective-permute-start(bf16[2,24,2560]{2,1,0:T(8,128)(2,1)S(1)} %bitcast.238), channel_id=1, source_target_pairs={{0,4},{1,5},{2,6},{3,7},{4,0},{5,1},{6,2},{7,3},{8,12},{9,13},{10,... | collective-permute-start | bytes 737288 | tf_op jit(solution)/shard_map/ppermute | solution.py:1491
  224.6 8.7 %collective-permute-start.41 = (bf16[64,768]{1,0:T(8,128)(2,1)S(1)}, bf16[64,768]{1,0:T(8,128)(2,1)S(1)}, u32[]{:S(2)}, u32[]{:S(2)}) collective-permute-start(bf16[64,768]{1,0:T(8,128)(2,1)S(1)} %shard_map.335.held), channel_id=1, source_target_pairs={{0,4},{1,5},{2,6},{3,7},{4,0},{5,1},{6,2},{7,3},{8,12},{9,13},{10,... | collective-permute-start | bytes 294920 | tf_op jit(solution)/shard_map/ppermute | solution.py:1491
  226.2 9.5 %collective-permute-start.43 = (bf16[8,2304]{1,0:T(8,128)(2,1)S(1)}, bf16[8,2304]{1,0:T(8,128)(2,1)S(1)}, u32[]{:S(2)}, u32[]{:S(2)}) collective-permute-start(bf16[8,2304]{1,0:T(8,128)(2,1)S(1)} %copy-done.46), channel_id=1, source_target_pairs={{0,16},{16,0},{1,17},{17,1},{2,18},{18,2},{3,19},{19,3},{4,20},{20... | collective-permute-start | bytes 110600 | tf_op jit(solution)/shard_map/ppermute | solution.py:1476
  235.8 12.3 %collective-permute-start.45 = (bf16[1,24,5120]{2,1,0:T(8,128)(2,1)S(1)}, bf16[1,24,5120]{2,1,0:T(8,128)(2,1)S(1)}, u32[]{:S(2)}, u32[]{:S(2)}) collective-permute-start(bf16[1,24,5120]{2,1,0:T(8,128)(2,1)S(1)} %bitcast.237), channel_id=1, source_target_pairs={{0,8},{1,9},{2,10},{3,11},{4,12},{5,13},{6,14},{7,15},{8,0},{9,1},... | collective-permute-start | bytes 737288 | tf_op jit(solution)/shard_map/ppermute | solution.py:1491
  (68 other events, 326.0 us)
Sparse Core Ops, SparseCore 0:
  133.4 62.9 all-gather.1

commit v6 on v4

--- a/solution.py
+++ b/solution.py
@@ -1659,9 +1659,7 @@
     f2_came = partner(f2_sent, y_bits[-1])
     low, a1_keep, a1_sent, m1_sums = mixer_backward(0, layouts, smalls, saved, *carried, upo)
     a1_keep, a1_sent = by_row(a1_keep), by_row(a1_sent)
-    low, a1_sent, f2_came, a2_came, f1_came, ada_all = lock(
-        low, a1_sent, f2_came, a2_came, f1_came, ada_all
-    )
+    low, a1_sent, f2_came, a2_came, f1_came = lock(low, a1_sent, f2_came, a2_came, f1_came)
     a1_came = swap(a1_sent)
     two_keep, two_sent = run(f2_keep + a2_keep, [(f2_came, 1), (a2_came, 1)], z_bits[:1])
     f1_keep, f1_sent = run(f1_keep, [(f1_came, 1)], y_bits)
@@ -1674,8 +1672,8 @@
         0, low, mid_grad, f1_sums, m1_sums, (gx_two, mod_low_two)
     )
     misc = pack_misc(conds, mod_low_one, mod_low_two, sums_one, sums_two)
-    misc, a1_came, two_came, f1_came, gx_sent, mod_sent = lock(
-        misc, a1_came, two_came, f1_came, gx_sent, mod_sent
+    misc, a1_came, two_came, f1_came, gx_sent, mod_sent, ada_all = lock(
+        misc, a1_came, two_came, f1_came, gx_sent, mod_sent, ada_all
     )
 
     a1_keep, a1_sent = run(a1_keep, [(a1_came, 1)], y_bits)

time: 260 us -> 258 us (level)
  local copies, waits for them, and re-layouts: 18.5 us -> 14.5 us
  waiting for transfers between devices: 62.1 us -> 65 us
    all_gather x1, waiting for transfers between devices: 4.93 us -> 9.86 us  [on_device(): ada_all = lax.all_gather(late, 'row', axis=0, tiled=True)]
    unnamed x91 -> x81, local copies, waits for them, and re-layouts: 18.3 us -> 14.3 us
  transfers between devices with their start and end apart: 52 -> 52, of which waited for: 17 -> 18; matrix products, arithmetic and copies ran while one was open for 1% -> 1% of each run, Pallas kernels for 27% -> 26%
where the time goes in v6:
time: 258 us; the launch traced here: 254 us
  Pallas kernels  111 us (43%)
  waiting for transfers between devices  65 us (25%)
  starting transfers between devices  47.1 us (18%)
  between operations  15.1 us (6%)
  local copies, waits for them, and re-layouts  14.5 us (6%)
    pallas_call x7, Pallas kernels, call(): pl.pallas_call(kernel, out_shape=[jax.ShapeDtypeStruct(shape, kind) for s...  88.2 us
    ppermute x35, waiting for transfers between devices, across(): return lax.ppermute(values, 'row', [(i, i ^ flips) for i in range(size)])  46.2 us
    ppermute x35, starting transfers between devices, across(): return lax.ppermute(values, 'row', [(i, i ^ flips) for i in range(size)])  44.3 us
    unnamed x81, local copies, waits for them, and re-layouts  14.3 us
    pallas_call x11, Pallas kernels, step(): pl.pallas_call(functools.partial(step_kernel, bit, widths, [count for _,...  12.5 us
    all_gather x1, waiting for transfers between devices, on_device(): ada_all = lax.all_gather(late, 'row', axis=0, tiled=True)  9.86 us
    ppermute x16, waiting for transfers between devices, swap(): return lax.ppermute(values, 'section', [(0, 1), (1, 0)])  8.97 us
  transfers between devices with their start and end apart: 52, of which 18 were waited for; matrix products, arithmetic and copies ran while one was open for 1% of the time, Pallas kernels for 26%

profile of v6, /device:TPU:0, one launch (start us, length us, event | category | flops | bytes accessed | tf_op | source)
XLA Modules:
  0.0 253.9 jit_solution(5755367628103904338)
XLA Ops:
  7.2 1.9 shard_map.305
  9.1 4.0 %collective-permute-start = (bf16[1,4,384]{2,1,0:T(4,128)(2,1)}, bf16[1,4,384]{2,1,0:T(4,128)(2,1)S(1)}, u32[]{:S(2)}, u32[]{:S(2)}) collective-permute-start(bf16[1,4,384]{2,1,0:T(4,128)(2,1)} %get-tuple-element.175), channel_id=1, source_target_pairs={{0,8},{1,9},{2,10},{3,11},{4,12},{5,13},{6,14},{7,15},{8,0},{9,1},... | collective-permute-start | bytes 9224 | tf_op jit(solution)/shard_map/ppermute | solution.py:1492
  15.0 2.6 %collective-permute-start.9 = (bf16[1,1,1,1,96,384]{5,4,3,2,1,0:T(8,128)(2,1)}, bf16[1,1,1,1,96,384]{5,4,3,2,1,0:T(8,128)(2,1)S(1)}, u32[]{:S(2)}, u32[]{:S(2)}) collective-permute-start(bf16[1,1,1,1,96,384]{5,4,3,2,1,0:T(8,128)(2,1)} %bitcast.206), channel_id=1, source_target_pairs={{0,8},{1,9},{2,10},{3,11},{4,12},{5,13},{6,14},{7,15},{8,0},{9,1},... | collective-permute-start | bytes 221192 | tf_op jit(solution)/shard_map/ppermute | solution.py:1492
  22.3 5.9 %collective-permute-done.8 = bf16[1,1,1,1,24,896]{5,4,3,2,1,0:T(8,128)(2,1)S(1)} collective-permute-done((bf16[1,1,1,1,24,896]{5,4,3,2,1,0:T(8,128)(2,1)}, bf16[1,1,1,1,24,896]{5,4,3,2,1,0:T(8,128)(2,1)S(1)}, u32[]{:S(2)}, u32[]{:S(2)}) %collective-permute-start.8) | collective-permute-done | bytes 43040 | tf_op jit(solution)/shard_map/ppermute | solution.py:1492
  32.5 1.9 collective-permute-start.12
  34.5 1.9 collective-permute-start.11
  36.4 5.7 %collective-permute-done.1 = bf16[2,4,384]{2,1,0:T(4,128)(2,1)S(1)} collective-permute-done((bf16[2,4,384]{2,1,0:T(4,128)(2,1)S(1)}, bf16[2,4,384]{2,1,0:T(4,128)(2,1)S(1)}, u32[]{:S(2)}, u32[]{:S(2)}) %collective-permute-start.1) | collective-permute-done | bytes 6176 | tf_op jit(solution)/shard_map/ppermute | solution.py:1492
  46.4 4.1 %collective-permute-done.4 = f32[2,4,2304]{2,1,0:T(4,128)S(1)} collective-permute-done((f32[2,4,2304]{2,1,0:T(4,128)S(1)}, f32[2,4,2304]{2,1,0:T(4,128)S(1)}, u32[]{:S(2)}, u32[]{:S(2)}) %collective-permute-start.4) | collective-permute-done | bytes 73760 | tf_op jit(solution)/shard_map/ppermute | solution.py:1492
  51.8 3.8 %collective-permute-done.5.refs_6_ = f32[1,4,2304]{2,1,0:T(4,128)S(1)} collective-permute-done((f32[1,4,2304]{2,1,0:T(4,128)S(1)}, f32[1,4,2304]{2,1,0:T(4,128)S(1)}, u32[]{:S(2)}, u32[]{:S(2)}) %collective-permute-start.5) | collective-permute-done | bytes 36896 | tf_op jit(solution)/shard_map/ppermute | solution.py:1492
  61.8 6.3 %collective-permute-done.16 = bf16[2,2,1,2,24,768]{5,4,3,1,0,2:T(8,128)(2,1)} collective-permute-done((bf16[2,2,1,2,24,768]{5,4,3,1,0,2:T(8,128)(2,1)S(1)}, bf16[2,2,1,2,24,768]{5,4,3,1,0,2:T(8,128)(2,1)}, u32[]{:S(2)}, u32[]{:S(2)}) %collective-permute-start.16) | collective-permute-done | bytes 294944 | tf_op jit(solution)/shard_map/ppermute | solution.py:1492
  68.0 2.3 shard_map.314
  73.8 9.2 %shard_map.315 = (bf16[512,384]{1,0:T(8,128)(2,1)}, f32[512,1536]{1,0:T(8,128)}, f32[512,128]{1,0:T(8,128)}, f32[512,384]{1,0:T(8,128)}, f32[512,128]{1,0:T(8,12...) custom-call(s32[2,1]{1,0:T(2,128)} %copy.37.refs_0_, bf16[2,512,384]{2,1,0:T(8,128)(2,1)} %refs_6_.1, ...), custom_call_target="tpu_custom_call" | custom-call | flops 4000000000 | bytes 4194304 | tf_op jit(solution)/shard_map/pallas_call | solution.py:761
  84.8 4.4 %collective-permute-done.24.refs_12_.refs_16_ = bf16[1536,384]{1,0:T(8,128)(2,1)S(1)} collective-permute-done((bf16[1536,384]{1,0:T(8,128)(2,1)S(1)}, bf16[1536,384]{1,0:T(8,128)(2,1)S(1)}, u32[]{:S(2)}, u32[]{:S(2)}) %collective-permute-start.24) | collective-permute-done | bytes 1179680 | tf_op jit(solution)/shard_map/ppermute | solution.py:1477
  91.3 6.6 %shard_map.317 = (bf16[512,384]{1,0:T(8,128)(2,1)}, f32[512,384]{1,0:T(8,128)}, f32[512,384]{1,0:T(8,128)}) custom-call(s32[2,1]{1,0:T(2,128)} %copy.37.refs_0_, bf16[512,384]{1,0:T(8,128)(2,1)} %get-tuple-element.194.refs_4_.refs_1_.refs_13_, bf16[2,512,384]{2,1,0:T(8,128)(2,1)} %refs_6_.1, bf16[384,1920]{1,0:T(8,128)(2,1)} %bitcast.215, ...), custom_call_target="tpu_custom_call" | custom-call | flops 3000000000 | bytes 4194304 | tf_op jit(solution)/shard_map/pallas_call | solution.py:761
  97.9 31.9 %shard_map.318 = (bf16[512,384]{1,0:T(8,128)(2,1)}, bf16[512,384]{1,0:T(8,128)(2,1)}, f32[512,384]{1,0:T(8,128)}, f32[8,1536]{1,0:T(8,128)}, bf16[512,1664]{1,0:...) custom-call(s32[2,1]{1,0:T(2,128)} %copy.37.refs_0_, ...), custom_call_target="tpu_custom_call" | custom-call | flops 14000000000 | bytes 4194304 | tf_op jit(solution)/shard_map/pallas_call | solution.py:761
  130.6 6.4 %shard_map.319 = (f32[512,384]{1,0:T(8,128)}, bf16[512,384]{1,0:T(8,128)(2,1)}, bf16[8,2304]{1,0:T(8,128)(2,1)}, f32[8,768]{1,0:T(8,128)}) custom-call(s32[2,1]{1,0:T(2,128)} %copy.37.refs_0_, bf16[512,1664]{1,0:T(8,128)(2,1)} %get-tuple-element.204.refs_1_, bf16[384,768]{1,0:T(8,128)(2,1)} %bitcast.52.refs_4_.refs_2_, ...), custom_call_target="tpu_custom_call" | custom-call | flops 2000000000 | bytes 4194304 | tf_op jit(solution)/shard_map/pallas_call | solution.py:761
  141.0 2.7 %collective-permute-start.29 = (bf16[8,24,1024]{2,1,0:T(8,128)(2,1)}, bf16[8,24,1024]{2,1,0:T(8,128)(2,1)S(1)}, u32[]{:S(2)}, u32[]{:S(2)}) collective-permute-start(bf16[8,24,1024]{2,1,0:T(8,128)(2,1)} %bitcast.227), channel_id=1, source_target_pairs={{0,2},{1,3},{2,0},{3,1},{4,6},{5,7},{6,4},{7,5},{8,10},{9,11},{10,... | collective-permute-start | bytes 1179656 | tf_op jit(solution)/shard_map/ppermute | solution.py:1492
  143.6 13.0 %shard_map.323 = (f32[512,384]{1,0:T(8,128)}, bf16[512,384]{1,0:T(8,128)(2,1)}, f32[384,384]{1,0:T(8,128)}, f32[8,1536]{1,0:T(8,128)}, f32[16,24,1536]{2,1,0:T(8,128)}, /*index=5*/bf16[16,24,1536]{2,1,0:T(8,128)(2,1)}) custom-call(s32[2,1]{1,0:T(2,128)} %copy.37.refs_0_, f32[4,2304]{1,0:T(4,128)} %copy-done.30, f32[4,2304]{1,0:T(4,128)} %copy-done.36, ...), custom_call_target="tpu_custom_call" | custom-call | flops 5000000000 | bytes 4194304 | tf_op jit(solution)/shard_map/pallas_call | solution.py:761
  162.2 1.9 collective-permute-start.31
  165.4 15.3 %shard_map.327 = (bf16[512,1664]{1,0:T(8,128)(2,1)}, f32[384,1024]{1,0:T(8,128)}, bf16[384,1024]{1,0:T(8,128)(2,1)}, f32[8,384]{1,0:T(8,128)}) custom-call(s32[2,1]{1,0:T(2,128)} %copy.37.refs_0_, bf16[512,384]{1,0:T(8,128)(2,1)} %get-tuple-element.240.refs_1_, bf16[384,1920]{1,0:T(8,128)(2,1)} %bitcast.220, bf16[384,1920]{1,0:T(8,128)(2,1)} %copy-done.33, ...), custom_call_target="tpu_custom_call" | custom-call | flops 7000000000 | bytes 4194304 | tf_op jit(solution)/shard_map/pallas_call | solution.py:761
  180.7 2.9 %collective-permute-done.32 = bf16[4,24,1024]{2,1,0:T(8,128)(2,1)S(1)} collective-permute-done((bf16[4,24,1024]{2,1,0:T(8,128)(2,1)S(1)}, bf16[4,24,1024]{2,1,0:T(8,128)(2,1)S(1)}, u32[]{:S(2)}, u32[]{:S(2)}) %collective-permute-start.32) | collective-permute-done | bytes 196640 | tf_op jit(solution)/shard_map/ppermute | solution.py:1492
  188.6 1.9 collective-permute-start.37
  190.5 5.9 %shard_map.331 = (f32[512,384]{1,0:T(8,128)}, bf16[512,384]{1,0:T(8,128)(2,1)}, bf16[8,2304]{1,0:T(8,128)(2,1)}, f32[8,768]{1,0:T(8,128)}, f32[512,384]{1,0:T(8,...) custom-call(s32[2,1]{1,0:T(2,128)} %copy.37.refs_0_, bf16[512,1664]{1,0:T(8,128)(2,1)} %get-tuple-element.266.refs_1_, ...), custom_call_target="tpu_custom_call" | custom-call | flops 2000000000 | bytes 4194304 | tf_op jit(solution)/shard_map/pallas_call | solution.py:761
  197.9 9.9 %all-gather.2.cloned.1.call-done.ada = bf16[384,2304]{1,0:T(8,128)(2,1)} async-done(((bf16[24,2304]{1,0:T(8,128)(2,1)}), bf16[384,2304]{1,0:T(8,128)(2,1)}) %all-gather.2.cloned.1.call-update) | async-done | bytes 1769488 | tf_op jit(solution)/shard_map/all_gather | solution.py:1589
  209.7 1.8 collective-permute-start.39
  211.5 5.1 %collective-permute-done.39.arrived = bf16[48,768]{1,0:T(8,128)(2,1)S(1)} collective-permute-done((bf16[48,768]{1,0:T(8,128)(2,1)S(1)}, bf16[48,768]{1,0:T(8,128)(2,1)S(1)}, u32[]{:S(2)}, u32[]{:S(2)}) %collective-permute-start.39) | collective-permute-done | bytes 73760 | tf_op jit(solution)/shard_map/ppermute | solution.py:1492
  218.0 1.9 collective-permute-start.40
  220.1 7.8 %collective-permute-done.41.arrived = bf16[64,768]{1,0:T(8,128)(2,1)S(1)} collective-permute-done((bf16[64,768]{1,0:T(8,128)(2,1)S(1)}, bf16[64,768]{1,0:T(8,128)(2,1)S(1)}, u32[]{:S(2)}, u32[]{:S(2)}) %collective-permute-start.41) | collective-permute-done | bytes 98336 | tf_op jit(solution)/shard_map/ppermute | solution.py:1492
  227.9 2.4 shard_map.336
  230.4 2.0 collective-permute-start.45
  233.0 2.9 %collective-permute-start.48 = (bf16[96,768]{1,0:T(8,128)(2,1)S(1)}, bf16[96,768]{1,0:T(8,128)(2,1)S(1)}, u32[]{:S(2)}, u32[]{:S(2)}) collective-permute-start(bf16[96,768]{1,0:T(8,128)(2,1)S(1)} %shard_map.337.refs_5_), channel_id=1, source_target_pairs={{0,3},{1,2},{2,1},{3,0},{4,7},{5,6},{6,5},{7,4},{8,11},{9,10},{10,... | collective-permute-start | bytes 442376 | tf_op jit(solution)/shard_map/ppermute | solution.py:1492
  240.1 3.3 %collective-permute-done.45.refs_4_ = bf16[1,24,5120]{2,1,0:T(8,128)(2,1)S(1)} collective-permute-done((bf16[1,24,5120]{2,1,0:T(8,128)(2,1)S(1)}, bf16[1,24,5120]{2,1,0:T(8,128)(2,1)S(1)}, u32[]{:S(2)}, u32[]{:S(2)}) %collective-permute-start.45) | collective-permute-done | bytes 245792 | tf_op jit(solution)/shard_map/ppermute | solution.py:1492
  (203 shorter events, 59.4 us)
Async XLA Ops:
  7.2 200.6 %all-gather.2.cloned.1.call-start = ((), (), s32[]{:S(2)}) async-start(), calls=%async_computation | async-start | bytes 1880064 | tf_op jit(solution)/shard_map/all_gather | solution.py:1589
  9.1 12.2 %collective-permute-start = (bf16[1,4,384]{2,1,0:T(4,128)(2,1)}, bf16[1,4,384]{2,1,0:T(4,128)(2,1)S(1)}, u32[]{:S(2)}, u32[]{:S(2)}) collective-permute-start(bf16[1,4,384]{2,1,0:T(4,128)(2,1)} %get-tuple-element.175), channel_id=1, source_target_pairs={{0,8},{1,9},{2,10},{3,11},{4,12},{5,13},{6,14},{7,15},{8,0},{9,1},... | collective-permute-start | bytes 9224 | tf_op jit(solution)/shard_map/ppermute | solution.py:1492
  13.2 8.2 %collective-permute-start.2 = (bf16[1,1,1,1,24,2304]{5,4,3,2,1,0:T(8,128)(2,1)}, bf16[1,1,1,1,24,2304]{5,4,3,2,1,0:T(8,128)(2,1)S(1)}, u32[]{:S(2)}, u32[]{:S(2)}) collective-permute-start(bf16[1,1,1,1,24,2304]{5,4,3,2,1,0:T(8,128)(2,1)} %bitcast.198), channel_id=1, source_target_pairs={{0,1},{1,0},{2,3},{3,2},{4,5},{5,4},{6,7},{7,6},{8,9},{9,8},{10,11... | collective-permute-start | bytes 331784 | tf_op jit(solution)/shard_map/ppermute | solution.py:1492
  14.7 13.5 %collective-permute-start.7 = (bf16[1,1,1,1,24,2688]{5,4,3,2,1,0:T(8,128)(2,1)}, bf16[1,1,1,1,24,2688]{5,4,3,2,1,0:T(8,128)(2,1)S(1)}, u32[]{:S(2)}, u32[]{:S(2)}) collective-permute-start(bf16[1,1,1,1,24,2688]{5,4,3,2,1,0:T(8,128)(2,1)} %bitcast.195), channel_id=1, source_target_pairs={{0,8},{1,9},{2,10},{3,11},{4,12},{5,13},{6,14},{7,15},{8,0},{9,1},... | collective-permute-start | bytes 387080 | tf_op jit(solution)/shard_map/ppermute | solution.py:1492
  15.0 13.2 %collective-permute-start.9 = (bf16[1,1,1,1,96,384]{5,4,3,2,1,0:T(8,128)(2,1)}, bf16[1,1,1,1,96,384]{5,4,3,2,1,0:T(8,128)(2,1)S(1)}, u32[]{:S(2)}, u32[]{:S(2)}) collective-permute-start(bf16[1,1,1,1,96,384]{5,4,3,2,1,0:T(8,128)(2,1)} %bitcast.206), channel_id=1, source_target_pairs={{0,8},{1,9},{2,10},{3,11},{4,12},{5,13},{6,14},{7,15},{8,0},{9,1},... | collective-permute-start | bytes 221192 | tf_op jit(solution)/shard_map/ppermute | solution.py:1492
  17.6 10.6 %collective-permute-start.8 = (bf16[1,1,1,1,24,896]{5,4,3,2,1,0:T(8,128)(2,1)}, bf16[1,1,1,1,24,896]{5,4,3,2,1,0:T(8,128)(2,1)S(1)}, u32[]{:S(2)}, u32[]{:S(2)}) collective-permute-start(bf16[1,1,1,1,24,896]{5,4,3,2,1,0:T(8,128)(2,1)} %bitcast.211), channel_id=1, source_target_pairs={{0,8},{1,9},{2,10},{3,11},{4,12},{5,13},{6,14},{7,15},{8,0},{9,1},... | collective-permute-start | bytes 129032 | tf_op jit(solution)/shard_map/ppermute | solution.py:1492
  30.8 12.3 %collective-permute-start.10 = (bf16[2,1,1,1,24,2688]{5,4,0,3,2,1:T(8,128)(2,1)S(1)}, bf16[2,1,1,1,24,2688]{5,4,0,3,2,1:T(8,128)(2,1)S(1)}, u32[]{:S(2)}, u32[]{:S(2)}) collective-permute-start(bf16[2,1,1,1,24,2688]{5,4,0,3,2,1:T(8,128)(2,1)S(1)} %bitcast.177), channel_id=1, source_target_pairs={{0,4},{1,5},{2,6},{3,7},{4,0},{5,1},{6,2},{7,3},{8,12},{9,13},{10,... | collective-permute-start | bytes 774152 | tf_op jit(solution)/shard_map/ppermute | solution.py:1492
  30.9 11.3 %collective-permute-start.3 = (bf16[1,1,1,2,24,2304]{5,4,3,2,1,0:T(8,128)(2,1)S(1)}, bf16[1,1,1,2,24,2304]{5,4,3,2,1,0:T(8,128)(2,1)S(1)}, u32[]{:S(2)}, u32[]{:S(2)}) collective-permute-start(bf16[1,1,1,2,24,2304]{5,4,3,2,1,0:T(8,128)(2,1)S(1)} %bitcast.138), channel_id=1, source_target_pairs={{0,2},{1,3},{2,0},{3,1},{4,6},{5,7},{6,4},{7,5},{8,10},{9,11},{10,... | collective-permute-start | bytes 663560 | tf_op jit(solution)/shard_map/ppermute | solution.py:1492
  32.5 10.6 %collective-permute-start.12 = (bf16[2,1,1,1,96,384]{5,4,0,3,2,1:T(8,128)(2,1)S(1)}, bf16[2,1,1,1,96,384]{5,4,0,3,2,1:T(8,128)(2,1)S(1)}, u32[]{:S(2)}, u32[]{:S(2)}) collective-permute-start(bf16[2,1,1,1,96,384]{5,4,0,3,2,1:T(8,128)(2,1)S(1)} %bitcast.190), channel_id=1, source_target_pairs={{0,4},{1,5},{2,6},{3,7},{4,0},{5,1},{6,2},{7,3},{8,12},{9,13},{10,... | collective-permute-start | bytes 442376 | tf_op jit(solution)/shard_map/ppermute | solution.py:1492
  34.5 8.6 %collective-permute-start.11 = (bf16[2,1,1,1,24,896]{5,4,0,3,2,1:T(8,128)(2,1)S(1)}, bf16[2,1,1,1,24,896]{5,4,0,3,2,1:T(8,128)(2,1)S(1)}, u32[]{:S(2)}, u32[]{:S(2)}) collective-permute-start(bf16[2,1,1,1,24,896]{5,4,0,3,2,1:T(8,128)(2,1)S(1)} %bitcast.203), channel_id=1, source_target_pairs={{0,4},{1,5},{2,6},{3,7},{4,0},{5,1},{6,2},{7,3},{8,12},{9,13},{10,... | collective-permute-start | bytes 258056 | tf_op jit(solution)/shard_map/ppermute | solution.py:1492
  43.2 12.4 %collective-permute-start.13 = (bf16[2,2,1,1,24,2688]{5,4,1,0,3,2:T(8,128)(2,1)S(1)}, bf16[2,2,1,1,24,2688]{5,4,1,0,3,2:T(8,128)(2,1)S(1)}, u32[]{:S(2)}, u32[]{:S(2)}) collective-permute-start(bf16[2,2,1,1,24,2688]{5,4,1,0,3,2:T(8,128)(2,1)S(1)} %bitcast.161), channel_id=1, source_target_pairs={{0,1},{1,0},{2,3},{3,2},{4,5},{5,4},{6,7},{7,6},{8,9},{9,8},{10,11... | collective-permute-start | bytes 1548296 | tf_op jit(solution)/shard_map/ppermute | solution.py:1492
  43.8 11.8 %collective-permute-start.15 = (bf16[2,2,1,1,96,384]{5,4,1,0,3,2:T(8,128)(2,1)S(1)}, bf16[2,2,1,1,96,384]{5,4,1,0,3,2:T(8,128)(2,1)S(1)}, u32[]{:S(2)}, u32[]{:S(2)}) collective-permute-start(bf16[2,2,1,1,96,384]{5,4,1,0,3,2:T(8,128)(2,1)S(1)} %bitcast.171), channel_id=1, source_target_pairs={{0,2},{1,3},{2,0},{3,1},{4,6},{5,7},{6,4},{7,5},{8,10},{9,11},{10,... | collective-permute-start | bytes 884744 | tf_op jit(solution)/shard_map/ppermute | solution.py:1492
  45.4 10.2 %collective-permute-start.14 = (bf16[2,2,1,1,24,896]{5,4,1,0,3,2:T(8,128)(2,1)S(1)}, bf16[2,2,1,1,24,896]{5,4,1,0,3,2:T(8,128)(2,1)S(1)}, u32[]{:S(2)}, u32[]{:S(2)}) collective-permute-start(bf16[2,2,1,1,24,896]{5,4,1,0,3,2:T(8,128)(2,1)S(1)} %bitcast.187), channel_id=1, source_target_pairs={{0,2},{1,3},{2,0},{3,1},{4,6},{5,7},{6,4},{7,5},{8,10},{9,11},{10,... | collective-permute-start | bytes 516104 | tf_op jit(solution)/shard_map/ppermute | solution.py:1492
  57.4 10.6 %collective-permute-start.17 = (bf16[2,2,2,1,24,896]{5,4,2,1,0,3:T(8,128)(2,1)}, bf16[2,2,2,1,24,896]{5,4,2,1,0,3:T(8,128)(2,1)}, u32[]{:S(2)}, u32[]{:S(2)}) collective-permute-start(bf16[2,2,2,1,24,896]{5,4,2,1,0,3:T(8,128)(2,1)} %bitcast.50), channel_id=1, source_target_pairs={{0,1},{1,0},{2,3},{3,2},{4,5},{5,4},{6,7},{7,6},{8,9},{9,8},{10,11... | collective-permute-start | bytes 1032200 | tf_op jit(solution)/shard_map/ppermute | solution.py:1492
  59.2 8.8 %collective-permute-start.16 = (bf16[2,2,1,2,24,768]{5,4,3,1,0,2:T(8,128)(2,1)S(1)}, bf16[2,2,1,2,24,768]{5,4,3,1,0,2:T(8,128)(2,1)}, u32[]{:S(2)}, u32[]{:S(2)}) collective-permute-start(bf16[2,2,1,2,24,768]{5,4,3,1,0,2:T(8,128)(2,1)S(1)} %slice.8), channel_id=1, source_target_pairs={{0,2},{1,3},{2,0},{3,1},{4,6},{5,7},{6,4},{7,5},{8,10},{9,11},{10,... | collective-permute-start | bytes 884744 | tf_op jit(solution)/shard_map/ppermute | solution.py:1492
  60.8 10.1 %collective-permute-start.20 = (f32[8,1536]{1,0:T(8,128)S(1)}, f32[8,1536]{1,0:T(8,128)S(1)}, u32[]{:S(2)}, u32[]{:S(2)}) collective-permute-start(f32[8,1536]{1,0:T(8,128)S(1)} %shard_map.310.refs_6_.refs_8_.refs_7_.refs_3_.refs_9_), channel_id=1, source_target_pairs={{0,16},{16,0},{1,17},{17,1},{2,18},{18,2},{3,19},{19,3},{4,20},{20... | collective-permute-start | bytes 147464 | tf_op jit(solution)/shard_map/ppermute | solution.py:1477
  60.9 22.0 %collective-permute-start.21 = (bf16[2,2,1,2,24,1920]{5,4,3,1,0,2:T(8,128)(2,1)S(1)}, bf16[2,2,1,2,24,1920]{5,4,3,1,0,2:T(8,128)(2,1)S(1)}, u32[]{:S(2)}, u32[]{:S(2)}) collective-permute-start(bf16[2,2,1,2,24,1920]{5,4,3,1,0,2:T(8,128)(2,1)S(1)} %slice.9), channel_id=1, source_target_pairs={{0,2},{1,3},{2,0},{3,1},{4,6},{5,7},{6,4},{7,5},{8,10},{9,11},{10,... | collective-permute-start | bytes 2211848 | tf_op jit(solution)/shard_map/ppermute | solution.py:1492
  61.5 21.4 %collective-permute-start.22 = (bf16[2,2,2,1,96,384]{5,4,2,1,0,3:T(8,128)(2,1)S(1)}, bf16[2,2,2,1,96,384]{5,4,2,1,0,3:T(8,128)(2,1)S(1)}, u32[]{:S(2)}, u32[]{:S(2)}) collective-permute-start(bf16[2,2,2,1,96,384]{5,4,2,1,0,3:T(8,128)(2,1)S(1)} %bitcast.157), channel_id=1, source_target_pairs={{0,1},{1,0},{2,3},{3,2},{4,5},{5,4},{6,7},{7,6},{8,9},{9,8},{10,11... | collective-permute-start | bytes 1769480 | tf_op jit(solution)/shard_map/ppermute | solution.py:1492
  140.2 16.5 %collective-permute-start.28 = (bf16[8,24,1536]{2,1,0:T(8,128)(2,1)S(1)}, bf16[8,24,1536]{2,1,0:T(8,128)(2,1)S(1)}, u32[]{:S(2)}, u32[]{:S(2)}) collective-permute-start(bf16[8,24,1536]{2,1,0:T(8,128)(2,1)S(1)} %bitcast.226), channel_id=1, source_target_pairs={{0,1},{1,0},{2,3},{3,2},{4,5},{5,4},{6,7},{7,6},{8,9},{9,8},{10,11... | collective-permute-start | bytes 1769480 | tf_op jit(solution)/shard_map/ppermute | solution.py:1492
  141.0 15.7 %collective-permute-start.29 = (bf16[8,24,1024]{2,1,0:T(8,128)(2,1)}, bf16[8,24,1024]{2,1,0:T(8,128)(2,1)S(1)}, u32[]{:S(2)}, u32[]{:S(2)}) collective-permute-start(bf16[8,24,1024]{2,1,0:T(8,128)(2,1)} %bitcast.227), channel_id=1, source_target_pairs={{0,2},{1,3},{2,0},{3,1},{4,6},{5,7},{6,4},{7,5},{8,10},{9,11},{10,... | collective-permute-start | bytes 1179656 | tf_op jit(solution)/shard_map/ppermute | solution.py:1492
  160.9 22.8 %collective-permute-start.33 = (bf16[8,24,1536]{2,1,0:T(8,128)(2,1)S(1)}, bf16[8,24,1536]{2,1,0:T(8,128)(2,1)S(1)}, u32[]{:S(2)}, u32[]{:S(2)}) collective-permute-start(bf16[8,24,1536]{2,1,0:T(8,128)(2,1)S(1)} %bitcast.225), channel_id=1, source_target_pairs={{0,1},{1,0},{2,3},{3,2},{4,5},{5,4},{6,7},{7,6},{8,9},{9,8},{10,11... | collective-permute-start | bytes 1769480 | tf_op jit(solution)/shard_map/ppermute | solution.py:1492
  162.2 21.5 %collective-permute-start.31 = (bf16[4,24,1536]{2,1,0:T(8,128)(2,1)S(1)}, bf16[4,24,1536]{2,1,0:T(8,128)(2,1)S(1)}, u32[]{:S(2)}, u32[]{:S(2)}) collective-permute-start(bf16[4,24,1536]{2,1,0:T(8,128)(2,1)S(1)} %bitcast.229), channel_id=1, source_target_pairs={{0,2},{1,3},{2,0},{3,1},{4,6},{5,7},{6,4},{7,5},{8,10},{9,11},{10,... | collective-permute-start | bytes 884744 | tf_op jit(solution)/shard_map/ppermute | solution.py:1492
  164.1 19.6 %collective-permute-start.32 = (bf16[4,24,1024]{2,1,0:T(8,128)(2,1)S(1)}, bf16[4,24,1024]{2,1,0:T(8,128)(2,1)S(1)}, u32[]{:S(2)}, u32[]{:S(2)}) collective-permute-start(bf16[4,24,1024]{2,1,0:T(8,128)(2,1)S(1)} %bitcast.232), channel_id=1, source_target_pairs={{0,1},{1,0},{2,3},{3,2},{4,5},{5,4},{6,7},{7,6},{8,9},{9,8},{10,11... | collective-permute-start | bytes 589832 | tf_op jit(solution)/shard_map/ppermute | solution.py:1492
  187.2 20.6 %collective-permute-start.35 = (bf16[8,24,1024]{2,1,0:T(8,128)(2,1)}, bf16[8,24,1024]{2,1,0:T(8,128)(2,1)S(1)}, u32[]{:S(2)}, u32[]{:S(2)}) collective-permute-start(bf16[8,24,1024]{2,1,0:T(8,128)(2,1)} %bitcast.91), channel_id=1, source_target_pairs={{0,1},{1,0},{2,3},{3,2},{4,5},{5,4},{6,7},{7,6},{8,9},{9,8},{10,11... | collective-permute-start | bytes 1179656 | tf_op jit(solution)/shard_map/ppermute | solution.py:1492
  188.6 19.2 %collective-permute-start.37 = (bf16[4,24,1536]{2,1,0:T(8,128)(2,1)S(1)}, bf16[4,24,1536]{2,1,0:T(8,128)(2,1)S(1)}, u32[]{:S(2)}, u32[]{:S(2)}) collective-permute-start(bf16[4,24,1536]{2,1,0:T(8,128)(2,1)S(1)} %bitcast.228), channel_id=1, source_target_pairs={{0,2},{1,3},{2,0},{3,1},{4,6},{5,7},{6,4},{7,5},{8,10},{9,11},{10,... | collective-permute-start | bytes 884744 | tf_op jit(solution)/shard_map/ppermute | solution.py:1492
  190.4 17.4 %collective-permute-start.36 = (bf16[2,24,2560]{2,1,0:T(8,128)(2,1)}, bf16[2,24,2560]{2,1,0:T(8,128)(2,1)S(1)}, u32[]{:S(2)}, u32[]{:S(2)}) collective-permute-start(bf16[2,24,2560]{2,1,0:T(8,128)(2,1)} %bitcast.85), channel_id=1, source_target_pairs={{0,4},{1,5},{2,6},{3,7},{4,0},{5,1},{6,2},{7,3},{8,12},{9,13},{10,... | collective-permute-start | bytes 737288 | tf_op jit(solution)/shard_map/ppermute | solution.py:1492
  207.8 22.6 %collective-permute-start.42 = (f32[512,384]{1,0:T(8,128)}, f32[512,384]{1,0:T(8,128)S(1)}, u32[]{:S(2)}, u32[]{:S(2)}) collective-permute-start(f32[512,384]{1,0:T(8,128)} %get-tuple-element.300), channel_id=1, source_target_pairs={{0,16},{16,0},{1,17},{17,1},{2,18},{18,2},{3,19},{19,3},{4,20},{20... | collective-permute-start | bytes 2359304 | tf_op jit(solution)/shard_map/ppermute | solution.py:1477
  208.7 7.9 %collective-permute-start.38 = (bf16[4,24,1024]{2,1,0:T(8,128)(2,1)S(1)}, bf16[4,24,1024]{2,1,0:T(8,128)(2,1)S(1)}, u32[]{:S(2)}, u32[]{:S(2)}) collective-permute-start(bf16[4,24,1024]{2,1,0:T(8,128)(2,1)S(1)} %bitcast.233), channel_id=1, source_target_pairs={{0,2},{1,3},{2,0},{3,1},{4,6},{5,7},{6,4},{7,5},{8,10},{9,11},{10,... | collective-permute-start | bytes 589832 | tf_op jit(solution)/shard_map/ppermute | solution.py:1492
  218.0 9.9 %collective-permute-start.40 = (bf16[2,24,2560]{2,1,0:T(8,128)(2,1)S(1)}, bf16[2,24,2560]{2,1,0:T(8,128)(2,1)S(1)}, u32[]{:S(2)}, u32[]{:S(2)}) collective-permute-start(bf16[2,24,2560]{2,1,0:T(8,128)(2,1)S(1)} %bitcast.231), channel_id=1, source_target_pairs={{0,4},{1,5},{2,6},{3,7},{4,0},{5,1},{6,2},{7,3},{8,12},{9,13},{10,... | collective-permute-start | bytes 737288 | tf_op jit(solution)/shard_map/ppermute | solution.py:1492
  220.0 7.9 %collective-permute-start.41 = (bf16[64,768]{1,0:T(8,128)(2,1)S(1)}, bf16[64,768]{1,0:T(8,128)(2,1)S(1)}, u32[]{:S(2)}, u32[]{:S(2)}) collective-permute-start(bf16[64,768]{1,0:T(8,128)(2,1)S(1)} %shard_map.335.held), channel_id=1, source_target_pairs={{0,4},{1,5},{2,6},{3,7},{4,0},{5,1},{6,2},{7,3},{8,12},{9,13},{10,... | collective-permute-start | bytes 294920 | tf_op jit(solution)/shard_map/ppermute | solution.py:1492
  220.1 10.3 %collective-permute-start.43 = (bf16[8,2304]{1,0:T(8,128)(2,1)S(1)}, bf16[8,2304]{1,0:T(8,128)(2,1)S(1)}, u32[]{:S(2)}, u32[]{:S(2)}) collective-permute-start(bf16[8,2304]{1,0:T(8,128)(2,1)S(1)} %copy-done.37), channel_id=1, source_target_pairs={{0,16},{16,0},{1,17},{17,1},{2,18},{18,2},{3,19},{19,3},{4,20},{20... | collective-permute-start | bytes 110600 | tf_op jit(solution)/shard_map/ppermute | solution.py:1477
  230.4 13.0 %collective-permute-start.45 = (bf16[1,24,5120]{2,1,0:T(8,128)(2,1)S(1)}, bf16[1,24,5120]{2,1,0:T(8,128)(2,1)S(1)}, u32[]{:S(2)}, u32[]{:S(2)}) collective-permute-start(bf16[1,24,5120]{2,1,0:T(8,128)(2,1)S(1)} %bitcast.230), channel_id=1, source_target_pairs={{0,8},{1,9},{2,10},{3,11},{4,12},{5,13},{6,14},{7,15},{8,0},{9,1},... | collective-permute-start | bytes 737288 | tf_op jit(solution)/shard_map/ppermute | solution.py:1492
  (59 other events, 325.1 us)
Sparse Core Ops, SparseCore 0:
  141.1 66.6 all-gather.1
